TPU v7x, 32 devices: a whole 2x2x4 slice. The times are simulated.
32 devices in a mesh: grp: 8 (over z, x), vocab: 4 (over y, core).
Axes of the slice: x: 2, y: 2, z: 4, core: 2. Of those that a mesh axis runs over, the one named last changes fastest.
Arguments:
- final_hidden: bfloat16 [2048, 2048], P('grp')
- norm_gain: float32 [2048], replicated, may hold values from 0.5 to 1.5
- head_weight: bfloat16 [25088, 2048], P(('vocab', 'grp'))
- token_ids: int32 [2048], replicated, may hold values from 0 to 25087
- group_lengths: int32 [8], replicated, may hold values from 1 to 256, as said below
- segment_ids: int32 [2048], P('grp'), may hold values from 0 to 3, as said below
- continues: int32 [8], replicated, may hold values from 0 to 1, as said below
- layer_input: bfloat16 [2048, 2048], P('grp')
- key_weight: bfloat16 [2048, 2048], P(None, 'vocab')
- key_gain: float32 [2048], P('vocab'), may hold values from 0.5 to 1.5
- positions: int32 [2048], P('grp'), may hold values from 0 to 16383
- key_rows: int32 [200], P('grp'), may hold values from 0 to 255, as said below
Outputs:
- token_logprob: float32 [2048], P('grp')
- token_entropy: float32 [2048], P('grp')
- request_mean: float32 [32], P('grp')
- keys: bfloat16 [200, 2048], P('grp', 'vocab')
Inputs may be any that keep to these rules, and one draw needn't show every extreme that they name: For every g below 4, group_lengths[g] + group_lengths[g + 4] <= 320; groups 0 and 4 reach that bound, and group 0 fills all 256 slots. `segment_ids`: never falls along a group's slots. `continues`: 0 for odd g, 1 for g = 0 and for g = 6. `key_rows`: each entry is below its group's length.
All inputs are finite; a program needn't handle non-finite values.
Results may differ from a plain program's by a relative error of at most 0.0071.
Values may be sent and summed in bfloat16 or wider, within the bound.
No kernel may reach another device: no remote copies, remote signals or barrier semaphores. Data moves between devices by JAX's collectives and lax.ppermute only.
A program may use at most 128 MiB of HBM per device.

v0:
```python
import jax
import jax.numpy as jnp
from jax import lax
from jax.sharding import PartitionSpec as P

HD = 128
SEGS = 4


NORM_EPS = 1e-06
ROPE_BASE = 500000.0


def joined_2(part, axis, combine):
    gathered = jax.tree.map(lambda a: lax.all_gather(a, axis), part)

    def take(source):
        return jax.tree.map(lambda a: lax.dynamic_index_in_dim(a, source, 0, False), gathered)

    return lax.fori_loop(
        1, lax.axis_size(axis), lambda source, state: combine(state, take(source)), take(0)
    )


def swapped(array, axis, apart):
    return lax.ppermute(array, axis, [(i, i ^ 1 << apart) for i in range(lax.axis_size(axis))])


def normalize(hidden, gain):
    widened = hidden.astype(jnp.float32)
    meansq = jnp.mean(widened * widened, axis=-1, keepdims=True)
    return (widened * lax.rsqrt(meansq + NORM_EPS) * gain).astype(jnp.bfloat16)


def logit_block(left, right):
    product = lax.dot_general(
        left, right, (((1,), (1,)), ((), ())), preferred_element_type=jnp.float32
    )
    return lax.optimization_barrier(product.astype(jnp.bfloat16)).astype(jnp.float32)


def block_stats(logits, targets, columns):
    highest = jnp.max(logits, axis=1)
    shifted = jnp.exp(logits - highest[:, None])
    expsum = jnp.sum(shifted, axis=1)
    moment = jnp.sum(shifted * logits, axis=1)
    picked = jnp.sum(jnp.where(columns[None, :] == targets[:, None], logits, 0.0), axis=1)
    return (highest, expsum, moment, picked)


def combine_stats(first, second):
    highest = jnp.maximum(first[0], second[0])
    left_scale = jnp.exp(first[0] - highest)
    right_scale = jnp.exp(second[0] - highest)
    return (
        highest,
        first[1] * left_scale + second[1] * right_scale,
        first[2] * left_scale + second[2] * right_scale,
        first[3] + second[3],
    )


def empty_stats(count):
    zeros = jnp.zeros((count,), jnp.float32)
    return (jnp.full((count,), -jnp.inf, jnp.float32), zeros, zeros, zeros)


def finish_stats(stats):
    merged = joined_2(stats, "vocab", combine_stats)
    logsum = merged[0] + jnp.log(merged[1])
    return (merged[3] - logsum, logsum - merged[2] / merged[1])


def rotate(values, places):
    count = values.shape[0]
    heads = values.shape[1] // HD
    half = HD // 2
    shaped = values.reshape(count, heads, HD)
    steps = jnp.arange(half).astype(jnp.float32)
    freqs = jnp.exp(-(2.0 * steps / HD) * jnp.log(jnp.float32(ROPE_BASE)))
    angles = places[:, None] * freqs[None, :]
    cosine = jnp.cos(angles)[:, None, :]
    sine = jnp.sin(angles)[:, None, :]
    first = shaped[..., :half]
    second = shaped[..., half:]
    turned = jnp.concatenate(
        [first * cosine - second * sine, second * cosine + first * sine], axis=-1
    )
    return turned.reshape(count, heads * HD)


def local(
    final_hidden,
    norm_gain,
    head_weight,
    token_ids,
    group_lengths,
    segment_ids,
    continues,
    layer_input,
    key_weight,
    key_gain,
    positions,
    key_rows,
):
    row_cap = final_hidden.shape[0]
    groups = lax.axis_size("grp")
    shards = lax.axis_size("vocab")
    group_here = lax.axis_index("grp")
    shard_here = lax.axis_index("vocab")
    local_vocab = head_weight.shape[0]
    shard_vocab = local_vocab * groups
    shard_start = shard_here * shard_vocab
    normed = normalize(final_hidden, norm_gain)
    my_len = group_lengths[group_here]
    slots = jnp.arange(row_cap, dtype=jnp.int32)
    live = slots < my_len
    my_ids = lax.dynamic_slice_in_dim(token_ids, group_here * row_cap, row_cap)
    piece = lax.all_gather(head_weight, "grp", axis=0, tiled=True)
    logits = logit_block(normed, piece)
    columns = shard_start + jnp.arange(piece.shape[0], dtype=jnp.int32)
    stats = combine_stats(empty_stats(normed.shape[0]), block_stats(logits, my_ids, columns))
    logprob, entropy = finish_stats(stats)
    logprob = jnp.where(live, logprob, 0.0)
    entropy = jnp.where(live, entropy, 0.0)
    labels = jnp.arange(SEGS, dtype=jnp.int32)
    member = (segment_ids[:, None] == labels[None, :]) & live[:, None]
    sums = jnp.sum(jnp.where(member, logprob[:, None], 0.0), axis=0)
    counts = jnp.sum(member.astype(jnp.float32), axis=0)
    partner_sums, partner_counts = swapped((sums, counts), "grp", 0)
    is_even = group_here % 2 == 0
    partner = jnp.bitwise_xor(group_here, 1)
    joined = jnp.where(is_even, continues[group_here], continues[partner]) == 1
    my_last = jnp.take(segment_ids, my_len - 1)
    partner_last = jnp.max(jnp.where(partner_counts > 0, labels, 0))
    extra_sum = jnp.where(is_even, partner_sums[0], jnp.take(partner_sums, partner_last))
    extra_count = jnp.where(is_even, partner_counts[0], jnp.take(partner_counts, partner_last))
    target_slot = jnp.where(is_even, my_last, 0)
    update = joined & (labels == target_slot)
    total_sum = sums + jnp.where(update, extra_sum, 0.0)
    total_count = counts + jnp.where(update, extra_count, 0.0)
    request_mean = total_sum / jnp.maximum(total_count, 1.0)
    chosen = jnp.take(layer_input, key_rows, axis=0)
    projected = jnp.dot(chosen, key_weight, preferred_element_type=jnp.float32)
    local_squares = jnp.sum(projected * projected, axis=1)
    all_squares = lax.psum(local_squares, "vocab")
    key_width = key_weight.shape[1] * shards
    scale = jnp.sqrt(all_squares / key_width + NORM_EPS)
    normal_keys = projected / scale[:, None] * key_gain
    places = jnp.take(positions, key_rows).astype(jnp.float32)
    keys = rotate(normal_keys, places).astype(jnp.bfloat16)
    return (logprob, entropy, request_mean, keys)


def solution(mesh):
    in_specs = (
        P("grp", None),
        P(),
        P(("vocab", "grp"), None),
        P(),
        P(),
        P("grp"),
        P(),
        P("grp", None),
        P(None, "vocab"),
        P("vocab"),
        P("grp"),
        P("grp"),
    )
    out_specs = (P("grp"), P("grp"), P("grp"), P("grp", "vocab"))
    return jax.shard_map(local, mesh=mesh, in_specs=in_specs, out_specs=out_specs, check_vma=False)
```

profile of v0, /device:TPU:0, one launch (start us, length us, event | category | flops | bytes accessed | tf_op | source)
XLA Modules:
  0.0 562.1 jit_solution(7395891202209995779)
XLA Ops:
  7.2 0.0 copy-start
  7.2 0.0 copy-start.9
  7.2 0.0 copy-start.5
  7.2 0.0 copy-start.6
  7.2 0.0 copy-start.7
  7.2 0.0 copy-start.1
  7.2 0.0 copy-start.4
  7.2 0.0 all-gather.8.cloned.1.call-start
  7.3 0.7 all-gather.8.cloned.1.call-update
  8.0 0.0 copy-start.2
  8.0 0.0 copy-start.8
  8.0 0.0 copy-done.9
  8.0 0.6 dynamic_slice.65
  9.9 0.0 copy-done.5
  9.9 0.6 fusion.19
  11.8 0.0 copy-done.6
  11.8 0.6 dynamic-slice.6
  13.1 0.0 copy-done.7
  13.1 2.1 gather_fusion
  15.2 0.7 gather_fusion.1
  15.9 0.6 multiply_reduce_fusion
  16.6 8.5 %psum.7 = f32[25]{0:T(128)S(1)} all-reduce(f32[25]{0:T(128)S(1)} %get-tuple-element.309), channel_id=1, replica_groups=mesh['grp'=8,'vocab'=4] {'vocab'}, use_global_device_ids=true, to_apply=%region_11.12 | all-reduce | flops 25 | bytes 200 | tf_op jit(solution)/shard_map/psum | solution.py:146
  25.1 0.1 divide_multiply_fusion
  25.2 0.1 multiply_cosine_fusion
  25.3 0.1 subtract_convert_fusion
  25.5 0.1 pad_maximum_fusion
  25.6 0.6 copy.20
  26.2 0.8 dynamic_slice.69
  27.0 0.6 iota_compare_fusion.1
  27.6 0.3 fusion.4
  27.9 474.7 %all-gather.8.cloned.1.call-done = bf16[6272,2048]{1,0:T(8,128)(2,1)} async-done(((bf16[784,2048]{1,0:T(8,128)(2,1)}), bf16[6272,2048]{1,0:T(8,128)(2,1)}) %all-gather.8.cloned.1.call-update) | async-done | bytes 25690128 | tf_op jit(solution)/shard_map/all_gather | solution.py:119
  502.6 14.0 %convolution_convert_fusion = bf16[256,6272]{1,0:T(8,128)(2,1)} fusion(bf16[6272,2048]{1,0:T(8,128)(2,1)} %all-gather.8.cloned.1.call-done, bf16[256,2048]{1,0:T(8,128)(2,1)S(1)} %copy-done.2, f32[2048]{0:T(1024)S(1)} %copy-done.8, f32[256]{0:T(256)S(1)} %add_rsqrt_fusion), kind=kOutput, calls=%fused_computation.13 | convolution fusion | flops 6580371456 | bytes 29959168 | tf_op jit(solution)/shard_map/dot_general | solution.py:36
  516.6 2.4 reduce_max.27
  519.0 5.1 all-gather.2
  524.1 3.9 fusion.2
  528.0 5.1 all-gather.3
  533.1 5.1 all-gather.4
  538.2 5.1 all-gather.5
  543.2 0.3 while.24
  543.5 1.2 subtract_select_fusion
  544.8 0.1 select_reduce_fusion
  544.9 0.4 collective-permute-start
  545.3 1.7 collective-permute-start.1
  547.0 1.9 collective-permute-done.1
  548.9 0.6 fusion.15
  551.4 0.0 collective-permute-done
  551.5 0.7 fusion.17
  554.7 0.5 maximum_divide_fusion
  (44 shorter events, 0.3 us)
Async XLA Ops:
  7.2 8.8 %copy-start = (bf16[2048,512]{1,0:T(8,128)(2,1)S(1)}, bf16[2048,512]{1,0:T(8,128)(2,1)}, u32[]{:S(2)}) copy-start(bf16[2048,512]{1,0:T(8,128)(2,1)} %param.22) | copy-start | bytes 6291460
  7.2 0.8 copy-start.9
  7.2 2.7 copy-start.5
  7.2 4.6 copy-start.6
  7.2 5.9 %copy-start.7 = (s32[25]{0:T(128)S(1)}, s32[25]{0:T(128)}, u32[]{:S(2)}) copy-start(s32[25]{0:T(128)} %param.25) | copy-start | bytes 304
  7.2 8.0 %copy-start.1 = (s32[256]{0:T(256)S(1)}, s32[256]{0:T(256)}, u32[]{:S(2)}) copy-start(s32[256]{0:T(256)} %param.24) | copy-start | bytes 3076
  7.2 17.8 %copy-start.4 = (f32[512]{0:T(512)S(1)}, f32[512]{0:T(512)}, u32[]{:S(2)}) copy-start(f32[512]{0:T(512)} %param.23) | copy-start | bytes 6148
  7.2 495.4 %all-gather.8.cloned.1.call-start = ((), (), s32[]{:S(2)}) async-start(), calls=%async_computation | async-start | bytes 28901376 | tf_op jit(solution)/shard_map/all_gather | solution.py:119
  8.0 19.6 %copy-start.2 = (bf16[256,2048]{1,0:T(8,128)(2,1)S(1)}, bf16[256,2048]{1,0:T(8,128)(2,1)}, u32[]{:S(2)}) copy-start(bf16[256,2048]{1,0:T(8,128)(2,1)} %param.14) | copy-start | bytes 3145732
  8.0 494.6 %copy-start.8 = (f32[2048]{0:T(1024)S(1)}, f32[2048]{0:T(1024)}, u32[]{:S(2)}) copy-start(f32[2048]{0:T(1024)} %param.15) | copy-start | bytes 24580
  544.8 10.5 %copy-start.3 = (f32[256]{0:T(256)}, f32[256]{0:T(256)S(1)}, u32[]{:S(2)}) copy-start(f32[256]{0:T(256)S(1)} %get-tuple-element.298) | copy-start | bytes 3076
  544.9 6.5 %collective-permute-start = (f32[4]{0:T(128)S(1)}, f32[4]{0:T(128)S(1)}, u32[]{:S(2)}, u32[]{:S(2)}) collective-permute-start(f32[4]{0:T(128)S(1)} %get-tuple-element.267), channel_id=1, source_target_pairs={{0,4},{4,0},{8,12},{12,8},{16,20},{20,16},{24,28},{28,24},{1,5},{5... | collective-permute-start | bytes 56 | tf_op jit(solution)/shard_map/ppermute | solution.py:26
  545.3 3.5 collective-permute-start.1
Sparse Core Ops, SparseCore 0:
  9.6 492.9 all-gather.7
where the time goes:
time: 563 us; the launch traced here: 562 us
  waiting for transfers between devices  477 us (85%)
  blocking collectives  28.7 us (5%)
  between operations  22.1 us (4%)
  matrix products  14.6 us (3%)
  other arithmetic  10.4 us (2%)
  local copies, waits for them, and re-layouts  6.76 us (1%)
    all_gather x1, waiting for transfers between devices, local(): piece = lax.all_gather(head_weight, 'grp', axis=0, tiled=True)  475 us
    all_gather x4, blocking collectives, joined_2(): gathered = jax.tree.map(lambda a: lax.all_gather(a, axis), part)  20.3 us
    dot_general x1, matrix products, logit_block(): lax.dot_general(left, right, (((1,), (1,)), ((), ())), preferred_element_...  14 us
  transfers between devices with their start and end apart: 3, of which 2 were waited for; matrix products, arithmetic and copies ran while one was open for 2% of the time, Pallas kernels for 0%

commit v1 on v0

v1 whole, which is shorter than its diff:
```python
import functools

import jax
import jax.numpy as jnp
from jax import lax
from jax.experimental import pallas as pl
from jax.experimental.pallas import tpu as pltpu
from jax.sharding import PartitionSpec as P

HD = 128
SEGS = 4
BAL = 160
CORES = 2

NORM_EPS = 1e-06
ROPE_BASE = 500000.0

VMEM_LIMIT = 48 * 1024 * 1024
WHOLE = pl.BlockSpec(memory_space=pltpu.VMEM)
SCALARS = pl.BlockSpec(memory_space=pltpu.SMEM)


def call(kernel, out_shape, in_specs, flops, moved, **more):
    return pl.pallas_call(
        kernel,
        out_shape=out_shape,
        in_specs=in_specs,
        compiler_params=pltpu.CompilerParams(vmem_limit_bytes=VMEM_LIMIT),
        cost_estimate=pl.CostEstimate(flops=flops, bytes_accessed=moved, transcendentals=0),
        **more,
    )


def source_row(place, quarter, is_first, quarters, rows):
    return jnp.where(
        is_first,
        quarters * place + quarter,
        quarters * (rows - 1 - place) + quarters - 1 - quarter,
    )


def prep_kernel(meta_ref, hidden_ref, gain_ref, out_ref):
    parts, rows, _ = out_ref.shape
    count = hidden_ref.shape[0]
    widened = hidden_ref[...].astype(jnp.float32)
    meansq = jnp.mean(widened * widened, axis=-1, keepdims=True)
    normed = (widened * lax.rsqrt(meansq + NORM_EPS) * gain_ref[...]).astype(jnp.bfloat16)
    place = lax.broadcasted_iota(jnp.int32, (rows, count), 0)
    column = lax.broadcasted_iota(jnp.int32, (rows, count), 1)
    for t in range(parts):
        quarter = (meta_ref[1] ^ t) * CORES + meta_ref[2]
        row = source_row(place, quarter, meta_ref[0] == 1, parts * CORES, rows)
        pick = (column == row).astype(jnp.float32).astype(jnp.bfloat16)
        out_ref[t] = jnp.dot(pick, normed, preferred_element_type=jnp.float32).astype(jnp.bfloat16)


def score_kernel(count, meta_ref, targets_ref, *refs):
    pieces, (near_ref, far_ref, out_ref, tokens_ref) = refs[:count], refs[count:]
    step = pl.program_id(0)
    tile = near_ref.shape[0]
    size = pieces[0].shape[0]

    @pl.when(step == 0)
    def _():
        for t, piece in enumerate(pieces):
            start = 0 if count == 1 else pl.multiple_of((meta_ref[2] ^ t) * size, 8)
            tokens_ref[pl.ds(start, size), :] = piece[...]
        out_ref[...] = jnp.zeros_like(out_ref)
        out_ref[0:1, :] = jnp.full((1, out_ref.shape[1]), -jnp.inf, jnp.float32)

    tokens = tokens_ref[...]
    targets = targets_ref[...]
    for which, weight_ref in enumerate((near_ref, far_ref)):
        logits = lax.dot_general(
            weight_ref[...], tokens, (((1,), (1,)), ((), ())), preferred_element_type=jnp.float32
        )
        logits = logits.astype(jnp.bfloat16).astype(jnp.float32)
        old = out_ref[0:1, :]
        top = jnp.maximum(old, jnp.max(logits, axis=0, keepdims=True))
        shifted = jnp.exp(logits - top)
        scale = jnp.exp(old - top)
        entry = lax.broadcasted_iota(jnp.int32, logits.shape, 0)
        wanted = targets - (meta_ref[which] + step * tile)
        out_ref[0:1, :] = top
        out_ref[1:2, :] = out_ref[1:2, :] * scale + jnp.sum(shifted, axis=0, keepdims=True)
        out_ref[2:3, :] = out_ref[2:3, :] * scale + jnp.sum(shifted * logits, axis=0, keepdims=True)
        out_ref[3:4, :] += jnp.sum(jnp.where(entry == wanted, logits, 0.0), axis=0, keepdims=True)


def score(meta, targets, pieces, near, far):
    vocab, width = near.shape
    tokens = sum(piece.shape[0] for piece in pieces)
    tile = vocab
    for parts in range(1, vocab // 16 + 1):
        if vocab % parts == 0 and (vocab // parts) % 16 == 0 and vocab // parts <= 128:
            tile = vocab // parts
            break
    head = pl.BlockSpec((tile, width), lambda i: (i, 0))
    return call(
        functools.partial(score_kernel, len(pieces)),
        jax.ShapeDtypeStruct((8, tokens), jnp.float32),
        [SCALARS, WHOLE] + [WHOLE] * len(pieces) + [head, head],
        4 * vocab * tokens * width,
        4 * vocab * width + 2 * tokens * width,
        out_specs=pl.BlockSpec((8, tokens), lambda i: (0, 0)),
        grid=(vocab // tile,),
        scratch_shapes=[pltpu.VMEM((tokens, width), jnp.bfloat16)],
    )(meta, targets, *pieces, near, far)


def keys_kernel(rows_ref, input_ref, weight_ref, gain_ref, cosine_ref, sine_ref, turned_ref, squares_ref):
    count, width = turned_ref.shape
    column = lax.broadcasted_iota(jnp.int32, (count, input_ref.shape[0]), 1)
    pick = (column == rows_ref[...]).astype(jnp.float32).astype(jnp.bfloat16)
    chosen = jnp.dot(pick, input_ref[...], preferred_element_type=jnp.float32).astype(jnp.bfloat16)
    projected = jnp.dot(chosen, weight_ref[...], preferred_element_type=jnp.float32)
    squares = jnp.sum(projected * projected, axis=1, keepdims=True)
    lanes = squares_ref.shape[1]
    diagonal = lax.broadcasted_iota(jnp.int32, (count, lanes), 0) == lax.broadcasted_iota(
        jnp.int32, (count, lanes), 1
    )
    squares_ref[...] = jnp.sum(jnp.where(diagonal, squares, 0.0), axis=0, keepdims=True)
    gained = projected * gain_ref[...]
    cosine, sine = cosine_ref[...], sine_ref[...]
    for start in range(0, width, HD):
        head = gained[:, start : start + HD]
        turned_ref[:, start : start + HD] = head * cosine + pltpu.roll(head, HD // 2, 1) * sine


def final_kernel(
    sizes,
    meta_ref,
    lengths_ref,
    continues_ref,
    got_ref,
    segments_ref,
    turned_ref,
    logprob_ref,
    entropy_ref,
    mean_ref,
    keys_ref,
):
    groups, shards = sizes
    parts, group = shards // CORES, meta_ref[0]
    cap, tokens = segments_ref.shape[1], got_ref.shape[3]
    columns = []
    for core in range(CORES):
        every = got_ref[:, core]
        top = jnp.max(every[:, 0:1, :], axis=0)
        scale = jnp.exp(every[:, 0:1, :] - top[None])
        expsum = jnp.sum(every[:, 1:2, :] * scale, axis=0)
        moment = jnp.sum(every[:, 2:3, :] * scale, axis=0)
        picked = jnp.sum(every[:, 3:4, :], axis=0)
        lse = top + jnp.log(expsum)
        columns.append(jnp.concatenate([picked - lse, lse - moment / expsum], axis=0))
    both = jnp.concatenate(columns, axis=1)
    values = jnp.concatenate([both, jnp.zeros((6, both.shape[1]), jnp.float32)], axis=0)

    slots = lax.broadcasted_iota(jnp.int32, (1, cap), 1)
    is_first = group < groups // 2
    quarter = jnp.where(is_first, slots % shards, shards - 1 - slots % shards)
    size = tokens // 2 // parts
    place = jnp.where(is_first, slots // shards, size - 1 - slots // shards)
    home = (quarter % CORES) * tokens + quarter // CORES * size + place
    stood = lax.broadcasted_iota(jnp.int32, (CORES * tokens, cap), 0)
    labels = lax.broadcasted_iota(jnp.int32, (1, SEGS), 1)

    def summed(who, segments):
        pick = (stood == home + who % 2 * (tokens // 2)).astype(jnp.float32)
        found = jnp.dot(
            values, pick, preferred_element_type=jnp.float32, precision=lax.Precision.HIGHEST
        )
        live = slots < lengths_ref[who]
        logprob = jnp.where(live, found[0:1, :], 0.0)
        entropy = jnp.where(live, found[1:2, :], 0.0)
        sums = jnp.zeros((1, SEGS), jnp.float32)
        counts = jnp.zeros((1, SEGS), jnp.float32)
        for label in range(SEGS):
            member = live & (segments == label)
            one_sum = jnp.sum(jnp.where(member, logprob, 0.0), axis=1, keepdims=True)
            one_count = jnp.sum(member.astype(jnp.float32), axis=1, keepdims=True)
            sums = jnp.where(labels == label, one_sum, sums)
            counts = jnp.where(labels == label, one_count, counts)
        return logprob, entropy, sums, counts

    partner = group ^ 1
    logprob, entropy, sums, counts = summed(group, segments_ref[0:1, :])
    _, _, partner_sums, partner_counts = summed(partner, segments_ref[1:2, :])
    is_even = group % 2 == 0
    joined = jnp.where(is_even, continues_ref[group], continues_ref[partner]) == 1
    last = slots == lengths_ref[group] - 1
    my_last = jnp.sum(jnp.where(last, segments_ref[0:1, :], 0), axis=1, keepdims=True)
    partner_last = jnp.max(jnp.where(partner_counts > 0, labels, 0), axis=1, keepdims=True)
    wanted = jnp.where(is_even, jnp.zeros_like(partner_last), partner_last)
    extra_sum = jnp.sum(jnp.where(labels == wanted, partner_sums, 0.0), axis=1, keepdims=True)
    extra_count = jnp.sum(jnp.where(labels == wanted, partner_counts, 0.0), axis=1, keepdims=True)
    target = jnp.where(is_even, my_last, jnp.zeros_like(my_last))
    update = joined & (labels == target)
    total_sum = sums + jnp.where(update, extra_sum, 0.0)
    total_count = counts + jnp.where(update, extra_count, 0.0)
    logprob_ref[...] = logprob
    entropy_ref[...] = entropy
    mean_ref[...] = total_sum / jnp.maximum(total_count, 1.0)

    count, width = turned_ref.shape
    squares = jnp.zeros((1, count), jnp.float32)
    for part in range(parts):
        for core in range(CORES):
            squares += got_ref[group * parts + part, core][4:5, :count]
    diagonal = lax.broadcasted_iota(jnp.int32, (count, count), 0) == lax.broadcasted_iota(
        jnp.int32, (count, count), 1
    )
    squares = jnp.sum(jnp.where(diagonal, squares, 0.0), axis=1, keepdims=True)
    scale = jnp.sqrt(squares / (width * shards) + NORM_EPS)
    keys_ref[...] = (turned_ref[...] / scale).astype(jnp.bfloat16)


def partners(axes, sizes, flips):
    (groups, shards), (group_flip, shard_flip) = sizes, flips
    return [
        (g * shards + v, (g ^ group_flip) * shards + (v ^ shard_flip))
        for g in range(groups)
        for v in range(shards)
    ]


def local(
    sizes,
    final_hidden,
    norm_gain,
    head_weight,
    token_ids,
    group_lengths,
    segment_ids,
    continues,
    layer_input,
    key_weight,
    key_gain,
    positions,
    key_rows,
):
    groups, shards = sizes
    parts, half = shards // CORES, groups // 2
    cap, width = final_hidden.shape
    rows = cap // shards
    size = 2 * BAL // shards
    tokens = 2 * parts * size
    group = lax.axis_index("grp")
    shard = lax.axis_index("vocab")
    y, core = shard // CORES, shard % CORES
    is_first = group < half
    axes = ("grp", "vocab")

    def swap(array, group_flip, shard_flip):
        return lax.ppermute(array, axes, partners(axes, sizes, (group_flip, shard_flip)))

    def front(which, quarter):
        return (group_lengths[which] - quarter + shards - 1) // shards

    def merge(own, other, which, quarter):
        first = jnp.where(is_first, own, other)
        second = jnp.where(is_first, other, own)
        gap = size - rows
        place = lax.broadcasted_iota(jnp.int32, (size, 1), 0)
        return jnp.where(
            place < front(which % half, quarter),
            jnp.pad(first, ((0, gap), (0, 0))),
            jnp.pad(second, ((gap, 0), (0, 0))),
        )

    vocab = head_weight.shape[0]
    far_weight = swap(head_weight, 0, 1)
    near_base = (shard * groups + group) * vocab
    far_base = ((shard ^ 1) * groups + group) * vocab
    segments = jnp.stack([segment_ids, swap(segment_ids, 1, 0)])

    dealt = token_ids.reshape(groups, rows, shards).transpose(0, 2, 1)
    gap = size - rows
    lower = jnp.pad(dealt[:half], ((0, 0), (0, 0), (0, gap)))
    upper = jnp.pad(dealt[half:, ::-1, ::-1], ((0, 0), (0, 0), (gap, 0)))
    taken = (group_lengths[:half, None] - jnp.arange(shards)[None, :] + shards - 1) // shards
    ids = jnp.where(jnp.arange(size)[None, None, :] < taken[:, :, None], lower, upper)
    ids = ids.reshape(half // 2, 2, parts, CORES, size)
    ids = lax.dynamic_index_in_dim(ids, core, 3, False).reshape(half // 2, 1, tokens)

    meta = jnp.stack([is_first.astype(jnp.int32), y, core])
    normed = call(
        prep_kernel,
        jax.ShapeDtypeStruct((parts, rows, width), jnp.bfloat16),
        [SCALARS, WHOLE, WHOLE],
        2 * parts * rows * cap * width,
        4 * cap * width,
    )(meta, final_hidden, norm_gain.reshape(1, width))

    places = jnp.sum(
        jnp.where(jnp.arange(cap)[None, :] == key_rows[:, None], positions[None, :], 0), axis=1
    ).astype(jnp.float32)
    steps = jnp.arange(HD // 2).astype(jnp.float32)
    freqs = jnp.exp(-(2.0 * steps / HD) * jnp.log(jnp.float32(ROPE_BASE)))
    angles = places[:, None] * freqs[None, :]
    cosine, sine = jnp.cos(angles), jnp.sin(angles)
    count, key_width = key_rows.shape[0], key_weight.shape[1]
    turned, squares = call(
        keys_kernel,
        (
            jax.ShapeDtypeStruct((count, key_width), jnp.float32),
            jax.ShapeDtypeStruct((1, tokens), jnp.float32),
        ),
        [WHOLE] * 6,
        2 * count * width * key_width,
        2 * width * key_width,
    )(
        key_rows.reshape(count, 1),
        layer_input,
        key_weight,
        key_gain.reshape(1, key_width),
        jnp.concatenate([cosine, cosine], axis=1),
        jnp.concatenate([-sine, sine], axis=1),
    )

    def statistics(slot, targets, pieces):
        where = jnp.stack([near_base, far_base, slot])
        return score(where, targets, pieces, head_weight, far_weight)

    if sizes == (8, 4):
        quarter, beyond = shard, shard ^ 2
        slot = group % 2 * parts + y
        here, there = normed[0], normed[1]
        other = swap(here, 4, 0)
        across = swap(normed, 1, 0)
        own = merge(here, other, group, quarter)
        far_own = swap(own, 2, 0)
        other_x = swap(other, 1, 0)
        other_y = swap(other, 0, 2)
        other_xy = swap(other, 1, 2)
        own_y = merge(there, other_y, group, beyond)
        own_x = merge(across[0], other_x, group ^ 1, quarter)
        own_xy = merge(across[1], other_xy, group ^ 1, beyond)
        far_x = swap(far_own, 1, 0)
        far_y = swap(far_own, 0, 2)
        far_xy = swap(own_xy, 2, 0)
        mine = (group % half) // 2
        own_stats = statistics(slot, ids[mine], (own, own_y, own_x, own_xy))
        far_stats = statistics(slot, ids[1 - mine], (far_own, far_y, far_x, far_xy))
        stats = jnp.where(
            (jnp.arange(half // 2) == mine)[:, None, None], own_stats[None], far_stats[None]
        )
    else:
        every = lax.all_gather(normed[0], axes).reshape(groups, parts, CORES, rows, width)
        every = lax.dynamic_index_in_dim(every, core, 2, False)
        first = jnp.pad(every[:half], ((0, 0), (0, 0), (0, gap), (0, 0)))
        second = jnp.pad(every[half:], ((0, 0), (0, 0), (gap, 0), (0, 0)))
        taken = lax.dynamic_index_in_dim(taken.reshape(half, parts, CORES), core, 2, False)
        every = jnp.where(
            jnp.arange(size)[None, None, :, None] < taken[:, :, None, None], first, second
        )
        stats = statistics(jnp.int32(0), ids.reshape(1, -1), (every.reshape(-1, width),))
        stats = stats.reshape(8, half // 2, tokens).transpose(1, 0, 2)

    row = jnp.arange(8)[None, :, None]
    stats = jnp.where(row == 4, squares[None], stats)
    sent = jnp.broadcast_to(
        stats[None, :, None, None], (2, half // 2, 2, shards, 8, tokens)
    ).reshape(groups * shards, 8, tokens)
    got = lax.all_to_all(sent, axes, 0, 0, tiled=False)

    logprob, entropy, means, keys = call(
        functools.partial(final_kernel, sizes),
        (
            jax.ShapeDtypeStruct((1, cap), jnp.float32),
            jax.ShapeDtypeStruct((1, cap), jnp.float32),
            jax.ShapeDtypeStruct((1, SEGS), jnp.float32),
            jax.ShapeDtypeStruct((count, key_width), jnp.bfloat16),
        ),
        [SCALARS] * 3 + [WHOLE] * 3,
        1 << 24,
        4 * groups * shards * 8 * tokens,
    )(
        group[None],
        group_lengths,
        continues,
        got.reshape(groups * parts, CORES, 8, tokens),
        segments,
        turned,
    )
    return logprob.reshape(cap), entropy.reshape(cap), means.reshape(SEGS), keys


def solution(mesh):
    sizes = (mesh.shape["grp"], mesh.shape["vocab"])
    in_specs = (
        P("grp", None),
        P(),
        P(("vocab", "grp"), None),
        P(),
        P(),
        P("grp"),
        P(),
        P("grp", None),
        P(None, "vocab"),
        P("vocab"),
        P("grp"),
        P("grp"),
    )
    out_specs = (P("grp"), P("grp"), P("grp"), P("grp", "vocab"))
    return jax.shard_map(
        functools.partial(local, sizes),
        mesh=mesh,
        in_specs=in_specs,
        out_specs=out_specs,
        check_vma=False,
    )
```

time: 563 us -> 82.3 us (0.15)
  waiting for transfers between devices: 477 us -> 21.4 us
  blocking collectives: 28.7 us -> 0 us
  Pallas kernels: 0 us -> 21.4 us
  starting transfers between devices: 2.13 us -> 21.3 us
  between operations: 22.1 us -> 3.65 us
  matrix products: 14.6 us -> 0 us
  other arithmetic: 10.4 us -> 4.71 us
    all_gather x1 -> x0, waiting for transfers between devices: 475 us -> none  [local(): piece = lax.all_gather(head_weight, 'grp', axis=0, tiled=True)]
    pallas_call x0 -> x5, Pallas kernels: none -> 21.4 us  [the longest x2 17 us: score(): call(functools.partial(score_kernel, len(pieces)), jax.ShapeDtypeStruct((...]
    all_gather x4 -> x0, blocking collectives: 20.3 us -> none  [joined_2(): gathered = jax.tree.map(lambda a: lax.all_gather(a, axis), part)]
    dot_general x2 -> x0, matrix products: 14.6 us -> none  [the longest x1 14 us: logit_block(): lax.dot_general(left, right, (((1,), (1,)), ((), ())), preferred_element_...]
    ppermute x2 -> x11, starting transfers between devices: 2.09 us -> 16.6 us  [swap(): lax.ppermute(array, axes, partners(axes, sizes, (group_flip, shard_flip)))]
    ppermute x2 -> x11, waiting for transfers between devices: 1.87 us -> 12.2 us  [swap(): lax.ppermute(array, axes, partners(axes, sizes, (group_flip, shard_flip)))]
    all_to_all x0 -> x1, waiting for transfers between devices: none -> 9.22 us  [local(): got = lax.all_to_all(sent, axes, 0, 0, tiled=False)]
    psum x1 -> x0, blocking collectives: 8.48 us -> none  [local(): all_squares = lax.psum(local_squares, 'vocab')]
  transfers between devices with their start and end apart: 3 -> 12, of which waited for: 2 -> 6; matrix products, arithmetic and copies ran while one was open for 2% -> 12% of each run, Pallas kernels for 0% -> 11%
where the time goes in v1:
time: 82.3 us; the launch traced here: 81.6 us
  Pallas kernels  21.4 us (26%)
  waiting for transfers between devices  21.4 us (26%)
  starting transfers between devices  21.3 us (26%)
  local copies, waits for them, and re-layouts  9.12 us (11%)
  other arithmetic  4.71 us (6%)
  between operations  3.65 us (4%)
    pallas_call x2, Pallas kernels, score(): call(functools.partial(score_kernel, len(pieces)), jax.ShapeDtypeStruct((...  17 us
    ppermute x11, starting transfers between devices, swap(): lax.ppermute(array, axes, partners(axes, sizes, (group_flip, shard_flip)))  16.6 us
    ppermute x11, waiting for transfers between devices, swap(): lax.ppermute(array, axes, partners(axes, sizes, (group_flip, shard_flip)))  12.2 us
    all_to_all x1, waiting for transfers between devices, local(): got = lax.all_to_all(sent, axes, 0, 0, tiled=False)  9.22 us
    all_to_all x1, starting transfers between devices, local(): got = lax.all_to_all(sent, axes, 0, 0, tiled=False)  4.67 us
    unnamed x20, local copies, waits for them, and re-layouts  3.31 us
    pallas_call x1, Pallas kernels, local(): call(functools.partial(final_kernel, sizes), (jax.ShapeDtypeStruct((1, ca...  2.24 us
  transfers between devices with their start and end apart: 12, of which 6 were waited for; matrix products, arithmetic and copies ran while one was open for 12% of the time, Pallas kernels for 11%

profile of v1, /device:TPU:0, one launch (start us, length us, event | category | flops | bytes accessed | tf_op | source)
XLA Modules:
  0.0 81.6 jit_solution(2405166562838704766)
XLA Ops:
  0.7 0.1 pad_add_fusion.2.meta_ref
  0.7 1.4 %copy-done.2 = bf16[256,2048]{1,0:T(8,128)(2,1)S(1)} copy-done((bf16[256,2048]{1,0:T(8,128)(2,1)S(1)}, bf16[256,2048]{1,0:T(8,128)(2,1)}, u32[]{:S(2)}) %copy-start.2) | copy-done | bytes 1048600
  2.1 0.7 copy-done.4
  2.8 1.3 %shard_map.148 = bf16[2,64,2048]{2,1,0:T(8,128)(2,1)S(1)} custom-call(s32[3]{0:T(128)S(1)} %pad_add_fusion.2.meta_ref, bf16[256,2048]{1,0:T(8,128)(2,1)S(1)} %copy-done.2, f32[1,2048]{1,0:T(1,128)S(1)} %bitcast.51), custom_call_target="tpu_custom_call" | custom-call | flops 134217728 | bytes 2097152 | tf_op jit(solution)/shard_map/pallas_call | solution.py:287
  4.1 3.0 %collective-permute-start.2 = (bf16[2,64,2048]{2,1,0:T(8,128)(2,1)S(1)}, bf16[2,64,2048]{2,1,0:T(8,128)(2,1)S(1)}, u32[]{:S(2)}, u32[]{:S(2)}) collective-permute-start(bf16[2,64,2048]{2,1,0:T(8,128)(2,1)S(1)} %shard_map.148), channel_id=1, source_target_pairs={{0,4},{1,5},{2,6},{3,7},{4,0},{5,1},{6,2},{7,3},{8,12},{9,13},{10,... | collective-permute-start | bytes 1572872 | tf_op jit(solution)/shard_map/ppermute | solution.py:255
  7.1 0.7 slice_bitcast_fusion.3
  7.9 2.6 %collective-permute-start = (bf16[64,2048]{1,0:T(8,128)(2,1)}, bf16[64,2048]{1,0:T(8,128)(2,1)}, u32[]{:S(2)}, u32[]{:S(2)}) collective-permute-start(bf16[64,2048]{1,0:T(8,128)(2,1)} %slice_bitcast_fusion.3), channel_id=1, source_target_pairs={{0,16},{1,17},{2,18},{3,19},{4,20},{5,21},{6,22},{7,23},{8,24},{9,... | collective-permute-start | bytes 786440 | tf_op jit(solution)/shard_map/ppermute | solution.py:255
  10.5 1.3 %fusion.5 = (s32[1]{0:T(128)}, s32[1]{0:T(128)}) fusion(s32[8]{0:T(128)} %lengths_ref.1, s32[]{:T(128)S(6)} %select_n.165, s32[]{:T(128)S(6)} %select_n.154), kind=kLoop, calls=%fused_computation.49 | loop fusion | bytes 24 | tf_op jit(solution)/shard_map/dynamic_slice | solution.py:258
  13.9 1.0 %reshape.128 = s32[8,64,4]{2,1,0:T(8,128)S(1)} reshape(s32[2048]{0:T(1024)} %param.15) | data formatting | bytes 16384 | tf_op jit(solution)/shard_map/reshape | solution.py:277
  14.8 0.7 fusion.4
  15.5 0.7 add_select_fusion
  16.3 0.9 %select_reduce_fusion = s32[25]{0:T(128)S(1)} fusion(s32[256]{0:T(256)} %param.22, s32[25]{0:T(128)} %param.23), kind=kLoop, calls=%fused_computation.18 | loop fusion | flops 19175 | bytes 1224 | tf_op jit(solution)/shard_map/reduce_sum | solution.py:295
  17.1 0.1 fusion
  18.0 0.1 pad_maximum_fusion
  18.1 1.0 %rev.3 = s32[4,4,64]{1,2,0:T(8,128)S(1)} reverse(s32[4,4,64]{1,2,0:T(8,128)} %get-tuple-element.29), dimensions={1,2} | reverse | bytes 8192 | tf_op jit(solution)/shard_map/rev | solution.py:280
  19.1 0.9 %pad_select_fusion.4 = s32[4,4,80]{1,2,0:T(8,128)S(1)} fusion(s32[4,4,64]{1,2,0:T(8,128)S(1)} %rev.3, s32[4,4,64]{1,2,0:T(8,128)} %get-tuple-element.28, s32[4,4]{1,0:T(4,128)S(1)} %add_select_fusion), kind=kLoop, calls=%fused_computation.16 | loop fusion | flops 2560 | bytes 13376 | tf_op jit(solution)/shard_map/jit(_where)/select_n | solution.py:282
  20.0 2.4 %collective-permute-done = bf16[64,2048]{1,0:T(8,128)(2,1)} collective-permute-done((bf16[64,2048]{1,0:T(8,128)(2,1)}, bf16[64,2048]{1,0:T(8,128)(2,1)}, u32[]{:S(2)}, u32[]{:S(2)}) %collective-permute-start) | collective-permute-done | bytes 262176 | tf_op jit(solution)/shard_map/ppermute | solution.py:255
  22.5 1.5 %collective-permute-start.1 = (bf16[64,2048]{1,0:T(8,128)(2,1)}, bf16[64,2048]{1,0:T(8,128)(2,1)}, u32[]{:S(2)}, u32[]{:S(2)}) collective-permute-start(bf16[64,2048]{1,0:T(8,128)(2,1)} %collective-permute-done), channel_id=1, source_target_pairs={{0,2},{1,3},{2,0},{3,1},{4,6},{5,7},{6,4},{7,5},{8,10},{9,11},{10,... | collective-permute-start | bytes 786440 | tf_op jit(solution)/shard_map/ppermute | solution.py:255
  24.0 0.1 copy.21
  24.1 0.1 reshape.130
  24.2 0.1 copy.20.rows_ref
  24.3 1.2 %copy-done.3 = bf16[256,2048]{1,0:T(8,128)(2,1)S(1)} copy-done((bf16[256,2048]{1,0:T(8,128)(2,1)S(1)}, bf16[256,2048]{1,0:T(8,128)(2,1)}, u32[]{:S(2)}) %copy-start.3) | copy-done | bytes 1048600
  25.5 0.8 %shard_map.147 = (f32[25,512]{1,0:T(8,128)S(1)}, f32[1,320]{1,0:T(1,128)S(1)}) custom-call(s32[25,1]{1,0:T(8,128)S(1)} %copy.20.rows_ref, bf16[256,2048]{1,0:T(8,128)(2,1)S(1)} %copy-done.3, bf16[2048,512]{1,0:T(8,128)(2,1)S(1)} %copy-done.1, f32[1,512]{1,0:T(1,128)S(1)} %bitcast.53, f32[25,128]{1,0:T(8,128)S(1)} %get-tuple-element.39.cosine_ref, ...), custom_call_target="tpu_custom_call" | custom-call | flops 52428800 | bytes 2097152 | tf_op jit(solution)/shard_map/pallas_call | solution.py:303
  26.4 0.1 pad_add_fusion.1.meta_ref
  26.5 0.6 collective-permute-start.3
  27.1 1.4 %collective-permute-start.4 = (bf16[64,2048]{1,0:T(8,128)(2,1)}, bf16[64,2048]{1,0:T(8,128)(2,1)S(1)}, u32[]{:S(2)}, u32[]{:S(2)}) collective-permute-start(bf16[64,2048]{1,0:T(8,128)(2,1)} %collective-permute-done), channel_id=1, source_target_pairs={{0,6},{1,7},{2,4},{3,5},{4,2},{5,3},{6,0},{7,1},{8,14},{9,15},{10,... | collective-permute-start | bytes 786440 | tf_op jit(solution)/shard_map/ppermute | solution.py:255
  28.5 1.4 %collective-permute-done.1 = bf16[64,2048]{1,0:T(8,128)(2,1)} collective-permute-done((bf16[64,2048]{1,0:T(8,128)(2,1)}, bf16[64,2048]{1,0:T(8,128)(2,1)}, u32[]{:S(2)}, u32[]{:S(2)}) %collective-permute-start.1) | collective-permute-done | bytes 262176 | tf_op jit(solution)/shard_map/ppermute | solution.py:255
  29.9 1.1 %broadcast_select_fusion.5 = (bf16[64,2048]{1,0:T(8,128)(2,1)S(1)}, bf16[64,2048]{1,0:T(8,128)(2,1)S(1)}, bf16[64,2048]{1,0:T(8,128)(2,1)S(1)}, bf16[64,2048]{1,0:T(8,128)(2,1)S(1)}) fusion(bf16[64,2048]{1,0:T(8,128)(2,1)} %collective-permute-done.1, pred[]{:T(512)S(6)} %lt.110, bf16[2,64,2048]{2,1,0:T(8,128)(2,1)S(1)} %shard_map.148, ...), kind=kLoop, calls=%fused_computation.13 | loop fusion | flops 524288 | bytes 2097153 | tf_op jit(solution)/shard_map/jit(_where)/select_n | solution.py:261
  31.1 0.1 pad_select_fusion.3.refs_0_
  31.2 1.8 %collective-permute-start.6 = (bf16[80,2048]{1,0:T(8,128)(2,1)S(1)}, bf16[80,2048]{1,0:T(8,128)(2,1)S(1)}, u32[]{:S(2)}, u32[]{:S(2)}) collective-permute-start(bf16[80,2048]{1,0:T(8,128)(2,1)S(1)} %pad_select_fusion.3.refs_0_), channel_id=1, source_target_pairs={{0,8},{1,9},{2,10},{3,11},{4,12},{5,13},{6,14},{7,15},{8,0},{9,1},... | collective-permute-start | bytes 983048 | tf_op jit(solution)/shard_map/ppermute | solution.py:255
  33.0 3.0 %collective-permute-done.3 = bf16[64,2048]{1,0:T(8,128)(2,1)S(1)} collective-permute-done((bf16[64,2048]{1,0:T(8,128)(2,1)}, bf16[64,2048]{1,0:T(8,128)(2,1)S(1)}, u32[]{:S(2)}, u32[]{:S(2)}) %collective-permute-start.3) | collective-permute-done | bytes 262176 | tf_op jit(solution)/shard_map/ppermute | solution.py:255
  36.0 3.2 %collective-permute-done.4 = bf16[64,2048]{1,0:T(8,128)(2,1)S(1)} collective-permute-done((bf16[64,2048]{1,0:T(8,128)(2,1)}, bf16[64,2048]{1,0:T(8,128)(2,1)S(1)}, u32[]{:S(2)}, u32[]{:S(2)}) %collective-permute-start.4) | collective-permute-done | bytes 262176 | tf_op jit(solution)/shard_map/ppermute | solution.py:255
  39.2 0.1 broadcast_select_fusion.3
  39.3 0.1 pad_select_fusion.refs_3_
  39.4 1.8 %collective-permute-start.9 = (bf16[80,2048]{1,0:T(8,128)(2,1)S(1)}, bf16[80,2048]{1,0:T(8,128)(2,1)S(1)}, u32[]{:S(2)}, u32[]{:S(2)}) collective-permute-start(bf16[80,2048]{1,0:T(8,128)(2,1)S(1)} %pad_select_fusion.refs_3_), channel_id=1, source_target_pairs={{0,8},{1,9},{2,10},{3,11},{4,12},{5,13},{6,14},{7,15},{8,0},{9,1},... | collective-permute-start | bytes 983048 | tf_op jit(solution)/shard_map/ppermute | solution.py:255
  41.2 1.5 %collective-permute-start.7 = (bf16[80,2048]{1,0:T(8,128)(2,1)S(1)}, bf16[80,2048]{1,0:T(8,128)(2,1)S(1)}, u32[]{:S(2)}, u32[]{:S(2)}) collective-permute-start(bf16[80,2048]{1,0:T(8,128)(2,1)S(1)} %collective-permute-done.6.refs_0_), channel_id=1, source_target_pairs={{0,2},{1,3},{2,0},{3,1},{4,6},{5,7},{6,4},{7,5},{8,10},{9,11},{10,... | collective-permute-start | bytes 983048 | tf_op jit(solution)/shard_map/ppermute | solution.py:255
  42.8 0.5 collective-permute-start.8
  43.3 0.2 pad_select_fusion.1
  43.5 8.5 %shard_map.149 = f32[8,320]{1,0:T(8,128)S(1)} custom-call(s32[3]{0:T(128)S(1)} %pad_add_fusion.1.meta_ref, s32[1,320]{1,0:T(1,128)S(1)} %get-tuple-element.30.targets_ref, bf16[80,2048]{1,0:T(8,128)(2,1)S(1)} %pad_select_fusion.3.refs_0_, bf16[80,2048]{1,0:T(8,128)(2,1)S(1)} %get-tuple-element.38.refs_1_, bf16[80,2048]{1,0:T(8,128)(2,1)S(1)} %get-tuple-element.37.refs_2_, ...), custom_call_target="tpu_custom_call" | custom-call | flops 2055208960 | bytes 7733248 | tf_op jit(solution)/shard_map/pallas_call | solution.py:99
  52.1 0.0 copy-start.5
  52.1 8.5 %shard_map.150 = f32[8,320]{1,0:T(8,128)S(1)} custom-call(s32[3]{0:T(128)S(1)} %pad_add_fusion.1.meta_ref, s32[1,320]{1,0:T(1,128)S(1)} %get-tuple-element.31.targets_ref, bf16[80,2048]{1,0:T(8,128)(2,1)S(1)} %collective-permute-done.6.refs_0_, bf16[80,2048]{1,0:T(8,128)(2,1)S(1)} %collective-permute-done.7.refs_1_, ...), custom_call_target="tpu_custom_call" | custom-call | flops 2055208960 | bytes 7733248 | tf_op jit(solution)/shard_map/pallas_call | solution.py:99
  60.6 0.1 select_select_fusion
  60.7 0.8 broadcast_in_dim.113
  61.5 4.7 %all-to-all-start = ((f32[32,8,320]{2,1,0:T(8,128)}), f32[32,8,320]{2,1,0:T(8,128)S(1)}, u32[]{:S(2)}, u32[]{:S(2)}) async-start(f32[32,8,320]{2,1,0:T(8,128)} %bitcast.20), calls=%async_computation | async-start | bytes 786432 | tf_op jit(solution)/shard_map/all_to_all | solution.py:365
  66.1 1.8 %collective-permute-start.10 = (s32[256]{0:T(256)S(1)}, s32[256]{0:T(256)S(1)}, u32[]{:S(2)}, u32[]{:S(2)}) collective-permute-start(s32[256]{0:T(256)S(1)} %copy-done.9), channel_id=1, source_target_pairs={{0,4},{1,5},{2,6},{3,7},{4,0},{5,1},{6,2},{7,3},{8,12},{9,13},{10,... | collective-permute-start | bytes 3080 | tf_op jit(solution)/shard_map/ppermute | solution.py:255
  68.0 2.1 %collective-permute-done.10 = s32[256]{0:T(256)S(1)} collective-permute-done((s32[256]{0:T(256)S(1)}, s32[256]{0:T(256)S(1)}, u32[]{:S(2)}, u32[]{:S(2)}) %collective-permute-start.10) | collective-permute-done | bytes 1056 | tf_op jit(solution)/shard_map/ppermute | solution.py:255
  70.1 9.2 %all-to-all-done = f32[32,8,320]{2,1,0:T(8,128)S(1)} async-done(((f32[32,8,320]{2,1,0:T(8,128)}), f32[32,8,320]{2,1,0:T(8,128)S(1)}, u32[]{:S(2)}, u32[]{:S(2)}) %all-to-all-start) | async-done | bytes 327712 | tf_op jit(solution)/shard_map/all_to_all | solution.py:365
  79.3 2.2 %shard_map.151 = (f32[1,256]{1,0:T(1,128)}, f32[1,256]{1,0:T(1,128)}, f32[1,4]{1,0:T(1,128)}, bf16[25,512]{1,0:T(8,128)(2,1)}) custom-call(s32[1]{0:T(128)} %bitcast.meta_ref, s32[8]{0:T(128)S(1)} %copy-done.5, s32[8]{0:T(128)S(1)} %copy-done.7, f32[16,2,8,320]{3,2,1,0:T(8,128)S(1)} %bitcast.50, s32[2,256]{1,0:T(2,128)S(1)} %pad_add_fusion.segments_ref, ...), custom_call_target="tpu_custom_call" | custom-call | flops 16777216 | bytes 327680 | tf_op jit(solution)/shard_map/pallas_call | solution.py:367
  (35 shorter events, 0.2 us)
Async XLA Ops:
  0.6 23.7 %copy-start.1 = (bf16[2048,512]{1,0:T(8,128)(2,1)S(1)}, bf16[2048,512]{1,0:T(8,128)(2,1)}, u32[]{:S(2)}) copy-start(bf16[2048,512]{1,0:T(8,128)(2,1)} %weight_ref.1) | copy-start | bytes 6291460
  0.7 1.4 %copy-start.2 = (bf16[256,2048]{1,0:T(8,128)(2,1)S(1)}, bf16[256,2048]{1,0:T(8,128)(2,1)}, u32[]{:S(2)}) copy-start(bf16[256,2048]{1,0:T(8,128)(2,1)} %hidden_ref.1) | copy-start | bytes 3145732
  2.1 0.7 copy-start.4
  2.8 21.4 %copy-start.8 = (s32[25]{0:T(128)S(1)}, s32[25]{0:T(128)}, u32[]{:S(2)}) copy-start(s32[25]{0:T(128)} %param.23) | copy-start | bytes 304
  2.8 21.5 %copy-start.6 = (f32[512]{0:T(512)S(1)}, f32[512]{0:T(512)}, u32[]{:S(2)}) copy-start(f32[512]{0:T(512)} %param.21) | copy-start | bytes 6148
  4.1 35.1 %collective-permute-start.2 = (bf16[2,64,2048]{2,1,0:T(8,128)(2,1)S(1)}, bf16[2,64,2048]{2,1,0:T(8,128)(2,1)S(1)}, u32[]{:S(2)}, u32[]{:S(2)}) collective-permute-start(bf16[2,64,2048]{2,1,0:T(8,128)(2,1)S(1)} %shard_map.148), channel_id=1, source_target_pairs={{0,4},{1,5},{2,6},{3,7},{4,0},{5,1},{6,2},{7,3},{8,12},{9,13},{10,... | collective-permute-start | bytes 1572872 | tf_op jit(solution)/shard_map/ppermute | solution.py:255
  7.9 14.6 %collective-permute-start = (bf16[64,2048]{1,0:T(8,128)(2,1)}, bf16[64,2048]{1,0:T(8,128)(2,1)}, u32[]{:S(2)}, u32[]{:S(2)}) collective-permute-start(bf16[64,2048]{1,0:T(8,128)(2,1)} %slice_bitcast_fusion.3), channel_id=1, source_target_pairs={{0,16},{1,17},{2,18},{3,19},{4,20},{5,21},{6,22},{7,23},{8,24},{9,... | collective-permute-start | bytes 786440 | tf_op jit(solution)/shard_map/ppermute | solution.py:255
  10.5 33.1 %collective-permute-start.5 = (bf16[784,2048]{1,0:T(8,128)(2,1)}, bf16[784,2048]{1,0:T(8,128)(2,1)}, u32[]{:S(2)}, u32[]{:S(2)}) collective-permute-start(bf16[784,2048]{1,0:T(8,128)(2,1)} %refs_4_.3), channel_id=1, source_target_pairs={{0,1},{1,0},{2,3},{3,2},{4,5},{5,4},{6,7},{7,6},{8,9},{9,8},{10,11... | collective-permute-start | bytes 9633800 | tf_op jit(solution)/shard_map/ppermute | solution.py:255
  22.5 7.5 %collective-permute-start.1 = (bf16[64,2048]{1,0:T(8,128)(2,1)}, bf16[64,2048]{1,0:T(8,128)(2,1)}, u32[]{:S(2)}, u32[]{:S(2)}) collective-permute-start(bf16[64,2048]{1,0:T(8,128)(2,1)} %collective-permute-done), channel_id=1, source_target_pairs={{0,2},{1,3},{2,0},{3,1},{4,6},{5,7},{6,4},{7,5},{8,10},{9,11},{10,... | collective-permute-start | bytes 786440 | tf_op jit(solution)/shard_map/ppermute | solution.py:255
  24.3 1.2 %copy-start.3 = (bf16[256,2048]{1,0:T(8,128)(2,1)S(1)}, bf16[256,2048]{1,0:T(8,128)(2,1)}, u32[]{:S(2)}) copy-start(bf16[256,2048]{1,0:T(8,128)(2,1)} %input_ref.1) | copy-start | bytes 3145732
  26.5 9.5 %collective-permute-start.3 = (bf16[64,2048]{1,0:T(8,128)(2,1)}, bf16[64,2048]{1,0:T(8,128)(2,1)S(1)}, u32[]{:S(2)}, u32[]{:S(2)}) collective-permute-start(bf16[64,2048]{1,0:T(8,128)(2,1)} %collective-permute-done), channel_id=1, source_target_pairs={{0,4},{1,5},{2,6},{3,7},{4,0},{5,1},{6,2},{7,3},{8,12},{9,13},{10,... | collective-permute-start | bytes 786440 | tf_op jit(solution)/shard_map/ppermute | solution.py:255
  27.1 12.1 %collective-permute-start.4 = (bf16[64,2048]{1,0:T(8,128)(2,1)}, bf16[64,2048]{1,0:T(8,128)(2,1)S(1)}, u32[]{:S(2)}, u32[]{:S(2)}) collective-permute-start(bf16[64,2048]{1,0:T(8,128)(2,1)} %collective-permute-done), channel_id=1, source_target_pairs={{0,6},{1,7},{2,4},{3,5},{4,2},{5,3},{6,0},{7,1},{8,14},{9,15},{10,... | collective-permute-start | bytes 786440 | tf_op jit(solution)/shard_map/ppermute | solution.py:255
  31.0 12.5 %copy-start = (bf16[784,2048]{1,0:T(8,128)(2,1)S(1)}, bf16[784,2048]{1,0:T(8,128)(2,1)}, u32[]{:S(2)}) copy-start(bf16[784,2048]{1,0:T(8,128)(2,1)} %refs_4_.3) | copy-start | bytes 9633796
  31.2 10.0 %collective-permute-start.6 = (bf16[80,2048]{1,0:T(8,128)(2,1)S(1)}, bf16[80,2048]{1,0:T(8,128)(2,1)S(1)}, u32[]{:S(2)}, u32[]{:S(2)}) collective-permute-start(bf16[80,2048]{1,0:T(8,128)(2,1)S(1)} %pad_select_fusion.3.refs_0_), channel_id=1, source_target_pairs={{0,8},{1,9},{2,10},{3,11},{4,12},{5,13},{6,14},{7,15},{8,0},{9,1},... | collective-permute-start | bytes 983048 | tf_op jit(solution)/shard_map/ppermute | solution.py:255
  39.4 12.6 %collective-permute-start.9 = (bf16[80,2048]{1,0:T(8,128)(2,1)S(1)}, bf16[80,2048]{1,0:T(8,128)(2,1)S(1)}, u32[]{:S(2)}, u32[]{:S(2)}) collective-permute-start(bf16[80,2048]{1,0:T(8,128)(2,1)S(1)} %pad_select_fusion.refs_3_), channel_id=1, source_target_pairs={{0,8},{1,9},{2,10},{3,11},{4,12},{5,13},{6,14},{7,15},{8,0},{9,1},... | collective-permute-start | bytes 983048 | tf_op jit(solution)/shard_map/ppermute | solution.py:255
  41.2 10.8 %collective-permute-start.7 = (bf16[80,2048]{1,0:T(8,128)(2,1)S(1)}, bf16[80,2048]{1,0:T(8,128)(2,1)S(1)}, u32[]{:S(2)}, u32[]{:S(2)}) collective-permute-start(bf16[80,2048]{1,0:T(8,128)(2,1)S(1)} %collective-permute-done.6.refs_0_), channel_id=1, source_target_pairs={{0,2},{1,3},{2,0},{3,1},{4,6},{5,7},{6,4},{7,5},{8,10},{9,11},{10,... | collective-permute-start | bytes 983048 | tf_op jit(solution)/shard_map/ppermute | solution.py:255
  42.8 9.3 %collective-permute-start.8 = (bf16[80,2048]{1,0:T(8,128)(2,1)S(1)}, bf16[80,2048]{1,0:T(8,128)(2,1)S(1)}, u32[]{:S(2)}, u32[]{:S(2)}) collective-permute-start(bf16[80,2048]{1,0:T(8,128)(2,1)S(1)} %collective-permute-done.6.refs_0_), channel_id=1, source_target_pairs={{0,4},{1,5},{2,6},{3,7},{4,0},{5,1},{6,2},{7,3},{8,12},{9,13},{10,... | collective-permute-start | bytes 983048 | tf_op jit(solution)/shard_map/ppermute | solution.py:255
  52.1 14.1 %copy-start.9 = (s32[256]{0:T(256)S(1)}, s32[256]{0:T(256)}, u32[]{:S(2)}) copy-start(s32[256]{0:T(256)} %param.17) | copy-start | bytes 3076
  52.1 27.2 %copy-start.5 = (s32[8]{0:T(128)S(1)}, s32[8]{0:T(128)}, u32[]{:S(2)}) copy-start(s32[8]{0:T(128)} %lengths_ref.1) | copy-start | bytes 100
  52.1 27.2 %copy-start.7 = (s32[8]{0:T(128)S(1)}, s32[8]{0:T(128)}, u32[]{:S(2)}) copy-start(s32[8]{0:T(128)} %continues_ref.1) | copy-start | bytes 100
  61.5 17.9 %all-to-all-start = ((f32[32,8,320]{2,1,0:T(8,128)}), f32[32,8,320]{2,1,0:T(8,128)S(1)}, u32[]{:S(2)}, u32[]{:S(2)}) async-start(f32[32,8,320]{2,1,0:T(8,128)} %bitcast.20), calls=%async_computation | async-start | bytes 786432 | tf_op jit(solution)/shard_map/all_to_all | solution.py:365
  66.1 3.9 %collective-permute-start.10 = (s32[256]{0:T(256)S(1)}, s32[256]{0:T(256)S(1)}, u32[]{:S(2)}, u32[]{:S(2)}) collective-permute-start(s32[256]{0:T(256)S(1)} %copy-done.9), channel_id=1, source_target_pairs={{0,4},{1,5},{2,6},{3,7},{4,0},{5,1},{6,2},{7,3},{8,12},{9,13},{10,... | collective-permute-start | bytes 3080 | tf_op jit(solution)/shard_map/ppermute | solution.py:255

commit v2 on v1

v2 whole, which is shorter than its diff:
```python
import functools

import jax
import jax.numpy as jnp
from jax import lax
from jax.experimental import pallas as pl
from jax.experimental.pallas import tpu as pltpu
from jax.sharding import PartitionSpec as P

HD = 128
SEGS = 4
BAL = 160
CORES = 2
LANES = 128
BREAKS = 31

NORM_EPS = 1e-06
ROPE_BASE = 500000.0

VMEM_LIMIT = 24 * 1024 * 1024
WHOLE = pl.BlockSpec(memory_space=pltpu.VMEM)
SCALARS = pl.BlockSpec(memory_space=pltpu.SMEM)
FAR = pl.BlockSpec(memory_space=pltpu.HBM)


def call(kernel, out_shape, in_specs, flops, moved, vmem=VMEM_LIMIT, **more):
    return pl.pallas_call(
        kernel,
        out_shape=out_shape,
        in_specs=in_specs,
        compiler_params=pltpu.CompilerParams(vmem_limit_bytes=vmem),
        cost_estimate=pl.CostEstimate(flops=flops, bytes_accessed=moved, transcendentals=0),
        **more,
    )


def place_of(shards):
    shard = lax.axis_index("vocab")
    return lax.axis_index("grp"), lax.div(shard, CORES), lax.rem(shard, CORES)


def source_row(place, quarter, is_first, quarters, rows):
    return jnp.where(
        is_first,
        quarters * place + quarter,
        quarters * (rows - 1 - place) + quarters - 1 - quarter,
    )


def front(length, quarter, shards):
    return lax.div(length - quarter + shards - 1, shards)


def fetch(sources, targets, semaphores):
    copies = [
        pltpu.make_async_copy(source, target, semaphores.at[i])
        for i, (source, target) in enumerate(zip(sources, targets))
    ]
    for copy in copies:
        copy.start()
    return copies


def prep_kernel(sizes, hidden_ref, gain_ref, *refs):
    *known, out_ref = refs
    groups, shards = sizes
    rows, width = out_ref.shape[-2:]
    group, y, core = place_of(shards)
    place = lax.broadcasted_iota(jnp.int32, (rows, hidden_ref.shape[0]), 0)
    column = lax.broadcasted_iota(jnp.int32, place.shape, 1)
    for t, known_ref in enumerate(known):
        out_ref[t] = known_ref[...]
    for t in range(len(known), out_ref.shape[0] if known else 1):
        row = source_row(place, (y ^ t) * CORES + core, group < groups // 2, shards, rows)
        pick = (column == row).astype(jnp.float32).astype(jnp.bfloat16)
        dealt = jnp.dot(pick, hidden_ref[...], preferred_element_type=jnp.float32)
        meansq = jnp.sum(dealt * dealt, axis=-1, keepdims=True) / width
        dealt = (dealt * lax.rsqrt(meansq + NORM_EPS) * gain_ref[...]).astype(jnp.bfloat16)
        if known:
            out_ref[t] = dealt
        else:
            out_ref[...] = dealt


def pack(out_ref, start, is_first, own, other, length, quarter, shards):
    rows = own.shape[0]
    size = 2 * BAL // shards
    gap = size - rows
    place = lax.broadcasted_iota(jnp.int32, (rows - gap, own.shape[1]), 0) + gap
    is_lower = place < front(length, quarter, shards)

    def lay(lower, upper):
        middle = jnp.where(
            is_lower, lower[gap:rows, :].astype(jnp.float32), upper[0 : rows - gap, :].astype(jnp.float32)
        )
        out_ref[start : start + gap, :] = lower[0:gap, :]
        out_ref[start + gap : start + rows, :] = middle.astype(jnp.bfloat16)
        out_ref[start + rows : start + size, :] = upper[rows - gap : rows, :]

    @pl.when(is_first)
    def _():
        lay(own, other)

    @pl.when(jnp.logical_not(is_first))
    def _():
        lay(other, own)


def merge_kernel(sizes, flips, lengths_ref, own_ref, other_ref, out_ref):
    groups, shards = sizes
    x_flip, y_flip = flips
    half = groups // 2
    group, y, core = place_of(shards)
    own = own_ref if len(own_ref.shape) == 2 else own_ref.at[y_flip]
    pack(
        out_ref,
        0,
        group < half,
        own,
        other_ref,
        lengths_ref[lax.rem(group, half) ^ x_flip],
        (y ^ y_flip) * CORES + core,
        shards,
    )


def statistics(bases, targets, tokens, heads):
    state = None
    for base, head_ref in zip(bases, heads):
        logits = lax.dot_general(
            head_ref[...], tokens, (((1,), (1,)), ((), ())), preferred_element_type=jnp.float32
        )
        logits = logits.astype(jnp.bfloat16).astype(jnp.float32)
        entry = lax.broadcasted_iota(jnp.int32, logits.shape, 0)
        found = jnp.where(entry == targets - base, logits, 0.0)
        picked = jnp.sum(found, axis=0, keepdims=True)
        top = jnp.max(logits, axis=0, keepdims=True)
        if state is not None:
            top = jnp.maximum(top, state[0])
        shifted = jnp.exp(logits - top)
        expsum = jnp.sum(shifted, axis=0, keepdims=True)
        moment = jnp.sum(shifted * logits, axis=0, keepdims=True)
        if state is not None:
            scale = jnp.exp(state[0] - top)
            expsum += state[1] * scale
            moment += state[2] * scale
            picked += state[3]
        state = (top, expsum, moment, picked)
    top, expsum, moment, picked = state
    return top + jnp.log(expsum), moment / expsum, picked


def packed(state, extra):
    flat = [row[:, : 2 * LANES] for row in state] + [row[:, 2 * LANES :] for row in state] + [extra]
    flat = jnp.concatenate(flat, axis=1)
    return jnp.concatenate(
        [flat[:, i : i + LANES] for i in range(0, flat.shape[1], LANES)], axis=0
    )


def unpacked(every):
    places = ((0, 6, 0), (2, 6, LANES // 2), (4, 7, 0))
    return [
        jnp.concatenate(
            [
                every[:, row : row + 1, :],
                every[:, row + 1 : row + 2, :],
                every[:, last : last + 1, start : start + LANES // 2],
            ],
            axis=2,
        )
        for row, last, start in places
    ]


def bases_of(sizes, head_ref):
    groups, shards = sizes
    group, shard = lax.axis_index("grp"), lax.axis_index("vocab")
    return [((shard ^ flip) * groups + group) * head_ref.shape[0] for flip in (0, 1)]


def rows_of(state, out_ref):
    rows = jnp.concatenate([*state, jnp.zeros((5, out_ref.shape[1]), jnp.float32)], axis=0)
    out_ref[...] = rows


def plain_kernel(sizes, targets_ref, near_ref, far_ref, tokens_ref, out_ref):
    state = statistics(
        bases_of(sizes, near_ref), targets_ref[...], tokens_ref[...], (near_ref, far_ref)
    )
    rows_of(state, out_ref)


def early_kernel(
    sizes,
    lengths_ref,
    targets_ref,
    near_ref,
    far_ref,
    own_ref,
    dealt_ref,
    other_y_ref,
    across_ref,
    other_x_ref,
    own_xy_ref,
    far_own_ref,
    out_ref,
    tokens_ref,
):
    groups, shards = sizes
    half = groups // 2
    group, y, core = place_of(shards)
    is_first, column = group < half, lax.rem(group, half)
    size = own_ref.shape[0]
    quarter = y * CORES + core
    tokens_ref[0:size, :] = own_ref[...]
    lower = lengths_ref[column]
    pack(tokens_ref, size, is_first, dealt_ref.at[1], other_y_ref, lower, quarter ^ CORES, shards)
    lower = lengths_ref[column ^ 1]
    pack(tokens_ref, 2 * size, is_first, across_ref.at[0], other_x_ref, lower, quarter, shards)
    tokens_ref[3 * size : 4 * size, :] = own_xy_ref[...]
    tokens_ref[4 * size : 5 * size, :] = far_own_ref[...]
    state = statistics(
        bases_of(sizes, near_ref), targets_ref[...], tokens_ref[...], (near_ref, far_ref)
    )
    rows_of(state, out_ref)


def send_kernel(sizes, targets_ref, near_ref, far_ref, early_ref, extra_ref, *refs):
    *pieces, out_ref, tokens_ref = refs
    groups, shards = sizes
    size = pieces[0].shape[0]
    for t, piece in enumerate(pieces):
        tokens_ref[t * size : (t + 1) * size, :] = piece[...]
    state = statistics(
        bases_of(sizes, near_ref), targets_ref[...], tokens_ref[...], (near_ref, far_ref)
    )
    tokens = early_ref.shape[1] - size
    early = [early_ref[i : i + 1, :] for i in range(3)]
    own = packed([row[:, :tokens] for row in early], extra_ref[...])
    beyond = [jnp.concatenate([row[:, tokens:], late], axis=1) for row, late in zip(early, state)]
    beyond = packed(beyond, extra_ref[...])
    mine = lax.div(lax.rem(lax.axis_index("grp"), groups // 2), 2)
    for which in range(groups // 4):
        block = jnp.where(mine == which, own, beyond)
        for group in range(groups):
            if group % (groups // 2) // 2 == which:
                for shard in range(shards):
                    out_ref[group * shards + shard] = block


def score(kernel, out_shape, targets, heads, extras, count, scratch=True, scalars=()):
    vocab, width = heads[0].shape
    return call(
        kernel,
        out_shape,
        [SCALARS] * len(scalars) + [WHOLE] * (3 + len(extras)),
        4 * vocab * count * width,
        4 * vocab * width + 2 * count * width,
        out_specs=WHOLE,
        scratch_shapes=[pltpu.VMEM((count, width), jnp.bfloat16)] if scratch else [],
    )(*scalars, targets, *heads, *extras)


def upright(row):
    count = row.shape[1]
    diagonal = lax.broadcasted_iota(jnp.int32, (count, count), 0) == lax.broadcasted_iota(
        jnp.int32, (count, count), 1
    )
    return jnp.sum(jnp.where(diagonal, row, 0), axis=1, keepdims=True)


def side_kernel(
    sizes,
    swapped,
    lengths_ref,
    rows_ref,
    positions_ref,
    segments_ref,
    ids_ref,
    gain_ref,
    input_hbm,
    weight_hbm,
    turned_ref,
    extra_ref,
    early_ref,
    late_ref,
    input_ref,
    weight_ref,
    semaphores,
):
    groups, shards = sizes
    copies = fetch((input_hbm, weight_hbm), (input_ref, weight_ref), semaphores)
    cap = segments_ref.shape[1]
    if swapped:
        tokens = (early_ref.shape[1] + late_ref.shape[1]) // 2
        half, size = groups // 2, 2 * BAL // shards
        group, y, core = place_of(shards)
        lane = lax.broadcasted_iota(jnp.int32, (1, 2 * tokens), 1)
        row = jnp.zeros((1, 2 * tokens), jnp.int32)
        source = jnp.zeros((1, 2 * tokens), jnp.int32)
        for slot in range(8):
            place = lane - slot * size
            lower = lax.rem(group, half) ^ (slot // 4 * 2) ^ (slot // 2 % 2)
            quarter = (y ^ (slot % 2)) * CORES + core
            is_lower = place < front(lengths_ref[lower], quarter, shards)
            here = (place >= 0) & (place < size)
            stands = jnp.where(
                is_lower, shards * place + quarter, shards * (size - 1 - place) + shards - 1 - quarter
            )
            row = jnp.where(here, stands, row)
            source = jnp.where(here, jnp.where(is_lower, lower, lower + half), source)
        ids = jnp.concatenate([ids_ref[0:1, g * cap : (g + 1) * cap] for g in range(groups)], axis=0)
        halves = jnp.concatenate([ids >> 8, ids & 255], axis=0)
        stood = lax.broadcasted_iota(jnp.int32, (cap, 2 * tokens), 0)
        pick = (stood == row).astype(jnp.float32).astype(jnp.bfloat16)
        found = jnp.dot(
            halves.astype(jnp.float32).astype(jnp.bfloat16), pick, preferred_element_type=jnp.float32
        )
        found = found[:groups] * 256.0 + found[groups:]
        of_group = lax.broadcasted_iota(jnp.int32, found.shape, 0) == source
        targets = jnp.sum(jnp.where(of_group, found, 0.0), axis=0, keepdims=True).astype(jnp.int32)
        early_ref[...] = targets[:, : early_ref.shape[1]]
        late_ref[...] = targets[:, early_ref.shape[1] :]
    else:
        early_ref[...] = jnp.zeros_like(early_ref)
        late_ref[...] = jnp.zeros_like(late_ref)

    count, width = turned_ref.shape
    column = lax.broadcasted_iota(jnp.int32, (count, cap), 1)
    chosen = column == upright(rows_ref[...])
    places = jnp.sum(jnp.where(chosen, positions_ref[...], 0), axis=1, keepdims=True)
    half_head = HD // 2
    steps = lax.broadcasted_iota(jnp.int32, (count, half_head), 1).astype(jnp.float32)
    freqs = jnp.exp(-(2.0 * steps / HD) * jnp.log(jnp.full(steps.shape, ROPE_BASE, jnp.float32)))
    angles = places.astype(jnp.float32) * freqs
    cosine, sine = jnp.cos(angles), jnp.sin(angles)
    cosine = jnp.concatenate([cosine, cosine], axis=1)
    sine = jnp.concatenate([-sine, sine], axis=1)
    for copy in copies:
        copy.wait()
    pick = chosen.astype(jnp.float32).astype(jnp.bfloat16)
    rows = jnp.dot(pick, input_ref[...], preferred_element_type=jnp.float32).astype(jnp.bfloat16)
    projected = jnp.dot(rows, weight_ref[...], preferred_element_type=jnp.float32)
    squares = jnp.sum(projected * projected, axis=1, keepdims=True)
    lane = lax.broadcasted_iota(jnp.int32, (count, extra_ref.shape[1]), 1)
    diagonal = lax.broadcasted_iota(jnp.int32, lane.shape, 0) == lane
    extra = jnp.sum(jnp.where(diagonal, squares, 0.0), axis=0, keepdims=True)
    for label in range(1, SEGS):
        before = (segments_ref[...] < label).astype(jnp.float32)
        before = jnp.sum(before, axis=1, keepdims=True)
        extra = jnp.where(lane[0:1] == BREAKS + label, before, extra)
    extra_ref[...] = extra
    gained = projected * gain_ref[...]
    for start in range(0, width, HD):
        head = gained[:, start : start + HD]
        turned_ref[:, start : start + HD] = head * cosine + pltpu.roll(head, half_head, 1) * sine


def combine(tops, expsums, moments, pickeds):
    top = jnp.max(tops, axis=0)
    scale = jnp.exp(tops - top[None])
    return (
        top,
        jnp.sum(expsums * scale, axis=0),
        jnp.sum(moments * scale, axis=0),
        jnp.sum(pickeds, axis=0),
    )


def final_kernel(
    sizes,
    swapped,
    lengths_ref,
    continues_ref,
    got_ref,
    segments_ref,
    turned_ref,
    logprob_ref,
    entropy_ref,
    mean_ref,
    keys_ref,
):
    groups, shards = sizes
    parts, group = shards // CORES, lax.axis_index("grp")
    cap = segments_ref.shape[1]
    size = 2 * BAL // shards
    tokens = 2 * parts * size
    columns = []
    for core in range(CORES):
        if swapped:
            whole = []
            for x in range(2):
                for y in range(parts):
                    lse, mean, picked = unpacked(got_ref[:, x, y, core])
                    merged = combine(lse, jnp.ones_like(lse), mean, picked)
                    blocks = [(x * parts + y) ^ slot for slot in range(2 * parts)]
                    rows = jnp.concatenate(merged, axis=0)
                    rows = [rows[:, b * size : (b + 1) * size] for b in blocks]
                    whole.append(jnp.concatenate(rows, axis=1))
            whole = jnp.stack(whole)
            merged = combine(*(whole[:, i : i + 1, :] for i in range(4)))
        else:
            every = got_ref[:, :, :, core]
            every = every.reshape((groups * parts,) + every.shape[3:])
            lse, mean, picked = unpacked(every)
            merged = combine(lse, jnp.ones_like(lse), mean, picked)
        top, expsum, moment, picked = merged
        lse = top + jnp.log(expsum)
        columns.append(jnp.concatenate([picked - lse, lse - moment / expsum], axis=0))

    column, span = lax.rem(group, 2), tokens // 2
    halves = [[both[:, :span], both[:, span:]] for both in columns]
    own = jnp.concatenate([jnp.where(column == 0, a, b) for a, b in halves], axis=1)
    beside = jnp.concatenate([jnp.where(column == 0, b, a) for a, b in halves], axis=1)
    rest = jnp.concatenate([own, beside], axis=0)
    terms = []
    for _ in range(3):
        term = rest.astype(jnp.bfloat16).astype(jnp.float32)
        terms.append(term)
        rest = rest - term
    terms = jnp.concatenate(terms + [jnp.zeros_like(rest)], axis=0).astype(jnp.bfloat16)

    slots = lax.broadcasted_iota(jnp.int32, (1, cap), 1)
    is_first = group < groups // 2
    quarter = jnp.where(is_first, slots % shards, shards - 1 - slots % shards)
    place = jnp.where(is_first, slots // shards, size - 1 - slots // shards)
    home = quarter % CORES * span + quarter // CORES * size + place
    stood = lax.broadcasted_iota(jnp.int32, (CORES * span, cap), 0)
    pick = (stood == home).astype(jnp.float32).astype(jnp.bfloat16)
    found = jnp.dot(terms, pick, preferred_element_type=jnp.float32)
    found = found[0:4] + found[4:8] + found[8:12]
    labels = lax.broadcasted_iota(jnp.int32, (1, SEGS), 1)

    def summed(who, logprob, breaks):
        live = slots < lengths_ref[who]
        logprob = jnp.where(live, logprob, 0.0)
        sums = jnp.zeros((1, SEGS), jnp.float32)
        counts = jnp.zeros((1, SEGS), jnp.float32)
        for label in range(SEGS):
            member = live
            if label > 0:
                member = member & (slots >= breaks[label - 1])
            if label < SEGS - 1:
                member = member & (slots < breaks[label])
            one_sum = jnp.sum(jnp.where(member, logprob, 0.0), axis=1, keepdims=True)
            one_count = jnp.sum(member.astype(jnp.float32), axis=1, keepdims=True)
            sums = jnp.where(labels == label, one_sum, sums)
            counts = jnp.where(labels == label, one_count, counts)
        return logprob, sums, counts

    partner = group ^ 1
    messages = [got_ref[who // 2, who % 2, 0, 0][7:8, LANES // 2 :] for who in (group, partner)]
    breaks = [
        [message[:, BREAKS + i : BREAKS + i + 1].astype(jnp.int32) for i in range(1, SEGS)]
        for message in messages
    ]
    logprob, sums, counts = summed(group, found[0:1], breaks[0])
    _, partner_sums, partner_counts = summed(partner, found[2:3], breaks[1])
    entropy = jnp.where(slots < lengths_ref[group], found[1:2], 0.0)
    segments = segments_ref[...]
    is_even = group % 2 == 0
    joined = jnp.where(is_even, continues_ref[group], continues_ref[partner]) == 1
    last = slots == lengths_ref[group] - 1
    my_last = jnp.sum(jnp.where(last, segments, 0), axis=1, keepdims=True)
    partner_last = jnp.max(jnp.where(partner_counts > 0, labels, 0), axis=1, keepdims=True)
    wanted = jnp.where(is_even, jnp.zeros_like(partner_last), partner_last)
    extra_sum = jnp.sum(jnp.where(labels == wanted, partner_sums, 0.0), axis=1, keepdims=True)
    extra_count = jnp.sum(jnp.where(labels == wanted, partner_counts, 0.0), axis=1, keepdims=True)
    target = jnp.where(is_even, my_last, jnp.zeros_like(my_last))
    update = joined & (labels == target)
    total_sum = sums + jnp.where(update, extra_sum, 0.0)
    total_count = counts + jnp.where(update, extra_count, 0.0)
    logprob_ref[...] = logprob
    entropy_ref[...] = entropy
    mean_ref[...] = total_sum / jnp.maximum(total_count, 1.0)

    count, width = turned_ref.shape
    squares = jnp.zeros((1, count), jnp.float32)
    for part in range(parts):
        for core in range(CORES):
            squares += got_ref[group // 2, group % 2, part, core][7:8, LANES // 2 : LANES // 2 + count]
    squares = upright(squares)
    scale = jnp.sqrt(squares / (width * shards) + NORM_EPS)
    keys_ref[...] = (turned_ref[...] / scale).astype(jnp.bfloat16)


def partners(sizes, flips):
    (groups, shards), (group_flip, shard_flip) = sizes, flips
    return [
        (g * shards + v, (g ^ group_flip) * shards + (v ^ shard_flip))
        for g in range(groups)
        for v in range(shards)
    ]


def local(
    sizes,
    final_hidden,
    norm_gain,
    head_weight,
    token_ids,
    group_lengths,
    segment_ids,
    continues,
    layer_input,
    key_weight,
    key_gain,
    positions,
    key_rows,
):
    groups, shards = sizes
    parts, half = shards // CORES, groups // 2
    cap, width = final_hidden.shape
    rows = cap // shards
    size = 2 * BAL // shards
    tokens = 2 * parts * size
    core = lax.axis_index("vocab") % CORES
    axes = ("grp", "vocab")
    swapped = sizes == (8, 4)

    def swap(array, group_flip, shard_flip):
        return lax.ppermute(array, axes, partners(sizes, (group_flip, shard_flip)))

    def merge(own, other, flips):
        return call(
            functools.partial(merge_kernel, sizes, flips),
            jax.ShapeDtypeStruct((size, width), jnp.bfloat16),
            [SCALARS, WHOLE, WHOLE],
            size * width,
            4 * size * width,
            out_specs=WHOLE,
        )(group_lengths, own, other)

    def prep(shape, *known):
        return call(
            functools.partial(prep_kernel, sizes),
            jax.ShapeDtypeStruct(shape, jnp.bfloat16),
            [WHOLE] * (2 + len(known)),
            2 * rows * cap * width,
            4 * cap * width,
            out_specs=WHOLE,
        )(final_hidden, norm_gain.reshape(1, width), *known)

    here = prep((rows, width))
    count, key_width = key_rows.shape[0], key_weight.shape[1]
    turned, extra, early_ids, late_ids = call(
        functools.partial(side_kernel, sizes, swapped),
        (
            jax.ShapeDtypeStruct((count, key_width), jnp.float32),
            jax.ShapeDtypeStruct((1, LANES // 2), jnp.float32),
            jax.ShapeDtypeStruct((1, tokens + size), jnp.int32),
            jax.ShapeDtypeStruct((1, tokens - size), jnp.int32),
        ),
        [SCALARS] + [WHOLE] * 5 + [FAR, FAR],
        2 * count * width * key_width,
        2 * width * key_width,
        scratch_shapes=[
            pltpu.VMEM(layer_input.shape, jnp.bfloat16),
            pltpu.VMEM(key_weight.shape, jnp.bfloat16),
            pltpu.SemaphoreType.DMA((2,)),
        ],
    )(
        group_lengths,
        key_rows.reshape(1, count),
        positions.reshape(1, cap),
        segment_ids.reshape(1, cap),
        token_ids.reshape(1, groups * cap),
        key_gain.reshape(1, key_width),
        layer_input,
        key_weight,
    )

    far_head = swap(head_weight, 0, 1)
    heads = (head_weight, far_head)
    sent_shape = jax.ShapeDtypeStruct((groups * shards, 8, LANES), jnp.float32)
    if swapped:
        other = swap(here, 4, 0)
        dealt = prep((parts, rows, width), here)
        across = swap(dealt, 1, 0)
        other, across, far_head, early_ids, late_ids, extra, turned = lax.optimization_barrier(
            (other, across, far_head, early_ids, late_ids, extra, turned)
        )
        heads = (head_weight, far_head)
        own = merge(here, other, (0, 0))
        other_xy = swap(other, 1, 2)
        far_own = swap(own, 2, 0)
        other_x = swap(other, 1, 0)
        other_y = swap(other, 0, 2)
        own_xy = merge(across, other_xy, (1, 1))
        far_x = swap(far_own, 1, 0)
        far_y = swap(far_own, 0, 2)
        far_xy = swap(own_xy, 2, 0)
        early = score(
            functools.partial(early_kernel, sizes),
            jax.ShapeDtypeStruct((8, tokens + size), jnp.float32),
            early_ids,
            heads,
            (own, dealt, other_y, across, other_x, own_xy, far_own),
            tokens + size,
            scalars=(group_lengths,),
        )
        sent = score(
            functools.partial(send_kernel, sizes),
            sent_shape,
            late_ids,
            heads,
            (early, extra, far_y, far_x, far_xy),
            tokens - size,
        )
    else:
        gap = size - rows
        taken = front(group_lengths[:half, None], jnp.arange(shards)[None, :], shards)
        ids = token_ids.reshape(groups, rows, shards).transpose(0, 2, 1)
        lower = jnp.pad(ids[:half], ((0, 0), (0, 0), (0, gap)))
        upper = jnp.pad(ids[half:, ::-1, ::-1], ((0, 0), (0, 0), (gap, 0)))
        is_lower = jnp.arange(size)[None, None, :] < taken[:, :, None]
        ids = jnp.where(is_lower, lower, upper).reshape(half, parts, CORES, size)
        ids = lax.dynamic_index_in_dim(ids, core, 2, False).reshape(1, -1)
        every = lax.all_gather(here, axes).reshape(groups, parts, CORES, rows, width)
        every = lax.dynamic_index_in_dim(every, core, 2, False)
        first = jnp.pad(every[:half], ((0, 0), (0, 0), (0, gap), (0, 0)))
        second = jnp.pad(every[half:], ((0, 0), (0, 0), (gap, 0), (0, 0)))
        is_lower = is_lower.reshape(half, parts, CORES, size)
        is_lower = lax.dynamic_index_in_dim(is_lower, core, 2, False)
        every = jnp.where(is_lower[..., None], first, second)
        stats = score(
            functools.partial(plain_kernel, sizes),
            jax.ShapeDtypeStruct((8, half // 2 * tokens), jnp.float32),
            ids,
            heads,
            (every.reshape(-1, width),),
            half // 2 * tokens,
            scratch=False,
        )
        sets = half // 2
        state = [row.reshape(sets, tokens) for row in stats[:3]]
        extra = jnp.broadcast_to(extra, (sets, LANES // 2))
        stats = packed(state, extra).reshape(8, sets, LANES).transpose(1, 0, 2)
        sent = jnp.broadcast_to(
            stats[None, :, None, None], (2, sets, 2, shards, 8, LANES)
        ).reshape(sent_shape.shape)
    got = lax.all_to_all(sent, axes, 0, 0, tiled=False)

    logprob, entropy, means, keys = call(
        functools.partial(final_kernel, sizes, swapped),
        (
            jax.ShapeDtypeStruct((1, cap), jnp.float32),
            jax.ShapeDtypeStruct((1, cap), jnp.float32),
            jax.ShapeDtypeStruct((1, SEGS), jnp.float32),
            jax.ShapeDtypeStruct((count, key_width), jnp.bfloat16),
        ),
        [SCALARS] * 2 + [WHOLE] * 3,
        1 << 24,
        4 * groups * shards * 8 * LANES,
    )(
        group_lengths,
        continues,
        got.reshape(half, 2, parts, CORES, 8, LANES),
        segment_ids.reshape(1, cap),
        turned,
    )
    return logprob.reshape(cap), entropy.reshape(cap), means.reshape(SEGS), keys


def solution(mesh):
    sizes = (mesh.shape["grp"], mesh.shape["vocab"])
    in_specs = (
        P("grp", None),
        P(),
        P(("vocab", "grp"), None),
        P(),
        P(),
        P("grp"),
        P(),
        P("grp", None),
        P(None, "vocab"),
        P("vocab"),
        P("grp"),
        P("grp"),
    )
    out_specs = (P("grp"), P("grp"), P("grp"), P("grp", "vocab"))
    return jax.shard_map(
        functools.partial(local, sizes),
        mesh=mesh,
        in_specs=in_specs,
        out_specs=out_specs,
        check_vma=False,
    )
```

time: 82.3 us -> 61.9 us (0.75)
  blocking collectives: 0 us -> 12.6 us
  Pallas kernels: 21.4 us -> 13.4 us
  starting transfers between devices: 21.3 us -> 13.4 us
  waiting for transfers between devices: 21.4 us -> 15.4 us
  other arithmetic: 4.71 us -> 0 us
  local copies, waits for them, and re-layouts: 9.12 us -> 6 us
  between operations: 3.65 us -> 0.75 us
    all_to_all x0 -> x1, blocking collectives: none -> 12.6 us  [local(): got = lax.all_to_all(sent, axes, 0, 0, tiled=False)]
    all_to_all x1 -> x0, waiting for transfers between devices: 9.22 us -> none  [local(): got = lax.all_to_all(sent, axes, 0, 0, tiled=False)]
    pallas_call x5 -> x8, Pallas kernels: 21.4 us -> 13.4 us  [the longest x2 7.56 us: score(): call(kernel, out_shape, [SCALARS] * len(scalars) + [WHOLE] * (3 + len(ext...]
    all_to_all x1 -> x0, starting transfers between devices: 4.67 us -> none  [local(): got = lax.all_to_all(sent, axes, 0, 0, tiled=False)]
    select_n x8 -> x0, other arithmetic: 3.4 us -> none  [the longest x2 1.17 us: merge(): first = jnp.where(is_first, own, other)]
    ppermute x11 -> x10, waiting for transfers between devices: 12.2 us -> 15.4 us  [swap(): return lax.ppermute(array, axes, partners(sizes, (group_flip, shard_flip)))]
    ppermute x11 -> x10, starting transfers between devices: 16.6 us -> 13.4 us  [swap(): return lax.ppermute(array, axes, partners(sizes, (group_flip, shard_flip)))]
    unnamed x20 -> x28, local copies, waits for them, and re-layouts: 3.31 us -> 6 us
  transfers between devices with their start and end apart: 12 -> 10, of which waited for: 6 -> 6; matrix products, arithmetic and copies ran while one was open for 12% -> 0% of each run, Pallas kernels for 11% -> 13%
where the time goes in v2:
time: 61.9 us; the launch traced here: 61.6 us
  waiting for transfers between devices  15.4 us (25%)
  starting transfers between devices  13.4 us (22%)
  Pallas kernels  13.4 us (22%)
  blocking collectives  12.6 us (20%)
  local copies, waits for them, and re-layouts  6 us (10%)
  between operations  0.75 us (1%)
    ppermute x10, waiting for transfers between devices, swap(): return lax.ppermute(array, axes, partners(sizes, (group_flip, shard_flip)))  15.4 us
    ppermute x10, starting transfers between devices, swap(): return lax.ppermute(array, axes, partners(sizes, (group_flip, shard_flip)))  13.4 us
    all_to_all x1, blocking collectives, local(): got = lax.all_to_all(sent, axes, 0, 0, tiled=False)  12.6 us
    pallas_call x2, Pallas kernels, score(): call(kernel, out_shape, [SCALARS] * len(scalars) + [WHOLE] * (3 + len(ext...  7.56 us
    unnamed x28, local copies, waits for them, and re-layouts  6 us
    pallas_call x1, Pallas kernels, local(): call(functools.partial(final_kernel, sizes, swapped), (jax.ShapeDtypeStru...  1.9 us
    pallas_call x1, Pallas kernels, local(): call(functools.partial(side_kernel, sizes, swapped), (jax.ShapeDtypeStruc...  1.89 us
  transfers between devices with their start and end apart: 10, of which 6 were waited for; matrix products, arithmetic and copies ran while one was open for 0% of the time, Pallas kernels for 13%

profile of v2, /device:TPU:0, one launch (start us, length us, event | category | flops | bytes accessed | tf_op | source)
XLA Modules:
  0.0 61.6 jit_solution(3351170224346643926)
XLA Ops:
  0.6 0.5 collective-permute-start.2
  1.1 0.0 copy-start
  1.2 1.2 %copy-done = bf16[256,2048]{1,0:T(8,128)(2,1)S(1)} copy-done((bf16[256,2048]{1,0:T(8,128)(2,1)S(1)}, bf16[256,2048]{1,0:T(8,128)(2,1)}, u32[]{:S(2)}) %copy-start) | copy-done | bytes 1048600
  2.4 0.7 %copy-done.4 = f32[2048]{0:T(1024)S(1)} copy-done((f32[2048]{0:T(1024)S(1)}, f32[2048]{0:T(1024)}, u32[]{:S(2)}) %copy-start.4) | copy-done | bytes 8216
  3.1 0.4 shard_map.147.refs_0_.own_ref
  3.5 0.0 copy-start.1
  3.5 0.4 shard_map.148.dealt_ref
  3.9 2.6 %collective-permute-start.1 = (bf16[2,64,2048]{2,1,0:T(8,128)(2,1)S(1)}, bf16[2,64,2048]{2,1,0:T(8,128)(2,1)S(1)}, u32[]{:S(2)}, u32[]{:S(2)}) collective-permute-start(bf16[2,64,2048]{2,1,0:T(8,128)(2,1)S(1)} %shard_map.148.dealt_ref), channel_id=1, source_target_pairs={{0,4},{1,5},{2,6},{3,7},{4,0},{5,1},{6,2},{7,3},{8,12},{9,13},{10,... | collective-permute-start | bytes 1572872 | tf_op jit(solution)/shard_map/ppermute | solution.py:523
  6.5 2.6 %collective-permute-start = (bf16[64,2048]{1,0:T(8,128)(2,1)S(1)}, bf16[64,2048]{1,0:T(8,128)(2,1)S(1)}, u32[]{:S(2)}, u32[]{:S(2)}) collective-permute-start(bf16[64,2048]{1,0:T(8,128)(2,1)S(1)} %shard_map.147.refs_0_.own_ref), channel_id=1, source_target_pairs={{0,16},{1,17},{2,18},{3,19},{4,20},{5,21},{6,22},{7,23},{8,24},{9,... | collective-permute-start | bytes 786440 | tf_op jit(solution)/shard_map/ppermute | solution.py:523
  9.1 0.0 copy-done.2
  9.1 0.0 copy-done.3
  9.1 0.7 %copy-done.5 = s32[2048]{0:T(1024)S(1)} copy-done((s32[2048]{0:T(1024)S(1)}, s32[2048]{0:T(1024)}, u32[]{:S(2)}) %copy-start.5) | copy-done | bytes 8216
  9.8 0.7 %copy-done.6 = s32[8]{0:T(128)S(1)} copy-done((s32[8]{0:T(128)S(1)}, s32[8]{0:T(128)}, u32[]{:S(2)}) %copy-start.6) | copy-done | bytes 56
  10.5 0.7 %copy-done.8 = s32[256]{0:T(256)S(1)} copy-done((s32[256]{0:T(256)S(1)}, s32[256]{0:T(256)}, u32[]{:S(2)}) %copy-start.8) | copy-done | bytes 1048
  11.1 0.7 %copy-done.10 = f32[512]{0:T(512)S(1)} copy-done((f32[512]{0:T(512)S(1)}, f32[512]{0:T(512)}, u32[]{:S(2)}) %copy-start.10) | copy-done | bytes 2072
  11.8 0.7 %copy-done.11 = s32[256]{0:T(256)S(1)} copy-done((s32[256]{0:T(256)S(1)}, s32[256]{0:T(256)}, u32[]{:S(2)}) %copy-start.11) | copy-done | bytes 1048
  12.5 0.7 %copy-done.12 = s32[25]{0:T(128)S(1)} copy-done((s32[25]{0:T(128)S(1)}, s32[25]{0:T(128)}, u32[]{:S(2)}) %copy-start.12) | copy-done | bytes 124
  13.2 1.9 %shard_map.149 = (f32[25,512]{1,0:T(8,128)S(1)}, f32[1,64]{1,0:T(1,128)S(1)}, s32[1,400]{1,0:T(1,128)S(1)}, s32[1,240]{1,0:T(1,128)S(1)}) custom-call(s32[8]{0:T(128)S(1)} %copy-done.6, s32[1,25]{1,0:T(1,128)S(1)} %bitcast.18, s32[1,256]{1,0:T(1,128)S(1)} %bitcast.17, s32[1,256]{1,0:T(1,128)S(1)} %bitcast.14, s32[1,2048]{1,0:T(1,128)S(1)} %bitcast.13, ...), custom_call_target="tpu_custom_call" | custom-call | flops 52428800 | bytes 2097152 | tf_op jit(solution)/shard_map/pallas_call | solution.py:547
  15.1 6.4 %collective-permute-done.other_ref = bf16[64,2048]{1,0:T(8,128)(2,1)S(1)} collective-permute-done((bf16[64,2048]{1,0:T(8,128)(2,1)S(1)}, bf16[64,2048]{1,0:T(8,128)(2,1)S(1)}, u32[]{:S(2)}, u32[]{:S(2)}) %collective-permute-start) | collective-permute-done | bytes 262176 | tf_op jit(solution)/shard_map/ppermute | solution.py:523
  21.5 0.0 collective-permute-done.1.own_ref.across_ref
  21.5 0.0 collective-permute-done.2.far_ref
  21.5 0.6 shard_map.150.own_ref
  22.1 0.7 %collective-permute-start.6 = (bf16[80,2048]{1,0:T(8,128)(2,1)S(1)}, bf16[80,2048]{1,0:T(8,128)(2,1)S(1)}, u32[]{:S(2)}, u32[]{:S(2)}) collective-permute-start(bf16[80,2048]{1,0:T(8,128)(2,1)S(1)} %shard_map.150.own_ref), channel_id=1, source_target_pairs={{0,8},{1,9},{2,10},{3,11},{4,12},{5,13},{6,14},{7,15},{8,0},{9,1},... | collective-permute-start | bytes 983048 | tf_op jit(solution)/shard_map/ppermute | solution.py:523
  22.8 1.5 %collective-permute-start.5 = (bf16[64,2048]{1,0:T(8,128)(2,1)S(1)}, bf16[64,2048]{1,0:T(8,128)(2,1)S(1)}, u32[]{:S(2)}, u32[]{:S(2)}) collective-permute-start(bf16[64,2048]{1,0:T(8,128)(2,1)S(1)} %collective-permute-done.other_ref), channel_id=1, source_target_pairs={{0,6},{1,7},{2,4},{3,5},{4,2},{5,3},{6,0},{7,1},{8,14},{9,15},{10,... | collective-permute-start | bytes 786440 | tf_op jit(solution)/shard_map/ppermute | solution.py:523
  24.3 0.5 collective-permute-start.3
  24.8 1.5 %collective-permute-start.4 = (bf16[64,2048]{1,0:T(8,128)(2,1)S(1)}, bf16[64,2048]{1,0:T(8,128)(2,1)S(1)}, u32[]{:S(2)}, u32[]{:S(2)}) collective-permute-start(bf16[64,2048]{1,0:T(8,128)(2,1)S(1)} %collective-permute-done.other_ref), channel_id=1, source_target_pairs={{0,4},{1,5},{2,6},{3,7},{4,0},{5,1},{6,2},{7,3},{8,12},{9,13},{10,... | collective-permute-start | bytes 786440 | tf_op jit(solution)/shard_map/ppermute | solution.py:523
  26.3 6.7 %collective-permute-done.5.other_ref = bf16[64,2048]{1,0:T(8,128)(2,1)S(1)} collective-permute-done((bf16[64,2048]{1,0:T(8,128)(2,1)S(1)}, bf16[64,2048]{1,0:T(8,128)(2,1)S(1)}, u32[]{:S(2)}, u32[]{:S(2)}) %collective-permute-start.5) | collective-permute-done | bytes 262176 | tf_op jit(solution)/shard_map/ppermute | solution.py:523
  33.0 0.6 shard_map.151.own_xy_ref
  33.6 1.5 %collective-permute-start.9 = (bf16[80,2048]{1,0:T(8,128)(2,1)S(1)}, bf16[80,2048]{1,0:T(8,128)(2,1)S(1)}, u32[]{:S(2)}, u32[]{:S(2)}) collective-permute-start(bf16[80,2048]{1,0:T(8,128)(2,1)S(1)} %shard_map.151.own_xy_ref), channel_id=1, source_target_pairs={{0,8},{1,9},{2,10},{3,11},{4,12},{5,13},{6,14},{7,15},{8,0},{9,1},... | collective-permute-start | bytes 983048 | tf_op jit(solution)/shard_map/ppermute | solution.py:523
  35.0 0.0 collective-permute-done.6.far_own_ref
  35.0 1.5 %collective-permute-start.7 = (bf16[80,2048]{1,0:T(8,128)(2,1)S(1)}, bf16[80,2048]{1,0:T(8,128)(2,1)S(1)}, u32[]{:S(2)}, u32[]{:S(2)}) collective-permute-start(bf16[80,2048]{1,0:T(8,128)(2,1)S(1)} %collective-permute-done.6.far_own_ref), channel_id=1, source_target_pairs={{0,2},{1,3},{2,0},{3,1},{4,6},{5,7},{6,4},{7,5},{8,10},{9,11},{10,... | collective-permute-start | bytes 983048 | tf_op jit(solution)/shard_map/ppermute | solution.py:523
  36.5 0.6 collective-permute-start.8
  37.1 0.3 collective-permute-done.3.other_y_ref
  37.4 1.2 %collective-permute-done.4.other_x_ref = bf16[64,2048]{1,0:T(8,128)(2,1)S(1)} collective-permute-done((bf16[64,2048]{1,0:T(8,128)(2,1)S(1)}, bf16[64,2048]{1,0:T(8,128)(2,1)S(1)}, u32[]{:S(2)}, u32[]{:S(2)}) %collective-permute-start.4) | collective-permute-done | bytes 262176 | tf_op jit(solution)/shard_map/ppermute | solution.py:523
  38.6 0.0 copy-done.1
  38.6 4.9 %shard_map.152.early_ref = f32[8,400]{1,0:T(8,128)S(1)} custom-call(s32[8]{0:T(128)S(1)} %copy-done.6, s32[1,400]{1,0:T(1,128)S(1)} %get-tuple-element.25.targets_ref, bf16[784,2048]{1,0:T(8,128)(2,1)S(1)} %copy-done.1, bf16[784,2048]{1,0:T(8,128)(2,1)S(1)} %collective-permute-done.2.far_ref, bf16[80,2048]{1,0:T(8,128)(2,1)S(1)} %shard_map.150.own_ref, ...), custom_call_target="tpu_custom_call" | custom-call | flops 2569011200 | bytes 8060928 | tf_op jit(solution)/shard_map/pallas_call | solution.py:254
  43.5 0.0 copy-start.7
  43.5 0.0 copy-start.9
  43.5 0.0 copy-start.13
  43.6 0.0 collective-permute-done.9.refs_2_
  43.6 0.8 %collective-permute-done.7.refs_0_ = bf16[80,2048]{1,0:T(8,128)(2,1)S(1)} collective-permute-done((bf16[80,2048]{1,0:T(8,128)(2,1)S(1)}, bf16[80,2048]{1,0:T(8,128)(2,1)S(1)}, u32[]{:S(2)}, u32[]{:S(2)}) %collective-permute-start.7) | collective-permute-done | bytes 327712 | tf_op jit(solution)/shard_map/ppermute | solution.py:523
  44.3 0.1 collective-permute-done.8.refs_1_
  44.4 2.6 %shard_map.153 = f32[32,8,128]{2,1,0:T(8,128)S(1)} custom-call(s32[1,240]{1,0:T(1,128)S(1)} %get-tuple-element.23.targets_ref, bf16[784,2048]{1,0:T(8,128)(2,1)S(1)} %copy-done.1, bf16[784,2048]{1,0:T(8,128)(2,1)S(1)} %collective-permute-done.2.far_ref, f32[8,400]{1,0:T(8,128)S(1)} %shard_map.152.early_ref, f32[1,64]{1,0:T(1,128)S(1)} %get-tuple-element.28.extra_ref, ...), custom_call_target="tpu_custom_call" | custom-call | flops 1541406720 | bytes 7405568 | tf_op jit(solution)/shard_map/pallas_call | solution.py:254
  47.1 12.6 %all_to_all.5 = f32[32,8,128]{2,1,0:T(8,128)S(1)} all-to-all(f32[32,8,128]{2,1,0:T(8,128)S(1)} %shard_map.153), channel_id=1, replica_groups=mesh['grp'=8,'vocab'=4] {'grp','vocab'}, dimensions={0} | all-to-all | bytes 262144 | tf_op jit(solution)/shard_map/all_to_all | solution.py:643
  59.7 0.0 copy-done.7
  59.7 0.0 copy-done.9
  59.7 0.0 copy-done.13
  59.7 1.9 %shard_map.154 = (f32[1,256]{1,0:T(1,128)}, f32[1,256]{1,0:T(1,128)}, f32[1,4]{1,0:T(1,128)}, bf16[25,512]{1,0:T(8,128)(2,1)}) custom-call(s32[8]{0:T(128)S(1)} %copy-done.7, s32[8]{0:T(128)S(1)} %copy-done.13, f32[4,2,2,2,8,128]{5,4,3,2,1,0:T(8,128)S(1)} %bitcast.10, s32[1,256]{1,0:T(1,128)S(1)} %bitcast.15, f32[25,512]{1,0:T(8,128)S(1)} %get-tuple-element.29.turned_ref), custom_call_target="tpu_custom_call" | custom-call | flops 16777216 | bytes 131072 | tf_op jit(solution)/shard_map/pallas_call | solution.py:645
  (9 shorter events, 0.0 us)
Async XLA Ops:
  0.6 20.8 %collective-permute-start.2 = (bf16[784,2048]{1,0:T(8,128)(2,1)}, bf16[784,2048]{1,0:T(8,128)(2,1)S(1)}, u32[]{:S(2)}, u32[]{:S(2)}) collective-permute-start(bf16[784,2048]{1,0:T(8,128)(2,1)} %near_ref.3), channel_id=1, source_target_pairs={{0,1},{1,0},{2,3},{3,2},{4,5},{5,4},{6,7},{7,6},{8,9},{9,8},{10,11... | collective-permute-start | bytes 9633800 | tf_op jit(solution)/shard_map/ppermute | solution.py:523
  1.1 1.2 %copy-start = (bf16[256,2048]{1,0:T(8,128)(2,1)S(1)}, bf16[256,2048]{1,0:T(8,128)(2,1)}, u32[]{:S(2)}) copy-start(bf16[256,2048]{1,0:T(8,128)(2,1)} %hidden_ref.3) | copy-start | bytes 3145732
  2.4 0.7 %copy-start.4 = (f32[2048]{0:T(1024)S(1)}, f32[2048]{0:T(1024)}, u32[]{:S(2)}) copy-start(f32[2048]{0:T(1024)} %param.13) | copy-start | bytes 24580
  3.1 6.0 %copy-start.2 = (bf16[2048,512]{1,0:T(8,128)(2,1)S(1)}, bf16[2048,512]{1,0:T(8,128)(2,1)}, u32[]{:S(2)}) copy-start(bf16[2048,512]{1,0:T(8,128)(2,1)} %weight_hbm.1) | copy-start | bytes 6291460
  3.1 6.0 %copy-start.3 = (bf16[256,2048]{1,0:T(8,128)(2,1)S(1)}, bf16[256,2048]{1,0:T(8,128)(2,1)}, u32[]{:S(2)}) copy-start(bf16[256,2048]{1,0:T(8,128)(2,1)} %input_hbm.1) | copy-start | bytes 3145732
  3.5 35.1 %copy-start.1 = (bf16[784,2048]{1,0:T(8,128)(2,1)S(1)}, bf16[784,2048]{1,0:T(8,128)(2,1)}, u32[]{:S(2)}) copy-start(bf16[784,2048]{1,0:T(8,128)(2,1)} %near_ref.3) | copy-start | bytes 9633796
  3.9 17.5 %collective-permute-start.1 = (bf16[2,64,2048]{2,1,0:T(8,128)(2,1)S(1)}, bf16[2,64,2048]{2,1,0:T(8,128)(2,1)S(1)}, u32[]{:S(2)}, u32[]{:S(2)}) collective-permute-start(bf16[2,64,2048]{2,1,0:T(8,128)(2,1)S(1)} %shard_map.148.dealt_ref), channel_id=1, source_target_pairs={{0,4},{1,5},{2,6},{3,7},{4,0},{5,1},{6,2},{7,3},{8,12},{9,13},{10,... | collective-permute-start | bytes 1572872 | tf_op jit(solution)/shard_map/ppermute | solution.py:523
  6.5 14.9 %collective-permute-start = (bf16[64,2048]{1,0:T(8,128)(2,1)S(1)}, bf16[64,2048]{1,0:T(8,128)(2,1)S(1)}, u32[]{:S(2)}, u32[]{:S(2)}) collective-permute-start(bf16[64,2048]{1,0:T(8,128)(2,1)S(1)} %shard_map.147.refs_0_.own_ref), channel_id=1, source_target_pairs={{0,16},{1,17},{2,18},{3,19},{4,20},{5,21},{6,22},{7,23},{8,24},{9,... | collective-permute-start | bytes 786440 | tf_op jit(solution)/shard_map/ppermute | solution.py:523
  9.1 0.7 %copy-start.5 = (s32[2048]{0:T(1024)S(1)}, s32[2048]{0:T(1024)}, u32[]{:S(2)}) copy-start(s32[2048]{0:T(1024)} %param.15) | copy-start | bytes 24580
  9.8 0.7 %copy-start.6 = (s32[8]{0:T(128)S(1)}, s32[8]{0:T(128)}, u32[]{:S(2)}) copy-start(s32[8]{0:T(128)} %lengths_ref.9) | copy-start | bytes 100
  10.5 0.7 %copy-start.8 = (s32[256]{0:T(256)S(1)}, s32[256]{0:T(256)}, u32[]{:S(2)}) copy-start(s32[256]{0:T(256)} %param.17) | copy-start | bytes 3076
  11.1 0.7 %copy-start.10 = (f32[512]{0:T(512)S(1)}, f32[512]{0:T(512)}, u32[]{:S(2)}) copy-start(f32[512]{0:T(512)} %param.21) | copy-start | bytes 6148
  11.8 0.7 %copy-start.11 = (s32[256]{0:T(256)S(1)}, s32[256]{0:T(256)}, u32[]{:S(2)}) copy-start(s32[256]{0:T(256)} %param.22) | copy-start | bytes 3076
  12.5 0.7 %copy-start.12 = (s32[25]{0:T(128)S(1)}, s32[25]{0:T(128)}, u32[]{:S(2)}) copy-start(s32[25]{0:T(128)} %param.23) | copy-start | bytes 304
  22.1 13.0 %collective-permute-start.6 = (bf16[80,2048]{1,0:T(8,128)(2,1)S(1)}, bf16[80,2048]{1,0:T(8,128)(2,1)S(1)}, u32[]{:S(2)}, u32[]{:S(2)}) collective-permute-start(bf16[80,2048]{1,0:T(8,128)(2,1)S(1)} %shard_map.150.own_ref), channel_id=1, source_target_pairs={{0,8},{1,9},{2,10},{3,11},{4,12},{5,13},{6,14},{7,15},{8,0},{9,1},... | collective-permute-start | bytes 983048 | tf_op jit(solution)/shard_map/ppermute | solution.py:523
  22.8 10.1 %collective-permute-start.5 = (bf16[64,2048]{1,0:T(8,128)(2,1)S(1)}, bf16[64,2048]{1,0:T(8,128)(2,1)S(1)}, u32[]{:S(2)}, u32[]{:S(2)}) collective-permute-start(bf16[64,2048]{1,0:T(8,128)(2,1)S(1)} %collective-permute-done.other_ref), channel_id=1, source_target_pairs={{0,6},{1,7},{2,4},{3,5},{4,2},{5,3},{6,0},{7,1},{8,14},{9,15},{10,... | collective-permute-start | bytes 786440 | tf_op jit(solution)/shard_map/ppermute | solution.py:523
  24.3 13.1 %collective-permute-start.3 = (bf16[64,2048]{1,0:T(8,128)(2,1)S(1)}, bf16[64,2048]{1,0:T(8,128)(2,1)S(1)}, u32[]{:S(2)}, u32[]{:S(2)}) collective-permute-start(bf16[64,2048]{1,0:T(8,128)(2,1)S(1)} %collective-permute-done.other_ref), channel_id=1, source_target_pairs={{0,2},{1,3},{2,0},{3,1},{4,6},{5,7},{6,4},{7,5},{8,10},{9,11},{10,... | collective-permute-start | bytes 786440 | tf_op jit(solution)/shard_map/ppermute | solution.py:523
  24.8 13.8 %collective-permute-start.4 = (bf16[64,2048]{1,0:T(8,128)(2,1)S(1)}, bf16[64,2048]{1,0:T(8,128)(2,1)S(1)}, u32[]{:S(2)}, u32[]{:S(2)}) collective-permute-start(bf16[64,2048]{1,0:T(8,128)(2,1)S(1)} %collective-permute-done.other_ref), channel_id=1, source_target_pairs={{0,4},{1,5},{2,6},{3,7},{4,0},{5,1},{6,2},{7,3},{8,12},{9,13},{10,... | collective-permute-start | bytes 786440 | tf_op jit(solution)/shard_map/ppermute | solution.py:523
  33.6 10.0 %collective-permute-start.9 = (bf16[80,2048]{1,0:T(8,128)(2,1)S(1)}, bf16[80,2048]{1,0:T(8,128)(2,1)S(1)}, u32[]{:S(2)}, u32[]{:S(2)}) collective-permute-start(bf16[80,2048]{1,0:T(8,128)(2,1)S(1)} %shard_map.151.own_xy_ref), channel_id=1, source_target_pairs={{0,8},{1,9},{2,10},{3,11},{4,12},{5,13},{6,14},{7,15},{8,0},{9,1},... | collective-permute-start | bytes 983048 | tf_op jit(solution)/shard_map/ppermute | solution.py:523
  35.0 9.3 %collective-permute-start.7 = (bf16[80,2048]{1,0:T(8,128)(2,1)S(1)}, bf16[80,2048]{1,0:T(8,128)(2,1)S(1)}, u32[]{:S(2)}, u32[]{:S(2)}) collective-permute-start(bf16[80,2048]{1,0:T(8,128)(2,1)S(1)} %collective-permute-done.6.far_own_ref), channel_id=1, source_target_pairs={{0,2},{1,3},{2,0},{3,1},{4,6},{5,7},{6,4},{7,5},{8,10},{9,11},{10,... | collective-permute-start | bytes 983048 | tf_op jit(solution)/shard_map/ppermute | solution.py:523
  36.5 7.9 %collective-permute-start.8 = (bf16[80,2048]{1,0:T(8,128)(2,1)S(1)}, bf16[80,2048]{1,0:T(8,128)(2,1)S(1)}, u32[]{:S(2)}, u32[]{:S(2)}) collective-permute-start(bf16[80,2048]{1,0:T(8,128)(2,1)S(1)} %collective-permute-done.6.far_own_ref), channel_id=1, source_target_pairs={{0,4},{1,5},{2,6},{3,7},{4,0},{5,1},{6,2},{7,3},{8,12},{9,13},{10,... | collective-permute-start | bytes 983048 | tf_op jit(solution)/shard_map/ppermute | solution.py:523
  43.5 16.2 %copy-start.7 = (s32[8]{0:T(128)S(1)}, s32[8]{0:T(128)}, u32[]{:S(2)}) copy-start(s32[8]{0:T(128)} %lengths_ref.9) | copy-start | bytes 100
  43.5 16.2 %copy-start.9 = (s32[256]{0:T(256)S(1)}, s32[256]{0:T(256)}, u32[]{:S(2)}) copy-start(s32[256]{0:T(256)} %param.17) | copy-start | bytes 3076
  43.5 16.1 %copy-start.13 = (s32[8]{0:T(128)S(1)}, s32[8]{0:T(128)}, u32[]{:S(2)}) copy-start(s32[8]{0:T(128)} %continues_ref.1) | copy-start | bytes 100

commit v3 on v2

--- a/solution.py
+++ b/solution.py
@@ -13,6 +13,7 @@
 CORES = 2
 LANES = 128
 BREAKS = 31
+SLOTS = (0, 3, 4, 1, 2, 5, 6, 7)
 
 NORM_EPS = 1e-06
 ROPE_BASE = 500000.0
@@ -61,67 +62,67 @@
     return copies
 
 
-def prep_kernel(sizes, hidden_ref, gain_ref, *refs):
-    *known, out_ref = refs
+def dealt(sizes, hidden_ref, gain_ref, t, rows, turned):
     groups, shards = sizes
-    rows, width = out_ref.shape[-2:]
     group, y, core = place_of(shards)
+    is_first = group < groups // 2
+    count = hidden_ref.shape[0] // shards
     place = lax.broadcasted_iota(jnp.int32, (rows, hidden_ref.shape[0]), 0)
     column = lax.broadcasted_iota(jnp.int32, place.shape, 1)
-    for t, known_ref in enumerate(known):
-        out_ref[t] = known_ref[...]
-    for t in range(len(known), out_ref.shape[0] if known else 1):
-        row = source_row(place, (y ^ t) * CORES + core, group < groups // 2, shards, rows)
-        pick = (column == row).astype(jnp.float32).astype(jnp.bfloat16)
-        dealt = jnp.dot(pick, hidden_ref[...], preferred_element_type=jnp.float32)
-        meansq = jnp.sum(dealt * dealt, axis=-1, keepdims=True) / width
-        dealt = (dealt * lax.rsqrt(meansq + NORM_EPS) * gain_ref[...]).astype(jnp.bfloat16)
-        if known:
-            out_ref[t] = dealt
-        else:
-            out_ref[...] = dealt
-
-
-def pack(out_ref, start, is_first, own, other, length, quarter, shards):
-    rows = own.shape[0]
-    size = 2 * BAL // shards
-    gap = size - rows
-    place = lax.broadcasted_iota(jnp.int32, (rows - gap, own.shape[1]), 0) + gap
-    is_lower = place < front(length, quarter, shards)
-
-    def lay(lower, upper):
-        middle = jnp.where(
-            is_lower, lower[gap:rows, :].astype(jnp.float32), upper[0 : rows - gap, :].astype(jnp.float32)
-        )
-        out_ref[start : start + gap, :] = lower[0:gap, :]
-        out_ref[start + gap : start + rows, :] = middle.astype(jnp.bfloat16)
-        out_ref[start + rows : start + size, :] = upper[rows - gap : rows, :]
-
-    @pl.when(is_first)
-    def _():
-        lay(own, other)
-
-    @pl.when(jnp.logical_not(is_first))
-    def _():
-        lay(other, own)
-
-
-def merge_kernel(sizes, flips, lengths_ref, own_ref, other_ref, out_ref):
+    if turned:
+        gap = 2 * BAL // shards - count
+        back = jnp.where(place < gap, place + (count - gap), place - gap)
+        place = jnp.where(is_first, place, back)
+    row = source_row(place, (y ^ t) * CORES + core, is_first, shards, count)
+    pick = (column == row).astype(jnp.float32).astype(jnp.bfloat16)
+    found = jnp.dot(pick, hidden_ref[...], preferred_element_type=jnp.float32)
+    meansq = jnp.sum(found * found, axis=-1, keepdims=True) / found.shape[1]
+    return (found * lax.rsqrt(meansq + NORM_EPS) * gain_ref[...]).astype(jnp.bfloat16)
+
+
+def prep_kernel(sizes, turned, hidden_ref, gain_ref, out_ref):
+    out_ref[...] = dealt(sizes, hidden_ref, gain_ref, 0, out_ref.shape[0], turned)
+
+
+def ends_kernel(sizes, hidden_ref, gain_ref, here_ref, out_ref):
+    rows = out_ref.shape[1]
+    out_ref[0] = here_ref[0:rows, :]
+    for t in range(1, out_ref.shape[0]):
+        out_ref[t] = dealt(sizes, hidden_ref, gain_ref, t, rows, True)
+
+
+def mix_kernel(sizes, lengths_ref, here_ref, other_ref, out_ref):
     groups, shards = sizes
-    x_flip, y_flip = flips
     half = groups // 2
     group, y, core = place_of(shards)
-    own = own_ref if len(own_ref.shape) == 2 else own_ref.at[y_flip]
-    pack(
-        out_ref,
-        0,
-        group < half,
-        own,
-        other_ref,
-        lengths_ref[lax.rem(group, half) ^ x_flip],
-        (y ^ y_flip) * CORES + core,
-        shards,
-    )
+    rows, width = here_ref.shape
+    gap = 2 * BAL // shards - rows
+    length = front(lengths_ref[lax.rem(group, half)], y * CORES + core, shards)
+    is_lower = lax.broadcasted_iota(jnp.int32, (rows - gap, width), 0) + gap < length
+
+    def lay(lower_ref, upper_ref):
+        lower, upper = (ref[gap:rows, :].astype(jnp.float32) for ref in (lower_ref, upper_ref))
+        out_ref[0 : rows - gap, :] = jnp.where(is_lower, lower, upper).astype(jnp.bfloat16)
+
+    @pl.when(group < half)
+    def _():
+        lay(here_ref, other_ref)
+
+    @pl.when(group >= half)
+    def _():
+        lay(other_ref, here_ref)
+
+    out_ref[rows - gap : rows, :] = other_ref[0:gap, :]
+
+
+def gather_pieces(pieces, tokens_ref):
+    start = 0
+    for end, rest_ref in pieces:
+        gap, rows = end.shape[0], rest_ref.shape[0]
+        tokens_ref[start : start + gap, :] = end[...]
+        tokens_ref[start + gap : start + gap + rows, :] = rest_ref[...]
+        start += gap + rows
+    return tokens_ref[...]
 
 
 def statistics(bases, targets, tokens, heads):
@@ -158,19 +159,28 @@
     )
 
 
-def unpacked(every):
-    places = ((0, 6, 0), (2, 6, LANES // 2), (4, 7, 0))
-    return [
-        jnp.concatenate(
-            [
-                every[:, row : row + 1, :],
-                every[:, row + 1 : row + 2, :],
-                every[:, last : last + 1, start : start + LANES // 2],
-            ],
-            axis=2,
-        )
-        for row, last, start in places
+def merged(every):
+    half = LANES // 2
+    row = lax.broadcasted_iota(jnp.int32, every.shape[1:], 0)
+    top = jnp.max(every, axis=0)
+    scale = jnp.exp(every - top[None])
+    means = [
+        jnp.where(row == 6, pltpu.roll(one, half, 1), pltpu.roll(one, one.shape[0] - 2, 0))
+        for one in (every[i] for i in range(every.shape[0]))
     ]
+    expsum = jnp.sum(scale, axis=0)
+    moment = sum(scale[i] * mean for i, mean in enumerate(means))
+    picked = jnp.sum(every, axis=0)
+    lse = top + jnp.log(expsum)
+    entropy = lse - moment / expsum
+
+    def lay(block, first, last):
+        return jnp.concatenate([block[first : first + 1], block[first + 1 : first + 2], last], axis=1)
+
+    lse_row = lay(lse, 0, lse[6:7, :half])
+    return jnp.concatenate(
+        [lay(picked, 4, picked[7:8, :half]) - lse_row, lay(entropy, 0, entropy[6:7, :half])], axis=0
+    )
 
 
 def bases_of(sizes, head_ref):
@@ -191,56 +201,45 @@
     rows_of(state, out_ref)
 
 
-def early_kernel(
-    sizes,
-    lengths_ref,
-    targets_ref,
-    near_ref,
-    far_ref,
-    own_ref,
-    dealt_ref,
-    other_y_ref,
-    across_ref,
-    other_x_ref,
-    own_xy_ref,
-    far_own_ref,
-    out_ref,
-    tokens_ref,
+def piece_kernel(sizes, picks, targets_ref, near_ref, far_ref, *refs):
+    *pieces, out_ref, tokens_ref = refs
+    ends = [ref.at[which] for ref, which in zip(pieces, picks)]
+    tokens = gather_pieces(zip(ends, pieces[len(picks) :]), tokens_ref)
+    state = statistics(bases_of(sizes, near_ref), targets_ref[...], tokens, (near_ref, far_ref))
+    rows_of(state, out_ref)
+
+
+def send_kernel(
+    sizes, targets_ref, near_ref, far_ref, first_ref, second_ref, extra_ref, beyond_ref, corner_ref, *refs
 ):
+    *rests, out_ref, tokens_ref = refs
     groups, shards = sizes
-    half = groups // 2
-    group, y, core = place_of(shards)
-    is_first, column = group < half, lax.rem(group, half)
-    size = own_ref.shape[0]
-    quarter = y * CORES + core
-    tokens_ref[0:size, :] = own_ref[...]
-    lower = lengths_ref[column]
-    pack(tokens_ref, size, is_first, dealt_ref.at[1], other_y_ref, lower, quarter ^ CORES, shards)
-    lower = lengths_ref[column ^ 1]
-    pack(tokens_ref, 2 * size, is_first, across_ref.at[0], other_x_ref, lower, quarter, shards)
-    tokens_ref[3 * size : 4 * size, :] = own_xy_ref[...]
-    tokens_ref[4 * size : 5 * size, :] = far_own_ref[...]
-    state = statistics(
-        bases_of(sizes, near_ref), targets_ref[...], tokens_ref[...], (near_ref, far_ref)
-    )
-    rows_of(state, out_ref)
-
-
-def send_kernel(sizes, targets_ref, near_ref, far_ref, early_ref, extra_ref, *refs):
-    *pieces, out_ref, tokens_ref = refs
-    groups, shards = sizes
-    size = pieces[0].shape[0]
-    for t, piece in enumerate(pieces):
-        tokens_ref[t * size : (t + 1) * size, :] = piece[...]
-    state = statistics(
-        bases_of(sizes, near_ref), targets_ref[...], tokens_ref[...], (near_ref, far_ref)
-    )
-    tokens = early_ref.shape[1] - size
-    early = [early_ref[i : i + 1, :] for i in range(3)]
-    own = packed([row[:, :tokens] for row in early], extra_ref[...])
-    beyond = [jnp.concatenate([row[:, tokens:], late], axis=1) for row, late in zip(early, state)]
-    beyond = packed(beyond, extra_ref[...])
-    mine = lax.div(lax.rem(lax.axis_index("grp"), groups // 2), 2)
+    size = 2 * BAL // shards
+    ends = (beyond_ref.at[1], corner_ref.at[0], corner_ref.at[1])
+    tokens = gather_pieces(zip(ends, rests), tokens_ref)
+    state = statistics(bases_of(sizes, near_ref), targets_ref[...], tokens, (near_ref, far_ref))
+    group, y, _ = place_of(shards)
+    gap = beyond_ref.shape[1]
+
+    def settled(rows):
+        blocks = [rows[:, i * size : (i + 1) * size] for i in range(4)]
+        blocks = [
+            jnp.concatenate([b[:, size - gap :], b[:, gap : size - gap], b[:, :gap]], axis=1) for b in blocks
+        ]
+        rows = jnp.where(group < groups // 2, rows, jnp.concatenate(blocks, axis=1))
+        turned = jnp.concatenate([rows[:, 2 * size :], rows[:, : 2 * size]], axis=1)
+        rows = jnp.where(lax.rem(group, 2) == 1, turned, rows)
+        quarters = [rows[:, i * size : (i + 1) * size] for i in (1, 0, 3, 2)]
+        return jnp.where(y == 1, jnp.concatenate(quarters, axis=1), rows)
+
+    first, second = first_ref[0:4, :], second_ref[0:4, :]
+    third = jnp.concatenate([*state, jnp.zeros_like(state[0])], axis=0)
+    own = settled(jnp.concatenate([first[:, :size], second, first[:, size : 2 * size]], axis=1))
+    beyond = settled(jnp.concatenate([first[:, 2 * size :], third], axis=1))
+    own, beyond = (
+        packed([rows[i : i + 1] for i in range(3)], extra_ref[...]) for rows in (own, beyond)
+    )
+    mine = lax.div(lax.rem(group, groups // 2), 2)
     for which in range(groups // 4):
         block = jnp.where(mine == which, own, beyond)
         for group in range(groups):
@@ -249,17 +248,17 @@
                     out_ref[group * shards + shard] = block
 
 
-def score(kernel, out_shape, targets, heads, extras, count, scratch=True, scalars=()):
+def score(kernel, out_shape, targets, heads, extras, count, scratch=True):
     vocab, width = heads[0].shape
     return call(
         kernel,
         out_shape,
-        [SCALARS] * len(scalars) + [WHOLE] * (3 + len(extras)),
+        [WHOLE] * (3 + len(extras)),
         4 * vocab * count * width,
         4 * vocab * width + 2 * count * width,
         out_specs=WHOLE,
         scratch_shapes=[pltpu.VMEM((count, width), jnp.bfloat16)] if scratch else [],
-    )(*scalars, targets, *heads, *extras)
+    )(targets, *heads, *extras)
 
 
 def upright(row):
@@ -283,8 +282,9 @@
     weight_hbm,
     turned_ref,
     extra_ref,
-    early_ref,
-    late_ref,
+    first_ref,
+    second_ref,
+    third_ref,
     input_ref,
     weight_ref,
     semaphores,
@@ -293,18 +293,22 @@
     copies = fetch((input_hbm, weight_hbm), (input_ref, weight_ref), semaphores)
     cap = segments_ref.shape[1]
     if swapped:
-        tokens = (early_ref.shape[1] + late_ref.shape[1]) // 2
+        tokens = first_ref.shape[1] + second_ref.shape[1] // 2
         half, size = groups // 2, 2 * BAL // shards
         group, y, core = place_of(shards)
         lane = lax.broadcasted_iota(jnp.int32, (1, 2 * tokens), 1)
         row = jnp.zeros((1, 2 * tokens), jnp.int32)
         source = jnp.zeros((1, 2 * tokens), jnp.int32)
-        for slot in range(8):
-            place = lane - slot * size
+        for start, slot in enumerate(SLOTS):
+            place = lane - start * size
+            here = (place >= 0) & (place < size)
+            gap = size - cap // shards
+            back = jnp.where(place < gap, place + size - gap, place - (size - gap))
+            back = jnp.where((place >= gap) & (place < size - gap), place, back)
+            place = jnp.where(group < half, place, back)
             lower = lax.rem(group, half) ^ (slot // 4 * 2) ^ (slot // 2 % 2)
             quarter = (y ^ (slot % 2)) * CORES + core
             is_lower = place < front(lengths_ref[lower], quarter, shards)
-            here = (place >= 0) & (place < size)
             stands = jnp.where(
                 is_lower, shards * place + quarter, shards * (size - 1 - place) + shards - 1 - quarter
             )
@@ -320,11 +324,13 @@
         found = found[:groups] * 256.0 + found[groups:]
         of_group = lax.broadcasted_iota(jnp.int32, found.shape, 0) == source
         targets = jnp.sum(jnp.where(of_group, found, 0.0), axis=0, keepdims=True).astype(jnp.int32)
-        early_ref[...] = targets[:, : early_ref.shape[1]]
-        late_ref[...] = targets[:, early_ref.shape[1] :]
+        start = 0
+        for ref in (first_ref, second_ref, third_ref):
+            ref[...] = targets[:, start : start + ref.shape[1]]
+            start += ref.shape[1]
     else:
-        early_ref[...] = jnp.zeros_like(early_ref)
-        late_ref[...] = jnp.zeros_like(late_ref)
+        for ref in (first_ref, second_ref, third_ref):
+            ref[...] = jnp.zeros_like(ref)
 
     count, width = turned_ref.shape
     column = lax.broadcasted_iota(jnp.int32, (count, cap), 1)
@@ -357,20 +363,8 @@
         turned_ref[:, start : start + HD] = head * cosine + pltpu.roll(head, half_head, 1) * sine
 
 
-def combine(tops, expsums, moments, pickeds):
-    top = jnp.max(tops, axis=0)
-    scale = jnp.exp(tops - top[None])
-    return (
-        top,
-        jnp.sum(expsums * scale, axis=0),
-        jnp.sum(moments * scale, axis=0),
-        jnp.sum(pickeds, axis=0),
-    )
-
-
 def final_kernel(
     sizes,
-    swapped,
     lengths_ref,
     continues_ref,
     got_ref,
@@ -386,28 +380,7 @@
     cap = segments_ref.shape[1]
     size = 2 * BAL // shards
     tokens = 2 * parts * size
-    columns = []
-    for core in range(CORES):
-        if swapped:
-            whole = []
-            for x in range(2):
-                for y in range(parts):
-                    lse, mean, picked = unpacked(got_ref[:, x, y, core])
-                    merged = combine(lse, jnp.ones_like(lse), mean, picked)
-                    blocks = [(x * parts + y) ^ slot for slot in range(2 * parts)]
-                    rows = jnp.concatenate(merged, axis=0)
-                    rows = [rows[:, b * size : (b + 1) * size] for b in blocks]
-                    whole.append(jnp.concatenate(rows, axis=1))
-            whole = jnp.stack(whole)
-            merged = combine(*(whole[:, i : i + 1, :] for i in range(4)))
-        else:
-            every = got_ref[:, :, :, core]
-            every = every.reshape((groups * parts,) + every.shape[3:])
-            lse, mean, picked = unpacked(every)
-            merged = combine(lse, jnp.ones_like(lse), mean, picked)
-        top, expsum, moment, picked = merged
-        lse = top + jnp.log(expsum)
-        columns.append(jnp.concatenate([picked - lse, lse - moment / expsum], axis=0))
+    columns = [merged(got_ref[:, core]) for core in range(CORES)]
 
     column, span = lax.rem(group, 2), tokens // 2
     halves = [[both[:, :span], both[:, span:]] for both in columns]
@@ -450,7 +423,7 @@
         return logprob, sums, counts
 
     partner = group ^ 1
-    messages = [got_ref[who // 2, who % 2, 0, 0][7:8, LANES // 2 :] for who in (group, partner)]
+    messages = [got_ref[who * parts, 0][7:8, LANES // 2 :] for who in (group, partner)]
     breaks = [
         [message[:, BREAKS + i : BREAKS + i + 1].astype(jnp.int32) for i in range(1, SEGS)]
         for message in messages
@@ -479,7 +452,7 @@
     squares = jnp.zeros((1, count), jnp.float32)
     for part in range(parts):
         for core in range(CORES):
-            squares += got_ref[group // 2, group % 2, part, core][7:8, LANES // 2 : LANES // 2 + count]
+            squares += got_ref[group * parts + part, core][7:8, LANES // 2 : LANES // 2 + count]
     squares = upright(squares)
     scale = jnp.sqrt(squares / (width * shards) + NORM_EPS)
     keys_ref[...] = (turned_ref[...] / scale).astype(jnp.bfloat16)
@@ -522,35 +495,29 @@
     def swap(array, group_flip, shard_flip):
         return lax.ppermute(array, axes, partners(sizes, (group_flip, shard_flip)))
 
-    def merge(own, other, flips):
+    def lay(kernel, shape, *operands, scalars=()):
         return call(
-            functools.partial(merge_kernel, sizes, flips),
-            jax.ShapeDtypeStruct((size, width), jnp.bfloat16),
-            [SCALARS, WHOLE, WHOLE],
-            size * width,
+            kernel,
+            jax.ShapeDtypeStruct(shape, jnp.bfloat16),
+            [SCALARS] * len(scalars) + [WHOLE] * len(operands),
+            size * cap * width,
             4 * size * width,
             out_specs=WHOLE,
-        )(group_lengths, own, other)
-
-    def prep(shape, *known):
-        return call(
-            functools.partial(prep_kernel, sizes),
-            jax.ShapeDtypeStruct(shape, jnp.bfloat16),
-            [WHOLE] * (2 + len(known)),
-            2 * rows * cap * width,
-            4 * cap * width,
-            out_specs=WHOLE,
-        )(final_hidden, norm_gain.reshape(1, width), *known)
-
-    here = prep((rows, width))
+        )(*scalars, *operands)
+
+    gap = size - rows
+    hidden = (final_hidden, norm_gain.reshape(1, width))
+    here = lay(functools.partial(prep_kernel, sizes, swapped), (rows, width), *hidden)
+
     count, key_width = key_rows.shape[0], key_weight.shape[1]
-    turned, extra, early_ids, late_ids = call(
+    turned, extra, *ids = call(
         functools.partial(side_kernel, sizes, swapped),
         (
             jax.ShapeDtypeStruct((count, key_width), jnp.float32),
             jax.ShapeDtypeStruct((1, LANES // 2), jnp.float32),
-            jax.ShapeDtypeStruct((1, tokens + size), jnp.int32),
-            jax.ShapeDtypeStruct((1, tokens - size), jnp.int32),
+            jax.ShapeDtypeStruct((1, 3 * size), jnp.int32),
+            jax.ShapeDtypeStruct((1, 2 * size), jnp.int32),
+            jax.ShapeDtypeStruct((1, 3 * size), jnp.int32),
         ),
         [SCALARS] + [WHOLE] * 5 + [FAR, FAR],
         2 * count * width * key_width,
@@ -571,45 +538,56 @@
         key_weight,
     )
 
+    head_weight, here = lax.optimization_barrier((head_weight, here))
     far_head = swap(head_weight, 0, 1)
     heads = (head_weight, far_head)
     sent_shape = jax.ShapeDtypeStruct((groups * shards, 8, LANES), jnp.float32)
     if swapped:
         other = swap(here, 4, 0)
-        dealt = prep((parts, rows, width), here)
-        across = swap(dealt, 1, 0)
-        other, across, far_head, early_ids, late_ids, extra, turned = lax.optimization_barrier(
-            (other, across, far_head, early_ids, late_ids, extra, turned)
+        ends = lay(functools.partial(ends_kernel, sizes), (parts, gap, width), *hidden, here)
+        across = swap(ends, 1, 0)
+        beyond = swap(ends, 2, 0)
+        corner = swap(ends, 3, 0)
+        other, across, beyond, corner, far_head, ids, extra, turned = lax.optimization_barrier(
+            (other, across, beyond, corner, far_head, ids, extra, turned)
         )
         heads = (head_weight, far_head)
-        own = merge(here, other, (0, 0))
-        other_xy = swap(other, 1, 2)
-        far_own = swap(own, 2, 0)
-        other_x = swap(other, 1, 0)
-        other_y = swap(other, 0, 2)
-        own_xy = merge(across, other_xy, (1, 1))
-        far_x = swap(far_own, 1, 0)
-        far_y = swap(far_own, 0, 2)
-        far_xy = swap(own_xy, 2, 0)
-        early = score(
-            functools.partial(early_kernel, sizes),
-            jax.ShapeDtypeStruct((8, tokens + size), jnp.float32),
-            early_ids,
+        rest = lay(
+            functools.partial(mix_kernel, sizes), (rows, width), here, other, scalars=(group_lengths,)
+        )
+        far_rest = swap(rest, 2, 0)
+        rest_xy = swap(rest, 1, 2)
+        rest_x = swap(rest, 1, 0)
+        rest_y = swap(rest, 0, 2)
+        far_x = swap(far_rest, 1, 0)
+        far_y = swap(far_rest, 0, 2)
+        far_xy = swap(rest_xy, 2, 0)
+        first = score(
+            functools.partial(piece_kernel, sizes, (0, 1, 0)),
+            jax.ShapeDtypeStruct((8, 3 * size), jnp.float32),
+            ids[0],
             heads,
-            (own, dealt, other_y, across, other_x, own_xy, far_own),
-            tokens + size,
-            scalars=(group_lengths,),
+            (ends, across, beyond, rest, rest_xy, far_rest),
+            3 * size,
+        )
+        rest_y, rest_x, first = lax.optimization_barrier((rest_y, rest_x, first))
+        second = score(
+            functools.partial(piece_kernel, sizes, (1, 0)),
+            jax.ShapeDtypeStruct((8, 2 * size), jnp.float32),
+            ids[1],
+            heads,
+            (ends, across, rest_y, rest_x),
+            2 * size,
         )
         sent = score(
             functools.partial(send_kernel, sizes),
             sent_shape,
-            late_ids,
+            ids[2],
             heads,
-            (early, extra, far_y, far_x, far_xy),
-            tokens - size,
+            (first, second, extra, beyond, corner, far_y, far_x, far_xy),
+            3 * size,
         )
     else:
-        gap = size - rows
         taken = front(group_lengths[:half, None], jnp.arange(shards)[None, :], shards)
         ids = token_ids.reshape(groups, rows, shards).transpose(0, 2, 1)
         lower = jnp.pad(ids[:half], ((0, 0), (0, 0), (0, gap)))
@@ -643,7 +621,7 @@
     got = lax.all_to_all(sent, axes, 0, 0, tiled=False)
 
     logprob, entropy, means, keys = call(
-        functools.partial(final_kernel, sizes, swapped),
+        functools.partial(final_kernel, sizes),
         (
             jax.ShapeDtypeStruct((1, cap), jnp.float32),
             jax.ShapeDtypeStruct((1, cap), jnp.float32),
@@ -656,7 +634,7 @@
     )(
         group_lengths,
         continues,
-        got.reshape(half, 2, parts, CORES, 8, LANES),
+        got.reshape(groups * parts, CORES, 8, LANES),
         segment_ids.reshape(1, cap),
         turned,
     )

time: 61.9 us -> 59.4 us (0.960)
  waiting for transfers between devices: 15.4 us -> 9.14 us
  local copies, waits for them, and re-layouts: 6 us -> 8.8 us
  starting transfers between devices: 13.4 us -> 16.1 us
  blocking collectives: 12.6 us -> 11.3 us
    ppermute x10 -> x12, waiting for transfers between devices: 15.4 us -> 9.14 us  [swap(): return lax.ppermute(array, axes, partners(sizes, (group_flip, shard_flip)))]
    unnamed x28, local copies, waits for them, and re-layouts: 6 us -> 8.8 us
    ppermute x10 -> x12, starting transfers between devices: 13.4 us -> 16.1 us  [swap(): return lax.ppermute(array, axes, partners(sizes, (group_flip, shard_flip)))]
    all_to_all x1, blocking collectives: 12.6 us -> 11.3 us  [local(): got = lax.all_to_all(sent, axes, 0, 0, tiled=False)]
  transfers between devices with their start and end apart: 10 -> 12, of which waited for: 6 -> 8; matrix products, arithmetic and copies ran while one was open for 0% -> 0% of each run, Pallas kernels for 13% -> 12%
where the time goes in v3:
time: 59.4 us; the launch traced here: 59 us
  starting transfers between devices  16.1 us (27%)
  Pallas kernels  12.9 us (22%)
  blocking collectives  11.3 us (19%)
  waiting for transfers between devices  9.14 us (15%)
  local copies, waits for them, and re-layouts  8.8 us (15%)
  between operations  0.74 us (1%)
    ppermute x12, starting transfers between devices, swap(): return lax.ppermute(array, axes, partners(sizes, (group_flip, shard_flip)))  16.1 us
    all_to_all x1, blocking collectives, local(): got = lax.all_to_all(sent, axes, 0, 0, tiled=False)  11.3 us
    ppermute x12, waiting for transfers between devices, swap(): return lax.ppermute(array, axes, partners(sizes, (group_flip, shard_flip)))  9.14 us
    unnamed x28, local copies, waits for them, and re-layouts  8.8 us
    pallas_call x3, Pallas kernels, score(): call(kernel, out_shape, [WHOLE] * (3 + len(extras)), 4 * vocab * count *...  7.87 us
    pallas_call x1, Pallas kernels, local(): call(functools.partial(side_kernel, sizes, swapped), (jax.ShapeDtypeStruc...  1.88 us
    pallas_call x1, Pallas kernels, local(): call(functools.partial(final_kernel, sizes), (jax.ShapeDtypeStruct((1, ca...  1.76 us
    pallas_call x3, Pallas kernels, lay(): call(kernel, jax.ShapeDtypeStruct(shape, jnp.bfloat16), [SCALARS] * len(s...  1.38 us
  transfers between devices with their start and end apart: 12, of which 8 were waited for; matrix products, arithmetic and copies ran while one was open for 0% of the time, Pallas kernels for 12%

profile of v3, /device:TPU:0, one launch (start us, length us, event | category | flops | bytes accessed | tf_op | source)
XLA Modules:
  0.0 59.0 jit_solution(13293140980331043751)
XLA Ops:
  0.6 0.0 copy-start.1
  0.6 1.2 %copy-done.1 = bf16[256,2048]{1,0:T(8,128)(2,1)S(1)} copy-done((bf16[256,2048]{1,0:T(8,128)(2,1)S(1)}, bf16[256,2048]{1,0:T(8,128)(2,1)}, u32[]{:S(2)}) %copy-start.1) | copy-done | bytes 1048600
  1.9 0.7 %copy-done.4 = f32[2048]{0:T(1024)S(1)} copy-done((f32[2048]{0:T(1024)S(1)}, f32[2048]{0:T(1024)}, u32[]{:S(2)}) %copy-start.4) | copy-done | bytes 8216
  2.6 0.4 shard_map.147.here_ref
  3.0 0.5 collective-permute-start.4
  3.5 3.7 %collective-permute-start = (bf16[64,2048]{1,0:T(8,128)(2,1)S(1)}, bf16[64,2048]{1,0:T(8,128)(2,1)S(1)}, u32[]{:S(2)}, u32[]{:S(2)}) collective-permute-start(bf16[64,2048]{1,0:T(8,128)(2,1)S(1)} %shard_map.147.here_ref), channel_id=1, source_target_pairs={{0,16},{1,17},{2,18},{3,19},{4,20},{5,21},{6,22},{7,23},{8,24},{9,... | collective-permute-start | bytes 786440 | tf_op jit(solution)/shard_map/ppermute | solution.py:496
  7.2 0.3 shard_map.148.refs_0_
  7.5 1.6 %collective-permute-start.1 = (bf16[2,16,2048]{2,1,0:T(8,128)(2,1)S(1)}, bf16[2,16,2048]{2,1,0:T(8,128)(2,1)S(1)}, u32[]{:S(2)}, u32[]{:S(2)}) collective-permute-start(bf16[2,16,2048]{2,1,0:T(8,128)(2,1)S(1)} %shard_map.148.refs_0_), channel_id=1, source_target_pairs={{0,4},{1,5},{2,6},{3,7},{4,0},{5,1},{6,2},{7,3},{8,12},{9,13},{10,... | collective-permute-start | bytes 393224 | tf_op jit(solution)/shard_map/ppermute | solution.py:496
  9.1 1.6 %collective-permute-start.2 = (bf16[2,16,2048]{2,1,0:T(8,128)(2,1)S(1)}, bf16[2,16,2048]{2,1,0:T(8,128)(2,1)S(1)}, u32[]{:S(2)}, u32[]{:S(2)}) collective-permute-start(bf16[2,16,2048]{2,1,0:T(8,128)(2,1)S(1)} %shard_map.148.refs_0_), channel_id=1, source_target_pairs={{0,8},{1,9},{2,10},{3,11},{4,12},{5,13},{6,14},{7,15},{8,0},{9,1},... | collective-permute-start | bytes 393224 | tf_op jit(solution)/shard_map/ppermute | solution.py:496
  10.7 0.4 collective-permute-start.3
  11.1 1.6 %copy-done.2 = bf16[2048,512]{1,0:T(8,128)(2,1)S(1)} copy-done((bf16[2048,512]{1,0:T(8,128)(2,1)S(1)}, bf16[2048,512]{1,0:T(8,128)(2,1)}, u32[]{:S(2)}) %copy-start.2) | copy-done | bytes 2097176
  12.7 1.2 %copy-done.3 = bf16[256,2048]{1,0:T(8,128)(2,1)S(1)} copy-done((bf16[256,2048]{1,0:T(8,128)(2,1)S(1)}, bf16[256,2048]{1,0:T(8,128)(2,1)}, u32[]{:S(2)}) %copy-start.3) | copy-done | bytes 1048600
  13.9 0.7 %copy-done.5 = s32[2048]{0:T(1024)S(1)} copy-done((s32[2048]{0:T(1024)S(1)}, s32[2048]{0:T(1024)}, u32[]{:S(2)}) %copy-start.5) | copy-done | bytes 8216
  14.6 0.7 %copy-done.6 = s32[8]{0:T(128)S(1)} copy-done((s32[8]{0:T(128)S(1)}, s32[8]{0:T(128)}, u32[]{:S(2)}) %copy-start.6) | copy-done | bytes 56
  15.2 0.7 %copy-done.8 = s32[256]{0:T(256)S(1)} copy-done((s32[256]{0:T(256)S(1)}, s32[256]{0:T(256)}, u32[]{:S(2)}) %copy-start.8) | copy-done | bytes 1048
  15.9 0.7 %copy-done.10 = f32[512]{0:T(512)S(1)} copy-done((f32[512]{0:T(512)S(1)}, f32[512]{0:T(512)}, u32[]{:S(2)}) %copy-start.10) | copy-done | bytes 2072
  16.6 0.7 %copy-done.11 = s32[256]{0:T(256)S(1)} copy-done((s32[256]{0:T(256)S(1)}, s32[256]{0:T(256)}, u32[]{:S(2)}) %copy-start.11) | copy-done | bytes 1048
  17.3 0.7 %copy-done.12 = s32[25]{0:T(128)S(1)} copy-done((s32[25]{0:T(128)S(1)}, s32[25]{0:T(128)}, u32[]{:S(2)}) %copy-start.12) | copy-done | bytes 124
  17.9 1.9 %shard_map.149 = (f32[25,512]{1,0:T(8,128)S(1)}, f32[1,64]{1,0:T(1,128)S(1)}, s32[1,240]{1,0:T(1,128)S(1)}, s32[1,160]{1,0:T(1,128)S(1)}, s32[1,240]{1,0:T(1,128)S(1)}) custom-call(s32[8]{0:T(128)S(1)} %copy-done.6, s32[1,25]{1,0:T(1,128)S(1)} %bitcast.18, s32[1,256]{1,0:T(1,128)S(1)} %bitcast.17, s32[1,256]{1,0:T(1,128)S(1)} %bitcast.14, ...), custom_call_target="tpu_custom_call" | custom-call | flops 52428800 | bytes 2097152 | tf_op jit(solution)/shard_map/pallas_call | solution.py:513
  19.8 0.0 collective-permute-done.1.refs_1_
  19.8 0.1 collective-permute-done.2.refs_2_.beyond_ref
  19.9 1.7 %collective-permute-done.3.corner_ref = bf16[2,16,2048]{2,1,0:T(8,128)(2,1)S(1)} collective-permute-done((bf16[2,16,2048]{2,1,0:T(8,128)(2,1)S(1)}, bf16[2,16,2048]{2,1,0:T(8,128)(2,1)S(1)}, u32[]{:S(2)}, u32[]{:S(2)}) %collective-permute-start.3) | collective-permute-done | bytes 131104 | tf_op jit(solution)/shard_map/ppermute | solution.py:496
  21.6 0.0 collective-permute-done.other_ref
  21.7 0.0 collective-permute-done.4.far_ref
  21.7 0.6 %shard_map.150.refs_3_ = bf16[64,2048]{1,0:T(8,128)(2,1)S(1)} custom-call(s32[8]{0:T(128)S(1)} %copy-done.6, bf16[64,2048]{1,0:T(8,128)(2,1)S(1)} %shard_map.147.here_ref, bf16[64,2048]{1,0:T(8,128)(2,1)S(1)} %collective-permute-done.other_ref), custom_call_target="tpu_custom_call" | custom-call | flops 41943040 | bytes 655360 | tf_op jit(solution)/shard_map/pallas_call | solution.py:499
  22.3 0.8 %collective-permute-start.8 = (bf16[64,2048]{1,0:T(8,128)(2,1)S(1)}, bf16[64,2048]{1,0:T(8,128)(2,1)S(1)}, u32[]{:S(2)}, u32[]{:S(2)}) collective-permute-start(bf16[64,2048]{1,0:T(8,128)(2,1)S(1)} %shard_map.150.refs_3_), channel_id=1, source_target_pairs={{0,8},{1,9},{2,10},{3,11},{4,12},{5,13},{6,14},{7,15},{8,0},{9,1},... | collective-permute-start | bytes 786440 | tf_op jit(solution)/shard_map/ppermute | solution.py:496
  23.1 1.8 %collective-permute-start.7 = (bf16[64,2048]{1,0:T(8,128)(2,1)S(1)}, bf16[64,2048]{1,0:T(8,128)(2,1)S(1)}, u32[]{:S(2)}, u32[]{:S(2)}) collective-permute-start(bf16[64,2048]{1,0:T(8,128)(2,1)S(1)} %shard_map.150.refs_3_), channel_id=1, source_target_pairs={{0,6},{1,7},{2,4},{3,5},{4,2},{5,3},{6,0},{7,1},{8,14},{9,15},{10,... | collective-permute-start | bytes 786440 | tf_op jit(solution)/shard_map/ppermute | solution.py:496
  24.9 0.4 collective-permute-start.5
  25.3 1.3 %collective-permute-start.6 = (bf16[64,2048]{1,0:T(8,128)(2,1)S(1)}, bf16[64,2048]{1,0:T(8,128)(2,1)S(1)}, u32[]{:S(2)}, u32[]{:S(2)}) collective-permute-start(bf16[64,2048]{1,0:T(8,128)(2,1)S(1)} %shard_map.150.refs_3_), channel_id=1, source_target_pairs={{0,4},{1,5},{2,6},{3,7},{4,0},{5,1},{6,2},{7,3},{8,12},{9,13},{10,... | collective-permute-start | bytes 786440 | tf_op jit(solution)/shard_map/ppermute | solution.py:496
  26.6 3.2 %collective-permute-done.8.refs_5_ = bf16[64,2048]{1,0:T(8,128)(2,1)S(1)} collective-permute-done((bf16[64,2048]{1,0:T(8,128)(2,1)S(1)}, bf16[64,2048]{1,0:T(8,128)(2,1)S(1)}, u32[]{:S(2)}, u32[]{:S(2)}) %collective-permute-start.8) | collective-permute-done | bytes 262176 | tf_op jit(solution)/shard_map/ppermute | solution.py:496
  29.8 1.5 %collective-permute-start.9 = (bf16[64,2048]{1,0:T(8,128)(2,1)S(1)}, bf16[64,2048]{1,0:T(8,128)(2,1)S(1)}, u32[]{:S(2)}, u32[]{:S(2)}) collective-permute-start(bf16[64,2048]{1,0:T(8,128)(2,1)S(1)} %collective-permute-done.8.refs_5_), channel_id=1, source_target_pairs={{0,2},{1,3},{2,0},{3,1},{4,6},{5,7},{6,4},{7,5},{8,10},{9,11},{10,... | collective-permute-start | bytes 786440 | tf_op jit(solution)/shard_map/ppermute | solution.py:496
  31.4 1.2 %collective-permute-start.10 = (bf16[64,2048]{1,0:T(8,128)(2,1)S(1)}, bf16[64,2048]{1,0:T(8,128)(2,1)S(1)}, u32[]{:S(2)}, u32[]{:S(2)}) collective-permute-start(bf16[64,2048]{1,0:T(8,128)(2,1)S(1)} %collective-permute-done.8.refs_5_), channel_id=1, source_target_pairs={{0,4},{1,5},{2,6},{3,7},{4,0},{5,1},{6,2},{7,3},{8,12},{9,13},{10,... | collective-permute-start | bytes 786440 | tf_op jit(solution)/shard_map/ppermute | solution.py:496
  32.6 0.7 %collective-permute-done.7.refs_4_ = bf16[64,2048]{1,0:T(8,128)(2,1)S(1)} collective-permute-done((bf16[64,2048]{1,0:T(8,128)(2,1)S(1)}, bf16[64,2048]{1,0:T(8,128)(2,1)S(1)}, u32[]{:S(2)}, u32[]{:S(2)}) %collective-permute-start.7) | collective-permute-done | bytes 262176 | tf_op jit(solution)/shard_map/ppermute | solution.py:496
  33.3 1.3 %collective-permute-start.11 = (bf16[64,2048]{1,0:T(8,128)(2,1)S(1)}, bf16[64,2048]{1,0:T(8,128)(2,1)S(1)}, u32[]{:S(2)}, u32[]{:S(2)}) collective-permute-start(bf16[64,2048]{1,0:T(8,128)(2,1)S(1)} %collective-permute-done.7.refs_4_), channel_id=1, source_target_pairs={{0,8},{1,9},{2,10},{3,11},{4,12},{5,13},{6,14},{7,15},{8,0},{9,1},... | collective-permute-start | bytes 786440 | tf_op jit(solution)/shard_map/ppermute | solution.py:496
  34.6 0.0 copy-done
  34.6 2.5 %shard_map.151.first_ref = f32[8,240]{1,0:T(8,128)S(1)} custom-call(s32[1,240]{1,0:T(1,128)S(1)} %get-tuple-element.38.targets_ref, bf16[784,2048]{1,0:T(8,128)(2,1)S(1)} %copy-done, bf16[784,2048]{1,0:T(8,128)(2,1)S(1)} %collective-permute-done.4.far_ref, bf16[2,16,2048]{2,1,0:T(8,128)(2,1)S(1)} %shard_map.148.refs_0_, ...), custom_call_target="tpu_custom_call" | custom-call | flops 1541406720 | bytes 7405568 | tf_op jit(solution)/shard_map/pallas_call | solution.py:253
  37.1 0.2 collective-permute-done.5.refs_2_
  37.3 1.6 %collective-permute-done.6.refs_3_ = bf16[64,2048]{1,0:T(8,128)(2,1)S(1)} collective-permute-done((bf16[64,2048]{1,0:T(8,128)(2,1)S(1)}, bf16[64,2048]{1,0:T(8,128)(2,1)S(1)}, u32[]{:S(2)}, u32[]{:S(2)}) %collective-permute-start.6) | collective-permute-done | bytes 262176 | tf_op jit(solution)/shard_map/ppermute | solution.py:496
  38.9 2.5 %shard_map.152.second_ref = f32[8,160]{1,0:T(8,128)S(1)} custom-call(s32[1,160]{1,0:T(1,128)S(1)} %get-tuple-element.42.targets_ref, bf16[784,2048]{1,0:T(8,128)(2,1)S(1)} %copy-done, bf16[784,2048]{1,0:T(8,128)(2,1)S(1)} %collective-permute-done.4.far_ref, bf16[2,16,2048]{2,1,0:T(8,128)(2,1)S(1)} %shard_map.148.refs_0_, ...), custom_call_target="tpu_custom_call" | custom-call | flops 1027604480 | bytes 7077888 | tf_op jit(solution)/shard_map/pallas_call | solution.py:253
  41.4 0.0 copy-start.7
  41.4 0.0 copy-start.9
  41.4 0.0 copy-start.13
  41.4 1.4 %collective-permute-done.9.refs_0_ = bf16[64,2048]{1,0:T(8,128)(2,1)S(1)} collective-permute-done((bf16[64,2048]{1,0:T(8,128)(2,1)S(1)}, bf16[64,2048]{1,0:T(8,128)(2,1)S(1)}, u32[]{:S(2)}, u32[]{:S(2)}) %collective-permute-start.9) | collective-permute-done | bytes 262176 | tf_op jit(solution)/shard_map/ppermute | solution.py:496
  42.8 0.1 collective-permute-done.10.refs_1_
  42.9 0.0 collective-permute-done.11.refs_2_
  42.9 2.9 %shard_map.153 = f32[32,8,128]{2,1,0:T(8,128)S(1)} custom-call(s32[1,240]{1,0:T(1,128)S(1)} %get-tuple-element.35.targets_ref, bf16[784,2048]{1,0:T(8,128)(2,1)S(1)} %copy-done, bf16[784,2048]{1,0:T(8,128)(2,1)S(1)} %collective-permute-done.4.far_ref, f32[8,240]{1,0:T(8,128)S(1)} %shard_map.151.first_ref, f32[8,160]{1,0:T(8,128)S(1)} %shard_map.152.second_ref, ...), custom_call_target="tpu_custom_call" | custom-call | flops 1541406720 | bytes 7405568 | tf_op jit(solution)/shard_map/pallas_call | solution.py:253
  45.9 11.3 %all_to_all.5 = f32[32,8,128]{2,1,0:T(8,128)S(1)} all-to-all(f32[32,8,128]{2,1,0:T(8,128)S(1)} %shard_map.153), channel_id=1, replica_groups=mesh['grp'=8,'vocab'=4] {'grp','vocab'}, dimensions={0} | all-to-all | bytes 262144 | tf_op jit(solution)/shard_map/all_to_all | solution.py:621
  57.2 1.8 %shard_map.154 = (f32[1,256]{1,0:T(1,128)}, f32[1,256]{1,0:T(1,128)}, f32[1,4]{1,0:T(1,128)}, bf16[25,512]{1,0:T(8,128)(2,1)}) custom-call(s32[8]{0:T(128)S(1)} %copy-done.7, s32[8]{0:T(128)S(1)} %copy-done.13, f32[16,2,8,128]{3,2,1,0:T(8,128)S(1)} %bitcast.10, s32[1,256]{1,0:T(1,128)S(1)} %bitcast.15, f32[25,512]{1,0:T(8,128)S(1)} %get-tuple-element.47.turned_ref), custom_call_target="tpu_custom_call" | custom-call | flops 16777216 | bytes 131072 | tf_op jit(solution)/shard_map/pallas_call | solution.py:623
  (13 shorter events, 0.0 us)
Async XLA Ops:
  0.6 1.2 %copy-start.1 = (bf16[256,2048]{1,0:T(8,128)(2,1)S(1)}, bf16[256,2048]{1,0:T(8,128)(2,1)}, u32[]{:S(2)}) copy-start(bf16[256,2048]{1,0:T(8,128)(2,1)} %hidden_ref.3) | copy-start | bytes 3145732
  1.9 0.7 %copy-start.4 = (f32[2048]{0:T(1024)S(1)}, f32[2048]{0:T(1024)}, u32[]{:S(2)}) copy-start(f32[2048]{0:T(1024)} %param.13) | copy-start | bytes 24580
  2.6 32.0 %copy-start = (bf16[784,2048]{1,0:T(8,128)(2,1)S(1)}, bf16[784,2048]{1,0:T(8,128)(2,1)}, u32[]{:S(2)}) copy-start(bf16[784,2048]{1,0:T(8,128)(2,1)} %near_ref.2) | copy-start | bytes 9633796
  3.0 18.7 %collective-permute-start.4 = (bf16[784,2048]{1,0:T(8,128)(2,1)}, bf16[784,2048]{1,0:T(8,128)(2,1)S(1)}, u32[]{:S(2)}, u32[]{:S(2)}) collective-permute-start(bf16[784,2048]{1,0:T(8,128)(2,1)} %near_ref.2), channel_id=1, source_target_pairs={{0,1},{1,0},{2,3},{3,2},{4,5},{5,4},{6,7},{7,6},{8,9},{9,8},{10,11... | collective-permute-start | bytes 9633800 | tf_op jit(solution)/shard_map/ppermute | solution.py:496
  3.5 18.2 %collective-permute-start = (bf16[64,2048]{1,0:T(8,128)(2,1)S(1)}, bf16[64,2048]{1,0:T(8,128)(2,1)S(1)}, u32[]{:S(2)}, u32[]{:S(2)}) collective-permute-start(bf16[64,2048]{1,0:T(8,128)(2,1)S(1)} %shard_map.147.here_ref), channel_id=1, source_target_pairs={{0,16},{1,17},{2,18},{3,19},{4,20},{5,21},{6,22},{7,23},{8,24},{9,... | collective-permute-start | bytes 786440 | tf_op jit(solution)/shard_map/ppermute | solution.py:496
  7.5 12.3 %collective-permute-start.1 = (bf16[2,16,2048]{2,1,0:T(8,128)(2,1)S(1)}, bf16[2,16,2048]{2,1,0:T(8,128)(2,1)S(1)}, u32[]{:S(2)}, u32[]{:S(2)}) collective-permute-start(bf16[2,16,2048]{2,1,0:T(8,128)(2,1)S(1)} %shard_map.148.refs_0_), channel_id=1, source_target_pairs={{0,4},{1,5},{2,6},{3,7},{4,0},{5,1},{6,2},{7,3},{8,12},{9,13},{10,... | collective-permute-start | bytes 393224 | tf_op jit(solution)/shard_map/ppermute | solution.py:496
  9.1 10.8 %collective-permute-start.2 = (bf16[2,16,2048]{2,1,0:T(8,128)(2,1)S(1)}, bf16[2,16,2048]{2,1,0:T(8,128)(2,1)S(1)}, u32[]{:S(2)}, u32[]{:S(2)}) collective-permute-start(bf16[2,16,2048]{2,1,0:T(8,128)(2,1)S(1)} %shard_map.148.refs_0_), channel_id=1, source_target_pairs={{0,8},{1,9},{2,10},{3,11},{4,12},{5,13},{6,14},{7,15},{8,0},{9,1},... | collective-permute-start | bytes 393224 | tf_op jit(solution)/shard_map/ppermute | solution.py:496
  10.7 11.0 %collective-permute-start.3 = (bf16[2,16,2048]{2,1,0:T(8,128)(2,1)S(1)}, bf16[2,16,2048]{2,1,0:T(8,128)(2,1)S(1)}, u32[]{:S(2)}, u32[]{:S(2)}) collective-permute-start(bf16[2,16,2048]{2,1,0:T(8,128)(2,1)S(1)} %shard_map.148.refs_0_), channel_id=1, source_target_pairs={{0,12},{1,13},{2,14},{3,15},{4,8},{5,9},{6,10},{7,11},{8,4},{9,5},... | collective-permute-start | bytes 393224 | tf_op jit(solution)/shard_map/ppermute | solution.py:496
  11.1 1.6 %copy-start.2 = (bf16[2048,512]{1,0:T(8,128)(2,1)S(1)}, bf16[2048,512]{1,0:T(8,128)(2,1)}, u32[]{:S(2)}) copy-start(bf16[2048,512]{1,0:T(8,128)(2,1)} %weight_hbm.1) | copy-start | bytes 6291460
  12.7 1.2 %copy-start.3 = (bf16[256,2048]{1,0:T(8,128)(2,1)S(1)}, bf16[256,2048]{1,0:T(8,128)(2,1)}, u32[]{:S(2)}) copy-start(bf16[256,2048]{1,0:T(8,128)(2,1)} %input_hbm.1) | copy-start | bytes 3145732
  13.9 0.7 %copy-start.5 = (s32[2048]{0:T(1024)S(1)}, s32[2048]{0:T(1024)}, u32[]{:S(2)}) copy-start(s32[2048]{0:T(1024)} %param.15) | copy-start | bytes 24580
  14.6 0.7 %copy-start.6 = (s32[8]{0:T(128)S(1)}, s32[8]{0:T(128)}, u32[]{:S(2)}) copy-start(s32[8]{0:T(128)} %lengths_ref.5) | copy-start | bytes 100
  15.2 0.7 %copy-start.8 = (s32[256]{0:T(256)S(1)}, s32[256]{0:T(256)}, u32[]{:S(2)}) copy-start(s32[256]{0:T(256)} %param.17) | copy-start | bytes 3076
  15.9 0.7 %copy-start.10 = (f32[512]{0:T(512)S(1)}, f32[512]{0:T(512)}, u32[]{:S(2)}) copy-start(f32[512]{0:T(512)} %param.21) | copy-start | bytes 6148
  16.6 0.7 %copy-start.11 = (s32[256]{0:T(256)S(1)}, s32[256]{0:T(256)}, u32[]{:S(2)}) copy-start(s32[256]{0:T(256)} %param.22) | copy-start | bytes 3076
  17.3 0.7 %copy-start.12 = (s32[25]{0:T(128)S(1)}, s32[25]{0:T(128)}, u32[]{:S(2)}) copy-start(s32[25]{0:T(128)} %param.23) | copy-start | bytes 304
  22.3 7.6 %collective-permute-start.8 = (bf16[64,2048]{1,0:T(8,128)(2,1)S(1)}, bf16[64,2048]{1,0:T(8,128)(2,1)S(1)}, u32[]{:S(2)}, u32[]{:S(2)}) collective-permute-start(bf16[64,2048]{1,0:T(8,128)(2,1)S(1)} %shard_map.150.refs_3_), channel_id=1, source_target_pairs={{0,8},{1,9},{2,10},{3,11},{4,12},{5,13},{6,14},{7,15},{8,0},{9,1},... | collective-permute-start | bytes 786440 | tf_op jit(solution)/shard_map/ppermute | solution.py:496
  23.1 10.2 %collective-permute-start.7 = (bf16[64,2048]{1,0:T(8,128)(2,1)S(1)}, bf16[64,2048]{1,0:T(8,128)(2,1)S(1)}, u32[]{:S(2)}, u32[]{:S(2)}) collective-permute-start(bf16[64,2048]{1,0:T(8,128)(2,1)S(1)} %shard_map.150.refs_3_), channel_id=1, source_target_pairs={{0,6},{1,7},{2,4},{3,5},{4,2},{5,3},{6,0},{7,1},{8,14},{9,15},{10,... | collective-permute-start | bytes 786440 | tf_op jit(solution)/shard_map/ppermute | solution.py:496
  24.9 12.4 %collective-permute-start.5 = (bf16[64,2048]{1,0:T(8,128)(2,1)S(1)}, bf16[64,2048]{1,0:T(8,128)(2,1)S(1)}, u32[]{:S(2)}, u32[]{:S(2)}) collective-permute-start(bf16[64,2048]{1,0:T(8,128)(2,1)S(1)} %shard_map.150.refs_3_), channel_id=1, source_target_pairs={{0,2},{1,3},{2,0},{3,1},{4,6},{5,7},{6,4},{7,5},{8,10},{9,11},{10,... | collective-permute-start | bytes 786440 | tf_op jit(solution)/shard_map/ppermute | solution.py:496
  25.3 13.6 %collective-permute-start.6 = (bf16[64,2048]{1,0:T(8,128)(2,1)S(1)}, bf16[64,2048]{1,0:T(8,128)(2,1)S(1)}, u32[]{:S(2)}, u32[]{:S(2)}) collective-permute-start(bf16[64,2048]{1,0:T(8,128)(2,1)S(1)} %shard_map.150.refs_3_), channel_id=1, source_target_pairs={{0,4},{1,5},{2,6},{3,7},{4,0},{5,1},{6,2},{7,3},{8,12},{9,13},{10,... | collective-permute-start | bytes 786440 | tf_op jit(solution)/shard_map/ppermute | solution.py:496
  29.8 13.0 %collective-permute-start.9 = (bf16[64,2048]{1,0:T(8,128)(2,1)S(1)}, bf16[64,2048]{1,0:T(8,128)(2,1)S(1)}, u32[]{:S(2)}, u32[]{:S(2)}) collective-permute-start(bf16[64,2048]{1,0:T(8,128)(2,1)S(1)} %collective-permute-done.8.refs_5_), channel_id=1, source_target_pairs={{0,2},{1,3},{2,0},{3,1},{4,6},{5,7},{6,4},{7,5},{8,10},{9,11},{10,... | collective-permute-start | bytes 786440 | tf_op jit(solution)/shard_map/ppermute | solution.py:496
  31.4 11.6 %collective-permute-start.10 = (bf16[64,2048]{1,0:T(8,128)(2,1)S(1)}, bf16[64,2048]{1,0:T(8,128)(2,1)S(1)}, u32[]{:S(2)}, u32[]{:S(2)}) collective-permute-start(bf16[64,2048]{1,0:T(8,128)(2,1)S(1)} %collective-permute-done.8.refs_5_), channel_id=1, source_target_pairs={{0,4},{1,5},{2,6},{3,7},{4,0},{5,1},{6,2},{7,3},{8,12},{9,13},{10,... | collective-permute-start | bytes 786440 | tf_op jit(solution)/shard_map/ppermute | solution.py:496
  33.3 9.6 %collective-permute-start.11 = (bf16[64,2048]{1,0:T(8,128)(2,1)S(1)}, bf16[64,2048]{1,0:T(8,128)(2,1)S(1)}, u32[]{:S(2)}, u32[]{:S(2)}) collective-permute-start(bf16[64,2048]{1,0:T(8,128)(2,1)S(1)} %collective-permute-done.7.refs_4_), channel_id=1, source_target_pairs={{0,8},{1,9},{2,10},{3,11},{4,12},{5,13},{6,14},{7,15},{8,0},{9,1},... | collective-permute-start | bytes 786440 | tf_op jit(solution)/shard_map/ppermute | solution.py:496
  41.4 15.8 %copy-start.7 = (s32[8]{0:T(128)S(1)}, s32[8]{0:T(128)}, u32[]{:S(2)}) copy-start(s32[8]{0:T(128)} %lengths_ref.5) | copy-start | bytes 100
  41.4 15.8 %copy-start.9 = (s32[256]{0:T(256)S(1)}, s32[256]{0:T(256)}, u32[]{:S(2)}) copy-start(s32[256]{0:T(256)} %param.17) | copy-start | bytes 3076
  41.4 15.8 %copy-start.13 = (s32[8]{0:T(128)S(1)}, s32[8]{0:T(128)}, u32[]{:S(2)}) copy-start(s32[8]{0:T(128)} %continues_ref.1) | copy-start | bytes 100

commit v4 on v3

--- a/solution.py
+++ b/solution.py
@@ -368,7 +368,6 @@
     lengths_ref,
     continues_ref,
     got_ref,
-    segments_ref,
     turned_ref,
     logprob_ref,
     entropy_ref,
@@ -377,7 +376,7 @@
 ):
     groups, shards = sizes
     parts, group = shards // CORES, lax.axis_index("grp")
-    cap = segments_ref.shape[1]
+    cap = logprob_ref.shape[1]
     size = 2 * BAL // shards
     tokens = 2 * parts * size
     columns = [merged(got_ref[:, core]) for core in range(CORES)]
@@ -403,50 +402,45 @@
     pick = (stood == home).astype(jnp.float32).astype(jnp.bfloat16)
     found = jnp.dot(terms, pick, preferred_element_type=jnp.float32)
     found = found[0:4] + found[4:8] + found[8:12]
-    labels = lax.broadcasted_iota(jnp.int32, (1, SEGS), 1)
-
-    def summed(who, logprob, breaks):
+    def summed(who, logprob):
+        note = got_ref[who * parts, 0][7:8, LANES // 2 :]
+        breaks = [note[:, BREAKS + i : BREAKS + i + 1].astype(jnp.int32) for i in range(1, SEGS)]
         live = slots < lengths_ref[who]
         logprob = jnp.where(live, logprob, 0.0)
-        sums = jnp.zeros((1, SEGS), jnp.float32)
-        counts = jnp.zeros((1, SEGS), jnp.float32)
+        sums, counts = [], []
         for label in range(SEGS):
             member = live
             if label > 0:
                 member = member & (slots >= breaks[label - 1])
             if label < SEGS - 1:
                 member = member & (slots < breaks[label])
-            one_sum = jnp.sum(jnp.where(member, logprob, 0.0), axis=1, keepdims=True)
-            one_count = jnp.sum(member.astype(jnp.float32), axis=1, keepdims=True)
-            sums = jnp.where(labels == label, one_sum, sums)
-            counts = jnp.where(labels == label, one_count, counts)
-        return logprob, sums, counts
+            sums.append(jnp.sum(jnp.where(member, logprob, 0.0), axis=1, keepdims=True))
+            counts.append(jnp.sum(member.astype(jnp.float32), axis=1, keepdims=True))
+        return logprob, sums, counts, breaks
 
     partner = group ^ 1
-    messages = [got_ref[who * parts, 0][7:8, LANES // 2 :] for who in (group, partner)]
-    breaks = [
-        [message[:, BREAKS + i : BREAKS + i + 1].astype(jnp.int32) for i in range(1, SEGS)]
-        for message in messages
-    ]
-    logprob, sums, counts = summed(group, found[0:1], breaks[0])
-    _, partner_sums, partner_counts = summed(partner, found[2:3], breaks[1])
+    logprob, sums, counts, breaks = summed(group, found[0:1])
+    _, partner_sums, partner_counts, _ = summed(partner, found[2:3])
     entropy = jnp.where(slots < lengths_ref[group], found[1:2], 0.0)
-    segments = segments_ref[...]
     is_even = group % 2 == 0
     joined = jnp.where(is_even, continues_ref[group], continues_ref[partner]) == 1
-    last = slots == lengths_ref[group] - 1
-    my_last = jnp.sum(jnp.where(last, segments, 0), axis=1, keepdims=True)
-    partner_last = jnp.max(jnp.where(partner_counts > 0, labels, 0), axis=1, keepdims=True)
-    wanted = jnp.where(is_even, jnp.zeros_like(partner_last), partner_last)
-    extra_sum = jnp.sum(jnp.where(labels == wanted, partner_sums, 0.0), axis=1, keepdims=True)
-    extra_count = jnp.sum(jnp.where(labels == wanted, partner_counts, 0.0), axis=1, keepdims=True)
+    my_last = sum((lengths_ref[group] - 1 >= begin).astype(jnp.int32) for begin in breaks)
     target = jnp.where(is_even, my_last, jnp.zeros_like(my_last))
-    update = joined & (labels == target)
-    total_sum = sums + jnp.where(update, extra_sum, 0.0)
-    total_count = counts + jnp.where(update, extra_count, 0.0)
+    extra_sum, extra_count = partner_sums[0], partner_counts[0]
+    for label in range(1, SEGS):
+        later = jnp.logical_not(is_even) & (partner_counts[label] > 0)
+        extra_sum = jnp.where(later, partner_sums[label], extra_sum)
+        extra_count = jnp.where(later, partner_counts[label], extra_count)
+    labels = lax.broadcasted_iota(jnp.int32, (1, SEGS), 1)
+    means = jnp.zeros((1, SEGS), jnp.float32)
+    for label in range(SEGS):
+        update = joined & (target == label)
+        total_sum = sums[label] + jnp.where(update, extra_sum, 0.0)
+        total_count = counts[label] + jnp.where(update, extra_count, 0.0)
+        means = jnp.where(labels == label, total_sum / jnp.maximum(total_count, 1.0), means)
     logprob_ref[...] = logprob
     entropy_ref[...] = entropy
-    mean_ref[...] = total_sum / jnp.maximum(total_count, 1.0)
+    mean_ref[...] = means
 
     count, width = turned_ref.shape
     squares = jnp.zeros((1, count), jnp.float32)
@@ -628,14 +622,13 @@
             jax.ShapeDtypeStruct((1, SEGS), jnp.float32),
             jax.ShapeDtypeStruct((count, key_width), jnp.bfloat16),
         ),
-        [SCALARS] * 2 + [WHOLE] * 3,
+        [SCALARS] * 2 + [WHOLE] * 2,
         1 << 24,
         4 * groups * shards * 8 * LANES,
     )(
         group_lengths,
         continues,
         got.reshape(groups * parts, CORES, 8, LANES),
-        segment_ids.reshape(1, cap),
         turned,
     )
     return logprob.reshape(cap), entropy.reshape(cap), means.reshape(SEGS), keys

time: 59.4 us -> 59.2 us (level)
    unnamed x28 -> x26, local copies, waits for them, and re-layouts: 8.8 us -> 8.79 us
where the time goes in v4:
time: 59.2 us; the launch traced here: 58.8 us
  starting transfers between devices  16.1 us (27%)
  Pallas kernels  12.8 us (22%)
  blocking collectives  11.3 us (19%)
  waiting for transfers between devices  9.15 us (15%)
  local copies, waits for them, and re-layouts  8.79 us (15%)
  between operations  0.73 us (1%)
    ppermute x12, starting transfers between devices, swap(): return lax.ppermute(array, axes, partners(sizes, (group_flip, shard_flip)))  16.1 us
    all_to_all x1, blocking collectives, local(): got = lax.all_to_all(sent, axes, 0, 0, tiled=False)  11.3 us
    ppermute x12, waiting for transfers between devices, swap(): return lax.ppermute(array, axes, partners(sizes, (group_flip, shard_flip)))  9.15 us
    unnamed x26, local copies, waits for them, and re-layouts  8.79 us
    pallas_call x3, Pallas kernels, score(): call(kernel, out_shape, [WHOLE] * (3 + len(extras)), 4 * vocab * count *...  7.87 us
    pallas_call x1, Pallas kernels, local(): call(functools.partial(side_kernel, sizes, swapped), (jax.ShapeDtypeStruc...  1.88 us
    pallas_call x1, Pallas kernels, local(): call(functools.partial(final_kernel, sizes), (jax.ShapeDtypeStruct((1, ca...  1.64 us
    pallas_call x3, Pallas kernels, lay(): call(kernel, jax.ShapeDtypeStruct(shape, jnp.bfloat16), [SCALARS] * len(s...  1.38 us
  transfers between devices with their start and end apart: 12, of which 8 were waited for; matrix products, arithmetic and copies ran while one was open for 0% of the time, Pallas kernels for 12%

profile of v4, /device:TPU:0, one launch (start us, length us, event | category | flops | bytes accessed | tf_op | source)
XLA Modules:
  0.0 58.8 jit_solution(11086367445578098165)
XLA Ops:
  0.6 0.0 copy-start.1
  0.6 1.2 %copy-done.1 = bf16[256,2048]{1,0:T(8,128)(2,1)S(1)} copy-done((bf16[256,2048]{1,0:T(8,128)(2,1)S(1)}, bf16[256,2048]{1,0:T(8,128)(2,1)}, u32[]{:S(2)}) %copy-start.1) | copy-done | bytes 1048600
  1.9 0.7 %copy-done.4 = f32[2048]{0:T(1024)S(1)} copy-done((f32[2048]{0:T(1024)S(1)}, f32[2048]{0:T(1024)}, u32[]{:S(2)}) %copy-start.4) | copy-done | bytes 8216
  2.6 0.4 shard_map.147.here_ref
  3.0 0.5 collective-permute-start.4
  3.5 3.7 %collective-permute-start = (bf16[64,2048]{1,0:T(8,128)(2,1)S(1)}, bf16[64,2048]{1,0:T(8,128)(2,1)S(1)}, u32[]{:S(2)}, u32[]{:S(2)}) collective-permute-start(bf16[64,2048]{1,0:T(8,128)(2,1)S(1)} %shard_map.147.here_ref), channel_id=1, source_target_pairs={{0,16},{1,17},{2,18},{3,19},{4,20},{5,21},{6,22},{7,23},{8,24},{9,... | collective-permute-start | bytes 786440 | tf_op jit(solution)/shard_map/ppermute | solution.py:490
  7.2 0.3 shard_map.148.refs_0_
  7.5 1.6 %collective-permute-start.1 = (bf16[2,16,2048]{2,1,0:T(8,128)(2,1)S(1)}, bf16[2,16,2048]{2,1,0:T(8,128)(2,1)S(1)}, u32[]{:S(2)}, u32[]{:S(2)}) collective-permute-start(bf16[2,16,2048]{2,1,0:T(8,128)(2,1)S(1)} %shard_map.148.refs_0_), channel_id=1, source_target_pairs={{0,4},{1,5},{2,6},{3,7},{4,0},{5,1},{6,2},{7,3},{8,12},{9,13},{10,... | collective-permute-start | bytes 393224 | tf_op jit(solution)/shard_map/ppermute | solution.py:490
  9.1 1.6 %collective-permute-start.2 = (bf16[2,16,2048]{2,1,0:T(8,128)(2,1)S(1)}, bf16[2,16,2048]{2,1,0:T(8,128)(2,1)S(1)}, u32[]{:S(2)}, u32[]{:S(2)}) collective-permute-start(bf16[2,16,2048]{2,1,0:T(8,128)(2,1)S(1)} %shard_map.148.refs_0_), channel_id=1, source_target_pairs={{0,8},{1,9},{2,10},{3,11},{4,12},{5,13},{6,14},{7,15},{8,0},{9,1},... | collective-permute-start | bytes 393224 | tf_op jit(solution)/shard_map/ppermute | solution.py:490
  10.7 0.4 collective-permute-start.3
  11.1 1.6 %copy-done.2 = bf16[2048,512]{1,0:T(8,128)(2,1)S(1)} copy-done((bf16[2048,512]{1,0:T(8,128)(2,1)S(1)}, bf16[2048,512]{1,0:T(8,128)(2,1)}, u32[]{:S(2)}) %copy-start.2) | copy-done | bytes 2097176
  12.7 1.2 %copy-done.3 = bf16[256,2048]{1,0:T(8,128)(2,1)S(1)} copy-done((bf16[256,2048]{1,0:T(8,128)(2,1)S(1)}, bf16[256,2048]{1,0:T(8,128)(2,1)}, u32[]{:S(2)}) %copy-start.3) | copy-done | bytes 1048600
  13.9 0.7 %copy-done.5 = s32[2048]{0:T(1024)S(1)} copy-done((s32[2048]{0:T(1024)S(1)}, s32[2048]{0:T(1024)}, u32[]{:S(2)}) %copy-start.5) | copy-done | bytes 8216
  14.6 0.7 %copy-done.6 = s32[8]{0:T(128)S(1)} copy-done((s32[8]{0:T(128)S(1)}, s32[8]{0:T(128)}, u32[]{:S(2)}) %copy-start.6) | copy-done | bytes 56
  15.2 0.7 %copy-done.8 = f32[512]{0:T(512)S(1)} copy-done((f32[512]{0:T(512)S(1)}, f32[512]{0:T(512)}, u32[]{:S(2)}) %copy-start.8) | copy-done | bytes 2072
  15.9 0.7 %copy-done.9 = s32[256]{0:T(256)S(1)} copy-done((s32[256]{0:T(256)S(1)}, s32[256]{0:T(256)}, u32[]{:S(2)}) %copy-start.9) | copy-done | bytes 1048
  16.6 0.7 %copy-done.10 = s32[256]{0:T(256)S(1)} copy-done((s32[256]{0:T(256)S(1)}, s32[256]{0:T(256)}, u32[]{:S(2)}) %copy-start.10) | copy-done | bytes 1048
  17.3 0.7 %copy-done.11 = s32[25]{0:T(128)S(1)} copy-done((s32[25]{0:T(128)S(1)}, s32[25]{0:T(128)}, u32[]{:S(2)}) %copy-start.11) | copy-done | bytes 124
  17.9 1.9 %shard_map.149 = (f32[25,512]{1,0:T(8,128)S(1)}, f32[1,64]{1,0:T(1,128)S(1)}, s32[1,240]{1,0:T(1,128)S(1)}, s32[1,160]{1,0:T(1,128)S(1)}, s32[1,240]{1,0:T(1,128)S(1)}) custom-call(s32[8]{0:T(128)S(1)} %copy-done.6, s32[1,25]{1,0:T(1,128)S(1)} %bitcast.17, s32[1,256]{1,0:T(1,128)S(1)} %bitcast.15, s32[1,256]{1,0:T(1,128)S(1)} %bitcast.16, ...), custom_call_target="tpu_custom_call" | custom-call | flops 52428800 | bytes 2097152 | tf_op jit(solution)/shard_map/pallas_call | solution.py:507
  19.8 0.0 collective-permute-done.1.refs_1_
  19.8 0.1 collective-permute-done.2.refs_2_.beyond_ref
  19.9 1.7 %collective-permute-done.3.corner_ref = bf16[2,16,2048]{2,1,0:T(8,128)(2,1)S(1)} collective-permute-done((bf16[2,16,2048]{2,1,0:T(8,128)(2,1)S(1)}, bf16[2,16,2048]{2,1,0:T(8,128)(2,1)S(1)}, u32[]{:S(2)}, u32[]{:S(2)}) %collective-permute-start.3) | collective-permute-done | bytes 131104 | tf_op jit(solution)/shard_map/ppermute | solution.py:490
  21.6 0.0 collective-permute-done.other_ref
  21.7 0.0 collective-permute-done.4.far_ref
  21.7 0.6 %shard_map.150.refs_3_ = bf16[64,2048]{1,0:T(8,128)(2,1)S(1)} custom-call(s32[8]{0:T(128)S(1)} %copy-done.6, bf16[64,2048]{1,0:T(8,128)(2,1)S(1)} %shard_map.147.here_ref, bf16[64,2048]{1,0:T(8,128)(2,1)S(1)} %collective-permute-done.other_ref), custom_call_target="tpu_custom_call" | custom-call | flops 41943040 | bytes 655360 | tf_op jit(solution)/shard_map/pallas_call | solution.py:493
  22.3 0.8 %collective-permute-start.8 = (bf16[64,2048]{1,0:T(8,128)(2,1)S(1)}, bf16[64,2048]{1,0:T(8,128)(2,1)S(1)}, u32[]{:S(2)}, u32[]{:S(2)}) collective-permute-start(bf16[64,2048]{1,0:T(8,128)(2,1)S(1)} %shard_map.150.refs_3_), channel_id=1, source_target_pairs={{0,8},{1,9},{2,10},{3,11},{4,12},{5,13},{6,14},{7,15},{8,0},{9,1},... | collective-permute-start | bytes 786440 | tf_op jit(solution)/shard_map/ppermute | solution.py:490
  23.1 1.8 %collective-permute-start.7 = (bf16[64,2048]{1,0:T(8,128)(2,1)S(1)}, bf16[64,2048]{1,0:T(8,128)(2,1)S(1)}, u32[]{:S(2)}, u32[]{:S(2)}) collective-permute-start(bf16[64,2048]{1,0:T(8,128)(2,1)S(1)} %shard_map.150.refs_3_), channel_id=1, source_target_pairs={{0,6},{1,7},{2,4},{3,5},{4,2},{5,3},{6,0},{7,1},{8,14},{9,15},{10,... | collective-permute-start | bytes 786440 | tf_op jit(solution)/shard_map/ppermute | solution.py:490
  24.9 0.4 collective-permute-start.5
  25.3 1.3 %collective-permute-start.6 = (bf16[64,2048]{1,0:T(8,128)(2,1)S(1)}, bf16[64,2048]{1,0:T(8,128)(2,1)S(1)}, u32[]{:S(2)}, u32[]{:S(2)}) collective-permute-start(bf16[64,2048]{1,0:T(8,128)(2,1)S(1)} %shard_map.150.refs_3_), channel_id=1, source_target_pairs={{0,4},{1,5},{2,6},{3,7},{4,0},{5,1},{6,2},{7,3},{8,12},{9,13},{10,... | collective-permute-start | bytes 786440 | tf_op jit(solution)/shard_map/ppermute | solution.py:490
  26.6 3.2 %collective-permute-done.8.refs_5_ = bf16[64,2048]{1,0:T(8,128)(2,1)S(1)} collective-permute-done((bf16[64,2048]{1,0:T(8,128)(2,1)S(1)}, bf16[64,2048]{1,0:T(8,128)(2,1)S(1)}, u32[]{:S(2)}, u32[]{:S(2)}) %collective-permute-start.8) | collective-permute-done | bytes 262176 | tf_op jit(solution)/shard_map/ppermute | solution.py:490
  29.8 1.5 %collective-permute-start.9 = (bf16[64,2048]{1,0:T(8,128)(2,1)S(1)}, bf16[64,2048]{1,0:T(8,128)(2,1)S(1)}, u32[]{:S(2)}, u32[]{:S(2)}) collective-permute-start(bf16[64,2048]{1,0:T(8,128)(2,1)S(1)} %collective-permute-done.8.refs_5_), channel_id=1, source_target_pairs={{0,2},{1,3},{2,0},{3,1},{4,6},{5,7},{6,4},{7,5},{8,10},{9,11},{10,... | collective-permute-start | bytes 786440 | tf_op jit(solution)/shard_map/ppermute | solution.py:490
  31.4 1.2 %collective-permute-start.10 = (bf16[64,2048]{1,0:T(8,128)(2,1)S(1)}, bf16[64,2048]{1,0:T(8,128)(2,1)S(1)}, u32[]{:S(2)}, u32[]{:S(2)}) collective-permute-start(bf16[64,2048]{1,0:T(8,128)(2,1)S(1)} %collective-permute-done.8.refs_5_), channel_id=1, source_target_pairs={{0,4},{1,5},{2,6},{3,7},{4,0},{5,1},{6,2},{7,3},{8,12},{9,13},{10,... | collective-permute-start | bytes 786440 | tf_op jit(solution)/shard_map/ppermute | solution.py:490
  32.6 0.7 %collective-permute-done.7.refs_4_ = bf16[64,2048]{1,0:T(8,128)(2,1)S(1)} collective-permute-done((bf16[64,2048]{1,0:T(8,128)(2,1)S(1)}, bf16[64,2048]{1,0:T(8,128)(2,1)S(1)}, u32[]{:S(2)}, u32[]{:S(2)}) %collective-permute-start.7) | collective-permute-done | bytes 262176 | tf_op jit(solution)/shard_map/ppermute | solution.py:490
  33.3 1.3 %collective-permute-start.11 = (bf16[64,2048]{1,0:T(8,128)(2,1)S(1)}, bf16[64,2048]{1,0:T(8,128)(2,1)S(1)}, u32[]{:S(2)}, u32[]{:S(2)}) collective-permute-start(bf16[64,2048]{1,0:T(8,128)(2,1)S(1)} %collective-permute-done.7.refs_4_), channel_id=1, source_target_pairs={{0,8},{1,9},{2,10},{3,11},{4,12},{5,13},{6,14},{7,15},{8,0},{9,1},... | collective-permute-start | bytes 786440 | tf_op jit(solution)/shard_map/ppermute | solution.py:490
  34.6 0.0 copy-done
  34.6 2.5 %shard_map.151.first_ref = f32[8,240]{1,0:T(8,128)S(1)} custom-call(s32[1,240]{1,0:T(1,128)S(1)} %get-tuple-element.38.targets_ref, bf16[784,2048]{1,0:T(8,128)(2,1)S(1)} %copy-done, bf16[784,2048]{1,0:T(8,128)(2,1)S(1)} %collective-permute-done.4.far_ref, bf16[2,16,2048]{2,1,0:T(8,128)(2,1)S(1)} %shard_map.148.refs_0_, ...), custom_call_target="tpu_custom_call" | custom-call | flops 1541406720 | bytes 7405568 | tf_op jit(solution)/shard_map/pallas_call | solution.py:253
  37.1 0.2 collective-permute-done.5.refs_2_
  37.3 1.6 %collective-permute-done.6.refs_3_ = bf16[64,2048]{1,0:T(8,128)(2,1)S(1)} collective-permute-done((bf16[64,2048]{1,0:T(8,128)(2,1)S(1)}, bf16[64,2048]{1,0:T(8,128)(2,1)S(1)}, u32[]{:S(2)}, u32[]{:S(2)}) %collective-permute-start.6) | collective-permute-done | bytes 262176 | tf_op jit(solution)/shard_map/ppermute | solution.py:490
  38.9 2.5 %shard_map.152.second_ref = f32[8,160]{1,0:T(8,128)S(1)} custom-call(s32[1,160]{1,0:T(1,128)S(1)} %get-tuple-element.42.targets_ref, bf16[784,2048]{1,0:T(8,128)(2,1)S(1)} %copy-done, bf16[784,2048]{1,0:T(8,128)(2,1)S(1)} %collective-permute-done.4.far_ref, bf16[2,16,2048]{2,1,0:T(8,128)(2,1)S(1)} %shard_map.148.refs_0_, ...), custom_call_target="tpu_custom_call" | custom-call | flops 1027604480 | bytes 7077888 | tf_op jit(solution)/shard_map/pallas_call | solution.py:253
  41.4 0.0 copy-start.7
  41.4 0.0 copy-start.12
  41.4 1.4 %collective-permute-done.9.refs_0_ = bf16[64,2048]{1,0:T(8,128)(2,1)S(1)} collective-permute-done((bf16[64,2048]{1,0:T(8,128)(2,1)S(1)}, bf16[64,2048]{1,0:T(8,128)(2,1)S(1)}, u32[]{:S(2)}, u32[]{:S(2)}) %collective-permute-start.9) | collective-permute-done | bytes 262176 | tf_op jit(solution)/shard_map/ppermute | solution.py:490
  42.8 0.1 collective-permute-done.10.refs_1_
  42.9 0.0 collective-permute-done.11.refs_2_
  42.9 2.9 %shard_map.153 = f32[32,8,128]{2,1,0:T(8,128)S(1)} custom-call(s32[1,240]{1,0:T(1,128)S(1)} %get-tuple-element.35.targets_ref, bf16[784,2048]{1,0:T(8,128)(2,1)S(1)} %copy-done, bf16[784,2048]{1,0:T(8,128)(2,1)S(1)} %collective-permute-done.4.far_ref, f32[8,240]{1,0:T(8,128)S(1)} %shard_map.151.first_ref, f32[8,160]{1,0:T(8,128)S(1)} %shard_map.152.second_ref, ...), custom_call_target="tpu_custom_call" | custom-call | flops 1541406720 | bytes 7405568 | tf_op jit(solution)/shard_map/pallas_call | solution.py:253
  45.9 11.3 %all_to_all.5 = f32[32,8,128]{2,1,0:T(8,128)S(1)} all-to-all(f32[32,8,128]{2,1,0:T(8,128)S(1)} %shard_map.153), channel_id=1, replica_groups=mesh['grp'=8,'vocab'=4] {'grp','vocab'}, dimensions={0} | all-to-all | bytes 262144 | tf_op jit(solution)/shard_map/all_to_all | solution.py:615
  57.2 0.0 copy-done.7
  57.2 1.6 %shard_map.154 = (f32[1,256]{1,0:T(1,128)}, f32[1,256]{1,0:T(1,128)}, f32[1,4]{1,0:T(1,128)}, bf16[25,512]{1,0:T(8,128)(2,1)}) custom-call(s32[8]{0:T(128)S(1)} %copy-done.7, s32[8]{0:T(128)S(1)} %copy-done.12, f32[16,2,8,128]{3,2,1,0:T(8,128)S(1)} %bitcast.10, f32[25,512]{1,0:T(8,128)S(1)} %get-tuple-element.47.turned_ref), custom_call_target="tpu_custom_call" | custom-call | flops 16777216 | bytes 131072 | tf_op jit(solution)/shard_map/pallas_call | solution.py:617
  (11 shorter events, 0.0 us)
Async XLA Ops:
  0.6 1.2 %copy-start.1 = (bf16[256,2048]{1,0:T(8,128)(2,1)S(1)}, bf16[256,2048]{1,0:T(8,128)(2,1)}, u32[]{:S(2)}) copy-start(bf16[256,2048]{1,0:T(8,128)(2,1)} %hidden_ref.3) | copy-start | bytes 3145732
  1.9 0.7 %copy-start.4 = (f32[2048]{0:T(1024)S(1)}, f32[2048]{0:T(1024)}, u32[]{:S(2)}) copy-start(f32[2048]{0:T(1024)} %param.13) | copy-start | bytes 24580
  2.6 32.0 %copy-start = (bf16[784,2048]{1,0:T(8,128)(2,1)S(1)}, bf16[784,2048]{1,0:T(8,128)(2,1)}, u32[]{:S(2)}) copy-start(bf16[784,2048]{1,0:T(8,128)(2,1)} %near_ref.2) | copy-start | bytes 9633796
  3.0 18.7 %collective-permute-start.4 = (bf16[784,2048]{1,0:T(8,128)(2,1)}, bf16[784,2048]{1,0:T(8,128)(2,1)S(1)}, u32[]{:S(2)}, u32[]{:S(2)}) collective-permute-start(bf16[784,2048]{1,0:T(8,128)(2,1)} %near_ref.2), channel_id=1, source_target_pairs={{0,1},{1,0},{2,3},{3,2},{4,5},{5,4},{6,7},{7,6},{8,9},{9,8},{10,11... | collective-permute-start | bytes 9633800 | tf_op jit(solution)/shard_map/ppermute | solution.py:490
  3.5 18.2 %collective-permute-start = (bf16[64,2048]{1,0:T(8,128)(2,1)S(1)}, bf16[64,2048]{1,0:T(8,128)(2,1)S(1)}, u32[]{:S(2)}, u32[]{:S(2)}) collective-permute-start(bf16[64,2048]{1,0:T(8,128)(2,1)S(1)} %shard_map.147.here_ref), channel_id=1, source_target_pairs={{0,16},{1,17},{2,18},{3,19},{4,20},{5,21},{6,22},{7,23},{8,24},{9,... | collective-permute-start | bytes 786440 | tf_op jit(solution)/shard_map/ppermute | solution.py:490
  7.5 12.3 %collective-permute-start.1 = (bf16[2,16,2048]{2,1,0:T(8,128)(2,1)S(1)}, bf16[2,16,2048]{2,1,0:T(8,128)(2,1)S(1)}, u32[]{:S(2)}, u32[]{:S(2)}) collective-permute-start(bf16[2,16,2048]{2,1,0:T(8,128)(2,1)S(1)} %shard_map.148.refs_0_), channel_id=1, source_target_pairs={{0,4},{1,5},{2,6},{3,7},{4,0},{5,1},{6,2},{7,3},{8,12},{9,13},{10,... | collective-permute-start | bytes 393224 | tf_op jit(solution)/shard_map/ppermute | solution.py:490
  9.1 10.8 %collective-permute-start.2 = (bf16[2,16,2048]{2,1,0:T(8,128)(2,1)S(1)}, bf16[2,16,2048]{2,1,0:T(8,128)(2,1)S(1)}, u32[]{:S(2)}, u32[]{:S(2)}) collective-permute-start(bf16[2,16,2048]{2,1,0:T(8,128)(2,1)S(1)} %shard_map.148.refs_0_), channel_id=1, source_target_pairs={{0,8},{1,9},{2,10},{3,11},{4,12},{5,13},{6,14},{7,15},{8,0},{9,1},... | collective-permute-start | bytes 393224 | tf_op jit(solution)/shard_map/ppermute | solution.py:490
  10.7 11.0 %collective-permute-start.3 = (bf16[2,16,2048]{2,1,0:T(8,128)(2,1)S(1)}, bf16[2,16,2048]{2,1,0:T(8,128)(2,1)S(1)}, u32[]{:S(2)}, u32[]{:S(2)}) collective-permute-start(bf16[2,16,2048]{2,1,0:T(8,128)(2,1)S(1)} %shard_map.148.refs_0_), channel_id=1, source_target_pairs={{0,12},{1,13},{2,14},{3,15},{4,8},{5,9},{6,10},{7,11},{8,4},{9,5},... | collective-permute-start | bytes 393224 | tf_op jit(solution)/shard_map/ppermute | solution.py:490
  11.1 1.6 %copy-start.2 = (bf16[2048,512]{1,0:T(8,128)(2,1)S(1)}, bf16[2048,512]{1,0:T(8,128)(2,1)}, u32[]{:S(2)}) copy-start(bf16[2048,512]{1,0:T(8,128)(2,1)} %weight_hbm.1) | copy-start | bytes 6291460
  12.7 1.2 %copy-start.3 = (bf16[256,2048]{1,0:T(8,128)(2,1)S(1)}, bf16[256,2048]{1,0:T(8,128)(2,1)}, u32[]{:S(2)}) copy-start(bf16[256,2048]{1,0:T(8,128)(2,1)} %input_hbm.1) | copy-start | bytes 3145732
  13.9 0.7 %copy-start.5 = (s32[2048]{0:T(1024)S(1)}, s32[2048]{0:T(1024)}, u32[]{:S(2)}) copy-start(s32[2048]{0:T(1024)} %param.15) | copy-start | bytes 24580
  14.6 0.7 %copy-start.6 = (s32[8]{0:T(128)S(1)}, s32[8]{0:T(128)}, u32[]{:S(2)}) copy-start(s32[8]{0:T(128)} %lengths_ref.5) | copy-start | bytes 100
  15.2 0.7 %copy-start.8 = (f32[512]{0:T(512)S(1)}, f32[512]{0:T(512)}, u32[]{:S(2)}) copy-start(f32[512]{0:T(512)} %param.21) | copy-start | bytes 6148
  15.9 0.7 %copy-start.9 = (s32[256]{0:T(256)S(1)}, s32[256]{0:T(256)}, u32[]{:S(2)}) copy-start(s32[256]{0:T(256)} %param.22) | copy-start | bytes 3076
  16.6 0.7 %copy-start.10 = (s32[256]{0:T(256)S(1)}, s32[256]{0:T(256)}, u32[]{:S(2)}) copy-start(s32[256]{0:T(256)} %param.17) | copy-start | bytes 3076
  17.3 0.7 %copy-start.11 = (s32[25]{0:T(128)S(1)}, s32[25]{0:T(128)}, u32[]{:S(2)}) copy-start(s32[25]{0:T(128)} %param.23) | copy-start | bytes 304
  22.3 7.6 %collective-permute-start.8 = (bf16[64,2048]{1,0:T(8,128)(2,1)S(1)}, bf16[64,2048]{1,0:T(8,128)(2,1)S(1)}, u32[]{:S(2)}, u32[]{:S(2)}) collective-permute-start(bf16[64,2048]{1,0:T(8,128)(2,1)S(1)} %shard_map.150.refs_3_), channel_id=1, source_target_pairs={{0,8},{1,9},{2,10},{3,11},{4,12},{5,13},{6,14},{7,15},{8,0},{9,1},... | collective-permute-start | bytes 786440 | tf_op jit(solution)/shard_map/ppermute | solution.py:490
  23.1 10.2 %collective-permute-start.7 = (bf16[64,2048]{1,0:T(8,128)(2,1)S(1)}, bf16[64,2048]{1,0:T(8,128)(2,1)S(1)}, u32[]{:S(2)}, u32[]{:S(2)}) collective-permute-start(bf16[64,2048]{1,0:T(8,128)(2,1)S(1)} %shard_map.150.refs_3_), channel_id=1, source_target_pairs={{0,6},{1,7},{2,4},{3,5},{4,2},{5,3},{6,0},{7,1},{8,14},{9,15},{10,... | collective-permute-start | bytes 786440 | tf_op jit(solution)/shard_map/ppermute | solution.py:490
  24.9 12.4 %collective-permute-start.5 = (bf16[64,2048]{1,0:T(8,128)(2,1)S(1)}, bf16[64,2048]{1,0:T(8,128)(2,1)S(1)}, u32[]{:S(2)}, u32[]{:S(2)}) collective-permute-start(bf16[64,2048]{1,0:T(8,128)(2,1)S(1)} %shard_map.150.refs_3_), channel_id=1, source_target_pairs={{0,2},{1,3},{2,0},{3,1},{4,6},{5,7},{6,4},{7,5},{8,10},{9,11},{10,... | collective-permute-start | bytes 786440 | tf_op jit(solution)/shard_map/ppermute | solution.py:490
  25.3 13.6 %collective-permute-start.6 = (bf16[64,2048]{1,0:T(8,128)(2,1)S(1)}, bf16[64,2048]{1,0:T(8,128)(2,1)S(1)}, u32[]{:S(2)}, u32[]{:S(2)}) collective-permute-start(bf16[64,2048]{1,0:T(8,128)(2,1)S(1)} %shard_map.150.refs_3_), channel_id=1, source_target_pairs={{0,4},{1,5},{2,6},{3,7},{4,0},{5,1},{6,2},{7,3},{8,12},{9,13},{10,... | collective-permute-start | bytes 786440 | tf_op jit(solution)/shard_map/ppermute | solution.py:490
  29.8 13.0 %collective-permute-start.9 = (bf16[64,2048]{1,0:T(8,128)(2,1)S(1)}, bf16[64,2048]{1,0:T(8,128)(2,1)S(1)}, u32[]{:S(2)}, u32[]{:S(2)}) collective-permute-start(bf16[64,2048]{1,0:T(8,128)(2,1)S(1)} %collective-permute-done.8.refs_5_), channel_id=1, source_target_pairs={{0,2},{1,3},{2,0},{3,1},{4,6},{5,7},{6,4},{7,5},{8,10},{9,11},{10,... | collective-permute-start | bytes 786440 | tf_op jit(solution)/shard_map/ppermute | solution.py:490
  31.4 11.6 %collective-permute-start.10 = (bf16[64,2048]{1,0:T(8,128)(2,1)S(1)}, bf16[64,2048]{1,0:T(8,128)(2,1)S(1)}, u32[]{:S(2)}, u32[]{:S(2)}) collective-permute-start(bf16[64,2048]{1,0:T(8,128)(2,1)S(1)} %collective-permute-done.8.refs_5_), channel_id=1, source_target_pairs={{0,4},{1,5},{2,6},{3,7},{4,0},{5,1},{6,2},{7,3},{8,12},{9,13},{10,... | collective-permute-start | bytes 786440 | tf_op jit(solution)/shard_map/ppermute | solution.py:490
  33.3 9.6 %collective-permute-start.11 = (bf16[64,2048]{1,0:T(8,128)(2,1)S(1)}, bf16[64,2048]{1,0:T(8,128)(2,1)S(1)}, u32[]{:S(2)}, u32[]{:S(2)}) collective-permute-start(bf16[64,2048]{1,0:T(8,128)(2,1)S(1)} %collective-permute-done.7.refs_4_), channel_id=1, source_target_pairs={{0,8},{1,9},{2,10},{3,11},{4,12},{5,13},{6,14},{7,15},{8,0},{9,1},... | collective-permute-start | bytes 786440 | tf_op jit(solution)/shard_map/ppermute | solution.py:490
  41.4 15.8 %copy-start.7 = (s32[8]{0:T(128)S(1)}, s32[8]{0:T(128)}, u32[]{:S(2)}) copy-start(s32[8]{0:T(128)} %lengths_ref.5) | copy-start | bytes 100
  41.4 15.8 %copy-start.12 = (s32[8]{0:T(128)S(1)}, s32[8]{0:T(128)}, u32[]{:S(2)}) copy-start(s32[8]{0:T(128)} %continues_ref.1) | copy-start | bytes 100

commit v5 on v4

--- a/solution.py
+++ b/solution.py
@@ -49,7 +49,13 @@
 
 
 def front(length, quarter, shards):
-    return lax.div(length - quarter + shards - 1, shards)
+    return (length - quarter + shards - 1) // shards
+
+
+def chosen(row_ref, index):
+    row = row_ref[...]
+    lane = lax.broadcasted_iota(jnp.int32, row.shape, 1)
+    return jnp.sum(jnp.where(lane == index, row, 0), axis=1, keepdims=True)
 
 
 def fetch(sources, targets, semaphores):
@@ -97,7 +103,7 @@
     group, y, core = place_of(shards)
     rows, width = here_ref.shape
     gap = 2 * BAL // shards - rows
-    length = front(lengths_ref[lax.rem(group, half)], y * CORES + core, shards)
+    length = front(chosen(lengths_ref, lax.rem(group, half)), y * CORES + core, shards)
     is_lower = lax.broadcasted_iota(jnp.int32, (rows - gap, width), 0) + gap < length
 
     def lay(lower_ref, upper_ref):
@@ -405,7 +411,7 @@
     def summed(who, logprob):
         note = got_ref[who * parts, 0][7:8, LANES // 2 :]
         breaks = [note[:, BREAKS + i : BREAKS + i + 1].astype(jnp.int32) for i in range(1, SEGS)]
-        live = slots < lengths_ref[who]
+        live = slots < chosen(lengths_ref, who)
         logprob = jnp.where(live, logprob, 0.0)
         sums, counts = [], []
         for label in range(SEGS):
@@ -421,10 +427,11 @@
     partner = group ^ 1
     logprob, sums, counts, breaks = summed(group, found[0:1])
     _, partner_sums, partner_counts, _ = summed(partner, found[2:3])
-    entropy = jnp.where(slots < lengths_ref[group], found[1:2], 0.0)
+    length = chosen(lengths_ref, group)
+    entropy = jnp.where(slots < length, found[1:2], 0.0)
     is_even = group % 2 == 0
-    joined = jnp.where(is_even, continues_ref[group], continues_ref[partner]) == 1
-    my_last = sum((lengths_ref[group] - 1 >= begin).astype(jnp.int32) for begin in breaks)
+    joined = chosen(continues_ref, jnp.where(is_even, group, partner)) == 1
+    my_last = sum((length - 1 >= begin).astype(jnp.int32) for begin in breaks)
     target = jnp.where(is_even, my_last, jnp.zeros_like(my_last))
     extra_sum, extra_count = partner_sums[0], partner_counts[0]
     for label in range(1, SEGS):
@@ -489,15 +496,15 @@
     def swap(array, group_flip, shard_flip):
         return lax.ppermute(array, axes, partners(sizes, (group_flip, shard_flip)))
 
-    def lay(kernel, shape, *operands, scalars=()):
+    def lay(kernel, shape, *operands):
         return call(
             kernel,
             jax.ShapeDtypeStruct(shape, jnp.bfloat16),
-            [SCALARS] * len(scalars) + [WHOLE] * len(operands),
+            [WHOLE] * len(operands),
             size * cap * width,
             4 * size * width,
             out_specs=WHOLE,
-        )(*scalars, *operands)
+        )(*operands)
 
     gap = size - rows
     hidden = (final_hidden, norm_gain.reshape(1, width))
@@ -547,7 +554,7 @@
         )
         heads = (head_weight, far_head)
         rest = lay(
-            functools.partial(mix_kernel, sizes), (rows, width), here, other, scalars=(group_lengths,)
+            functools.partial(mix_kernel, sizes), (rows, width), group_lengths.reshape(1, groups), here, other
         )
         far_rest = swap(rest, 2, 0)
         rest_xy = swap(rest, 1, 2)
@@ -622,12 +629,12 @@
             jax.ShapeDtypeStruct((1, SEGS), jnp.float32),
             jax.ShapeDtypeStruct((count, key_width), jnp.bfloat16),
         ),
-        [SCALARS] * 2 + [WHOLE] * 2,
+        [WHOLE] * 4,
         1 << 24,
         4 * groups * shards * 8 * LANES,
     )(
-        group_lengths,
-        continues,
+        group_lengths.reshape(1, groups),
+        continues.reshape(1, groups),
         got.reshape(groups * parts, CORES, 8, LANES),
         turned,
     )

time: 59.2 us -> 58.3 us (0.985)
  Pallas kernels: 12.8 us -> 11.9 us
  transfers between devices with their start and end apart: 12 -> 12, of which waited for: 8 -> 7; matrix products, arithmetic and copies ran while one was open for 0% -> 0% of each run, Pallas kernels for 12% -> 12%
where the time goes in v5:
time: 58.3 us; the launch traced here: 57.9 us
  starting transfers between devices  16.1 us (28%)
  Pallas kernels  11.9 us (20%)
  blocking collectives  11.3 us (19%)
  waiting for transfers between devices  9.14 us (16%)
  local copies, waits for them, and re-layouts  8.79 us (15%)
  between operations  0.73 us (1%)
    ppermute x12, starting transfers between devices, swap(): return lax.ppermute(array, axes, partners(sizes, (group_flip, shard_flip)))  16.1 us
    all_to_all x1, blocking collectives, local(): got = lax.all_to_all(sent, axes, 0, 0, tiled=False)  11.3 us
    ppermute x12, waiting for transfers between devices, swap(): return lax.ppermute(array, axes, partners(sizes, (group_flip, shard_flip)))  9.14 us
    unnamed x26, local copies, waits for them, and re-layouts  8.79 us
    pallas_call x3, Pallas kernels, score(): call(kernel, out_shape, [WHOLE] * (3 + len(extras)), 4 * vocab * count *...  7.87 us
    pallas_call x1, Pallas kernels, local(): call(functools.partial(side_kernel, sizes, swapped), (jax.ShapeDtypeStruc...  1.9 us
    pallas_call x1, Pallas kernels, local(): call(functools.partial(final_kernel, sizes), (jax.ShapeDtypeStruct((1, ca...  1.19 us
  transfers between devices with their start and end apart: 12, of which 7 were waited for; matrix products, arithmetic and copies ran while one was open for 0% of the time, Pallas kernels for 12%

profile of v5, /device:TPU:0, one launch (start us, length us, event | category | flops | bytes accessed | tf_op | source)
XLA Modules:
  0.0 57.9 jit_solution(5630841925053705621)
XLA Ops:
  0.6 0.0 copy-start.1
  0.6 1.2 %copy-done.1 = bf16[256,2048]{1,0:T(8,128)(2,1)S(1)} copy-done((bf16[256,2048]{1,0:T(8,128)(2,1)S(1)}, bf16[256,2048]{1,0:T(8,128)(2,1)}, u32[]{:S(2)}) %copy-start.1) | copy-done | bytes 1048600
  1.9 0.7 %copy-done.4 = f32[2048]{0:T(1024)S(1)} copy-done((f32[2048]{0:T(1024)S(1)}, f32[2048]{0:T(1024)}, u32[]{:S(2)}) %copy-start.4) | copy-done | bytes 8216
  2.6 0.4 shard_map.147.here_ref
  3.0 0.5 collective-permute-start.4
  3.5 3.7 %collective-permute-start = (bf16[64,2048]{1,0:T(8,128)(2,1)S(1)}, bf16[64,2048]{1,0:T(8,128)(2,1)S(1)}, u32[]{:S(2)}, u32[]{:S(2)}) collective-permute-start(bf16[64,2048]{1,0:T(8,128)(2,1)S(1)} %shard_map.147.here_ref), channel_id=1, source_target_pairs={{0,16},{1,17},{2,18},{3,19},{4,20},{5,21},{6,22},{7,23},{8,24},{9,... | collective-permute-start | bytes 786440 | tf_op jit(solution)/shard_map/ppermute | solution.py:497
  7.2 0.3 shard_map.148.refs_0_
  7.5 1.6 %collective-permute-start.1 = (bf16[2,16,2048]{2,1,0:T(8,128)(2,1)S(1)}, bf16[2,16,2048]{2,1,0:T(8,128)(2,1)S(1)}, u32[]{:S(2)}, u32[]{:S(2)}) collective-permute-start(bf16[2,16,2048]{2,1,0:T(8,128)(2,1)S(1)} %shard_map.148.refs_0_), channel_id=1, source_target_pairs={{0,4},{1,5},{2,6},{3,7},{4,0},{5,1},{6,2},{7,3},{8,12},{9,13},{10,... | collective-permute-start | bytes 393224 | tf_op jit(solution)/shard_map/ppermute | solution.py:497
  9.1 1.6 %collective-permute-start.2 = (bf16[2,16,2048]{2,1,0:T(8,128)(2,1)S(1)}, bf16[2,16,2048]{2,1,0:T(8,128)(2,1)S(1)}, u32[]{:S(2)}, u32[]{:S(2)}) collective-permute-start(bf16[2,16,2048]{2,1,0:T(8,128)(2,1)S(1)} %shard_map.148.refs_0_), channel_id=1, source_target_pairs={{0,8},{1,9},{2,10},{3,11},{4,12},{5,13},{6,14},{7,15},{8,0},{9,1},... | collective-permute-start | bytes 393224 | tf_op jit(solution)/shard_map/ppermute | solution.py:497
  10.7 0.4 collective-permute-start.3
  11.1 1.6 %copy-done.2 = bf16[2048,512]{1,0:T(8,128)(2,1)S(1)} copy-done((bf16[2048,512]{1,0:T(8,128)(2,1)S(1)}, bf16[2048,512]{1,0:T(8,128)(2,1)}, u32[]{:S(2)}) %copy-start.2) | copy-done | bytes 2097176
  12.7 1.2 %copy-done.3 = bf16[256,2048]{1,0:T(8,128)(2,1)S(1)} copy-done((bf16[256,2048]{1,0:T(8,128)(2,1)S(1)}, bf16[256,2048]{1,0:T(8,128)(2,1)}, u32[]{:S(2)}) %copy-start.3) | copy-done | bytes 1048600
  13.9 0.7 %copy-done.5 = s32[2048]{0:T(1024)S(1)} copy-done((s32[2048]{0:T(1024)S(1)}, s32[2048]{0:T(1024)}, u32[]{:S(2)}) %copy-start.5) | copy-done | bytes 8216
  14.6 0.7 %copy-done.6 = s32[8]{0:T(128)S(1)} copy-done((s32[8]{0:T(128)S(1)}, s32[8]{0:T(128)}, u32[]{:S(2)}) %copy-start.6) | copy-done | bytes 56
  15.2 0.7 %copy-done.8 = f32[512]{0:T(512)S(1)} copy-done((f32[512]{0:T(512)S(1)}, f32[512]{0:T(512)}, u32[]{:S(2)}) %copy-start.8) | copy-done | bytes 2072
  15.9 0.7 %copy-done.9 = s32[256]{0:T(256)S(1)} copy-done((s32[256]{0:T(256)S(1)}, s32[256]{0:T(256)}, u32[]{:S(2)}) %copy-start.9) | copy-done | bytes 1048
  16.6 0.7 %copy-done.10 = s32[256]{0:T(256)S(1)} copy-done((s32[256]{0:T(256)S(1)}, s32[256]{0:T(256)}, u32[]{:S(2)}) %copy-start.10) | copy-done | bytes 1048
  17.3 0.7 %copy-done.11 = s32[25]{0:T(128)S(1)} copy-done((s32[25]{0:T(128)S(1)}, s32[25]{0:T(128)}, u32[]{:S(2)}) %copy-start.11) | copy-done | bytes 124
  17.9 1.9 %shard_map.149 = (f32[25,512]{1,0:T(8,128)S(1)}, f32[1,64]{1,0:T(1,128)S(1)}, s32[1,240]{1,0:T(1,128)S(1)}, s32[1,160]{1,0:T(1,128)S(1)}, s32[1,240]{1,0:T(1,128)S(1)}) custom-call(s32[8]{0:T(128)S(1)} %copy-done.6, s32[1,25]{1,0:T(1,128)S(1)} %bitcast.21, s32[1,256]{1,0:T(1,128)S(1)} %bitcast.19, s32[1,256]{1,0:T(1,128)S(1)} %bitcast.20, ...), custom_call_target="tpu_custom_call" | custom-call | flops 52428800 | bytes 2097152 | tf_op jit(solution)/shard_map/pallas_call | solution.py:514
  19.8 0.0 collective-permute-done.1.refs_1_
  19.9 0.0 collective-permute-done.2.refs_2_.beyond_ref
  19.9 1.7 %collective-permute-done.3.corner_ref = bf16[2,16,2048]{2,1,0:T(8,128)(2,1)S(1)} collective-permute-done((bf16[2,16,2048]{2,1,0:T(8,128)(2,1)S(1)}, bf16[2,16,2048]{2,1,0:T(8,128)(2,1)S(1)}, u32[]{:S(2)}, u32[]{:S(2)}) %collective-permute-start.3) | collective-permute-done | bytes 131104 | tf_op jit(solution)/shard_map/ppermute | solution.py:497
  21.6 0.0 collective-permute-done.other_ref
  21.7 0.0 collective-permute-done.4.far_ref
  21.7 0.2 shard_map.150.refs_3_
  21.8 0.8 %collective-permute-start.8 = (bf16[64,2048]{1,0:T(8,128)(2,1)S(1)}, bf16[64,2048]{1,0:T(8,128)(2,1)S(1)}, u32[]{:S(2)}, u32[]{:S(2)}) collective-permute-start(bf16[64,2048]{1,0:T(8,128)(2,1)S(1)} %shard_map.150.refs_3_), channel_id=1, source_target_pairs={{0,8},{1,9},{2,10},{3,11},{4,12},{5,13},{6,14},{7,15},{8,0},{9,1},... | collective-permute-start | bytes 786440 | tf_op jit(solution)/shard_map/ppermute | solution.py:497
  22.6 1.8 %collective-permute-start.7 = (bf16[64,2048]{1,0:T(8,128)(2,1)S(1)}, bf16[64,2048]{1,0:T(8,128)(2,1)S(1)}, u32[]{:S(2)}, u32[]{:S(2)}) collective-permute-start(bf16[64,2048]{1,0:T(8,128)(2,1)S(1)} %shard_map.150.refs_3_), channel_id=1, source_target_pairs={{0,6},{1,7},{2,4},{3,5},{4,2},{5,3},{6,0},{7,1},{8,14},{9,15},{10,... | collective-permute-start | bytes 786440 | tf_op jit(solution)/shard_map/ppermute | solution.py:497
  24.4 0.4 collective-permute-start.5
  24.8 1.3 %collective-permute-start.6 = (bf16[64,2048]{1,0:T(8,128)(2,1)S(1)}, bf16[64,2048]{1,0:T(8,128)(2,1)S(1)}, u32[]{:S(2)}, u32[]{:S(2)}) collective-permute-start(bf16[64,2048]{1,0:T(8,128)(2,1)S(1)} %shard_map.150.refs_3_), channel_id=1, source_target_pairs={{0,4},{1,5},{2,6},{3,7},{4,0},{5,1},{6,2},{7,3},{8,12},{9,13},{10,... | collective-permute-start | bytes 786440 | tf_op jit(solution)/shard_map/ppermute | solution.py:497
  26.1 3.2 %collective-permute-done.8.refs_5_ = bf16[64,2048]{1,0:T(8,128)(2,1)S(1)} collective-permute-done((bf16[64,2048]{1,0:T(8,128)(2,1)S(1)}, bf16[64,2048]{1,0:T(8,128)(2,1)S(1)}, u32[]{:S(2)}, u32[]{:S(2)}) %collective-permute-start.8) | collective-permute-done | bytes 262176 | tf_op jit(solution)/shard_map/ppermute | solution.py:497
  29.4 1.5 %collective-permute-start.9 = (bf16[64,2048]{1,0:T(8,128)(2,1)S(1)}, bf16[64,2048]{1,0:T(8,128)(2,1)S(1)}, u32[]{:S(2)}, u32[]{:S(2)}) collective-permute-start(bf16[64,2048]{1,0:T(8,128)(2,1)S(1)} %collective-permute-done.8.refs_5_), channel_id=1, source_target_pairs={{0,2},{1,3},{2,0},{3,1},{4,6},{5,7},{6,4},{7,5},{8,10},{9,11},{10,... | collective-permute-start | bytes 786440 | tf_op jit(solution)/shard_map/ppermute | solution.py:497
  30.9 1.2 %collective-permute-start.10 = (bf16[64,2048]{1,0:T(8,128)(2,1)S(1)}, bf16[64,2048]{1,0:T(8,128)(2,1)S(1)}, u32[]{:S(2)}, u32[]{:S(2)}) collective-permute-start(bf16[64,2048]{1,0:T(8,128)(2,1)S(1)} %collective-permute-done.8.refs_5_), channel_id=1, source_target_pairs={{0,4},{1,5},{2,6},{3,7},{4,0},{5,1},{6,2},{7,3},{8,12},{9,13},{10,... | collective-permute-start | bytes 786440 | tf_op jit(solution)/shard_map/ppermute | solution.py:497
  32.1 0.7 %collective-permute-done.7.refs_4_ = bf16[64,2048]{1,0:T(8,128)(2,1)S(1)} collective-permute-done((bf16[64,2048]{1,0:T(8,128)(2,1)S(1)}, bf16[64,2048]{1,0:T(8,128)(2,1)S(1)}, u32[]{:S(2)}, u32[]{:S(2)}) %collective-permute-start.7) | collective-permute-done | bytes 262176 | tf_op jit(solution)/shard_map/ppermute | solution.py:497
  32.8 1.3 %collective-permute-start.11 = (bf16[64,2048]{1,0:T(8,128)(2,1)S(1)}, bf16[64,2048]{1,0:T(8,128)(2,1)S(1)}, u32[]{:S(2)}, u32[]{:S(2)}) collective-permute-start(bf16[64,2048]{1,0:T(8,128)(2,1)S(1)} %collective-permute-done.7.refs_4_), channel_id=1, source_target_pairs={{0,8},{1,9},{2,10},{3,11},{4,12},{5,13},{6,14},{7,15},{8,0},{9,1},... | collective-permute-start | bytes 786440 | tf_op jit(solution)/shard_map/ppermute | solution.py:497
  34.1 0.0 copy-done
  34.1 2.5 %shard_map.151.first_ref = f32[8,240]{1,0:T(8,128)S(1)} custom-call(s32[1,240]{1,0:T(1,128)S(1)} %get-tuple-element.38.targets_ref, bf16[784,2048]{1,0:T(8,128)(2,1)S(1)} %copy-done, bf16[784,2048]{1,0:T(8,128)(2,1)S(1)} %collective-permute-done.4.far_ref, bf16[2,16,2048]{2,1,0:T(8,128)(2,1)S(1)} %shard_map.148.refs_0_, ...), custom_call_target="tpu_custom_call" | custom-call | flops 1541406720 | bytes 7405568 | tf_op jit(solution)/shard_map/pallas_call | solution.py:259
  36.6 0.2 collective-permute-done.5.refs_2_
  36.8 1.6 %collective-permute-done.6.refs_3_ = bf16[64,2048]{1,0:T(8,128)(2,1)S(1)} collective-permute-done((bf16[64,2048]{1,0:T(8,128)(2,1)S(1)}, bf16[64,2048]{1,0:T(8,128)(2,1)S(1)}, u32[]{:S(2)}, u32[]{:S(2)}) %collective-permute-start.6) | collective-permute-done | bytes 262176 | tf_op jit(solution)/shard_map/ppermute | solution.py:497
  38.5 2.5 %shard_map.152.second_ref = f32[8,160]{1,0:T(8,128)S(1)} custom-call(s32[1,160]{1,0:T(1,128)S(1)} %get-tuple-element.42.targets_ref, bf16[784,2048]{1,0:T(8,128)(2,1)S(1)} %copy-done, bf16[784,2048]{1,0:T(8,128)(2,1)S(1)} %collective-permute-done.4.far_ref, bf16[2,16,2048]{2,1,0:T(8,128)(2,1)S(1)} %shard_map.148.refs_0_, ...), custom_call_target="tpu_custom_call" | custom-call | flops 1027604480 | bytes 7077888 | tf_op jit(solution)/shard_map/pallas_call | solution.py:259
  40.9 0.0 copy-start.7
  40.9 0.0 copy-start.12
  40.9 1.4 %collective-permute-done.9.refs_0_ = bf16[64,2048]{1,0:T(8,128)(2,1)S(1)} collective-permute-done((bf16[64,2048]{1,0:T(8,128)(2,1)S(1)}, bf16[64,2048]{1,0:T(8,128)(2,1)S(1)}, u32[]{:S(2)}, u32[]{:S(2)}) %collective-permute-start.9) | collective-permute-done | bytes 262176 | tf_op jit(solution)/shard_map/ppermute | solution.py:497
  42.4 0.1 collective-permute-done.10.refs_1_
  42.5 0.0 collective-permute-done.11.refs_2_
  42.5 2.9 %shard_map.153 = f32[32,8,128]{2,1,0:T(8,128)S(1)} custom-call(s32[1,240]{1,0:T(1,128)S(1)} %get-tuple-element.35.targets_ref, bf16[784,2048]{1,0:T(8,128)(2,1)S(1)} %copy-done, bf16[784,2048]{1,0:T(8,128)(2,1)S(1)} %collective-permute-done.4.far_ref, f32[8,240]{1,0:T(8,128)S(1)} %shard_map.151.first_ref, f32[8,160]{1,0:T(8,128)S(1)} %shard_map.152.second_ref, ...), custom_call_target="tpu_custom_call" | custom-call | flops 1541406720 | bytes 7405568 | tf_op jit(solution)/shard_map/pallas_call | solution.py:259
  45.4 11.3 %all_to_all.5 = f32[32,8,128]{2,1,0:T(8,128)S(1)} all-to-all(f32[32,8,128]{2,1,0:T(8,128)S(1)} %shard_map.153), channel_id=1, replica_groups=mesh['grp'=8,'vocab'=4] {'grp','vocab'}, dimensions={0} | all-to-all | bytes 262144 | tf_op jit(solution)/shard_map/all_to_all | solution.py:622
  56.7 0.0 copy-done.12
  56.7 1.2 %shard_map.154 = (f32[1,256]{1,0:T(1,128)}, f32[1,256]{1,0:T(1,128)}, f32[1,4]{1,0:T(1,128)}, bf16[25,512]{1,0:T(8,128)(2,1)}) custom-call(s32[1,8]{1,0:T(1,128)S(1)} %bitcast.17, s32[1,8]{1,0:T(1,128)S(1)} %bitcast.22, f32[16,2,8,128]{3,2,1,0:T(8,128)S(1)} %bitcast.12, f32[25,512]{1,0:T(8,128)S(1)} %get-tuple-element.47.turned_ref), custom_call_target="tpu_custom_call" | custom-call | flops 16777216 | bytes 131072 | tf_op jit(solution)/shard_map/pallas_call | solution.py:624
  (11 shorter events, 0.0 us)
Async XLA Ops:
  0.6 1.2 %copy-start.1 = (bf16[256,2048]{1,0:T(8,128)(2,1)S(1)}, bf16[256,2048]{1,0:T(8,128)(2,1)}, u32[]{:S(2)}) copy-start(bf16[256,2048]{1,0:T(8,128)(2,1)} %hidden_ref.3) | copy-start | bytes 3145732
  1.9 0.7 %copy-start.4 = (f32[2048]{0:T(1024)S(1)}, f32[2048]{0:T(1024)}, u32[]{:S(2)}) copy-start(f32[2048]{0:T(1024)} %param.13) | copy-start | bytes 24580
  2.6 31.5 %copy-start = (bf16[784,2048]{1,0:T(8,128)(2,1)S(1)}, bf16[784,2048]{1,0:T(8,128)(2,1)}, u32[]{:S(2)}) copy-start(bf16[784,2048]{1,0:T(8,128)(2,1)} %near_ref.2) | copy-start | bytes 9633796
  3.0 18.7 %collective-permute-start.4 = (bf16[784,2048]{1,0:T(8,128)(2,1)}, bf16[784,2048]{1,0:T(8,128)(2,1)S(1)}, u32[]{:S(2)}, u32[]{:S(2)}) collective-permute-start(bf16[784,2048]{1,0:T(8,128)(2,1)} %near_ref.2), channel_id=1, source_target_pairs={{0,1},{1,0},{2,3},{3,2},{4,5},{5,4},{6,7},{7,6},{8,9},{9,8},{10,11... | collective-permute-start | bytes 9633800 | tf_op jit(solution)/shard_map/ppermute | solution.py:497
  3.5 18.2 %collective-permute-start = (bf16[64,2048]{1,0:T(8,128)(2,1)S(1)}, bf16[64,2048]{1,0:T(8,128)(2,1)S(1)}, u32[]{:S(2)}, u32[]{:S(2)}) collective-permute-start(bf16[64,2048]{1,0:T(8,128)(2,1)S(1)} %shard_map.147.here_ref), channel_id=1, source_target_pairs={{0,16},{1,17},{2,18},{3,19},{4,20},{5,21},{6,22},{7,23},{8,24},{9,... | collective-permute-start | bytes 786440 | tf_op jit(solution)/shard_map/ppermute | solution.py:497
  7.5 12.3 %collective-permute-start.1 = (bf16[2,16,2048]{2,1,0:T(8,128)(2,1)S(1)}, bf16[2,16,2048]{2,1,0:T(8,128)(2,1)S(1)}, u32[]{:S(2)}, u32[]{:S(2)}) collective-permute-start(bf16[2,16,2048]{2,1,0:T(8,128)(2,1)S(1)} %shard_map.148.refs_0_), channel_id=1, source_target_pairs={{0,4},{1,5},{2,6},{3,7},{4,0},{5,1},{6,2},{7,3},{8,12},{9,13},{10,... | collective-permute-start | bytes 393224 | tf_op jit(solution)/shard_map/ppermute | solution.py:497
  9.1 10.8 %collective-permute-start.2 = (bf16[2,16,2048]{2,1,0:T(8,128)(2,1)S(1)}, bf16[2,16,2048]{2,1,0:T(8,128)(2,1)S(1)}, u32[]{:S(2)}, u32[]{:S(2)}) collective-permute-start(bf16[2,16,2048]{2,1,0:T(8,128)(2,1)S(1)} %shard_map.148.refs_0_), channel_id=1, source_target_pairs={{0,8},{1,9},{2,10},{3,11},{4,12},{5,13},{6,14},{7,15},{8,0},{9,1},... | collective-permute-start | bytes 393224 | tf_op jit(solution)/shard_map/ppermute | solution.py:497
  10.7 11.0 %collective-permute-start.3 = (bf16[2,16,2048]{2,1,0:T(8,128)(2,1)S(1)}, bf16[2,16,2048]{2,1,0:T(8,128)(2,1)S(1)}, u32[]{:S(2)}, u32[]{:S(2)}) collective-permute-start(bf16[2,16,2048]{2,1,0:T(8,128)(2,1)S(1)} %shard_map.148.refs_0_), channel_id=1, source_target_pairs={{0,12},{1,13},{2,14},{3,15},{4,8},{5,9},{6,10},{7,11},{8,4},{9,5},... | collective-permute-start | bytes 393224 | tf_op jit(solution)/shard_map/ppermute | solution.py:497
  11.1 1.6 %copy-start.2 = (bf16[2048,512]{1,0:T(8,128)(2,1)S(1)}, bf16[2048,512]{1,0:T(8,128)(2,1)}, u32[]{:S(2)}) copy-start(bf16[2048,512]{1,0:T(8,128)(2,1)} %weight_hbm.1) | copy-start | bytes 6291460
  12.7 1.2 %copy-start.3 = (bf16[256,2048]{1,0:T(8,128)(2,1)S(1)}, bf16[256,2048]{1,0:T(8,128)(2,1)}, u32[]{:S(2)}) copy-start(bf16[256,2048]{1,0:T(8,128)(2,1)} %input_hbm.1) | copy-start | bytes 3145732
  13.9 0.7 %copy-start.5 = (s32[2048]{0:T(1024)S(1)}, s32[2048]{0:T(1024)}, u32[]{:S(2)}) copy-start(s32[2048]{0:T(1024)} %param.15) | copy-start | bytes 24580
  14.6 0.7 %copy-start.6 = (s32[8]{0:T(128)S(1)}, s32[8]{0:T(128)}, u32[]{:S(2)}) copy-start(s32[8]{0:T(128)} %lengths_ref.1) | copy-start | bytes 100
  15.2 0.7 %copy-start.8 = (f32[512]{0:T(512)S(1)}, f32[512]{0:T(512)}, u32[]{:S(2)}) copy-start(f32[512]{0:T(512)} %param.21) | copy-start | bytes 6148
  15.9 0.7 %copy-start.9 = (s32[256]{0:T(256)S(1)}, s32[256]{0:T(256)}, u32[]{:S(2)}) copy-start(s32[256]{0:T(256)} %param.22) | copy-start | bytes 3076
  16.6 0.7 %copy-start.10 = (s32[256]{0:T(256)S(1)}, s32[256]{0:T(256)}, u32[]{:S(2)}) copy-start(s32[256]{0:T(256)} %param.17) | copy-start | bytes 3076
  17.3 0.7 %copy-start.11 = (s32[25]{0:T(128)S(1)}, s32[25]{0:T(128)}, u32[]{:S(2)}) copy-start(s32[25]{0:T(128)} %param.23) | copy-start | bytes 304
  21.8 7.6 %collective-permute-start.8 = (bf16[64,2048]{1,0:T(8,128)(2,1)S(1)}, bf16[64,2048]{1,0:T(8,128)(2,1)S(1)}, u32[]{:S(2)}, u32[]{:S(2)}) collective-permute-start(bf16[64,2048]{1,0:T(8,128)(2,1)S(1)} %shard_map.150.refs_3_), channel_id=1, source_target_pairs={{0,8},{1,9},{2,10},{3,11},{4,12},{5,13},{6,14},{7,15},{8,0},{9,1},... | collective-permute-start | bytes 786440 | tf_op jit(solution)/shard_map/ppermute | solution.py:497
  22.6 10.2 %collective-permute-start.7 = (bf16[64,2048]{1,0:T(8,128)(2,1)S(1)}, bf16[64,2048]{1,0:T(8,128)(2,1)S(1)}, u32[]{:S(2)}, u32[]{:S(2)}) collective-permute-start(bf16[64,2048]{1,0:T(8,128)(2,1)S(1)} %shard_map.150.refs_3_), channel_id=1, source_target_pairs={{0,6},{1,7},{2,4},{3,5},{4,2},{5,3},{6,0},{7,1},{8,14},{9,15},{10,... | collective-permute-start | bytes 786440 | tf_op jit(solution)/shard_map/ppermute | solution.py:497
  24.4 12.4 %collective-permute-start.5 = (bf16[64,2048]{1,0:T(8,128)(2,1)S(1)}, bf16[64,2048]{1,0:T(8,128)(2,1)S(1)}, u32[]{:S(2)}, u32[]{:S(2)}) collective-permute-start(bf16[64,2048]{1,0:T(8,128)(2,1)S(1)} %shard_map.150.refs_3_), channel_id=1, source_target_pairs={{0,2},{1,3},{2,0},{3,1},{4,6},{5,7},{6,4},{7,5},{8,10},{9,11},{10,... | collective-permute-start | bytes 786440 | tf_op jit(solution)/shard_map/ppermute | solution.py:497
  24.8 13.6 %collective-permute-start.6 = (bf16[64,2048]{1,0:T(8,128)(2,1)S(1)}, bf16[64,2048]{1,0:T(8,128)(2,1)S(1)}, u32[]{:S(2)}, u32[]{:S(2)}) collective-permute-start(bf16[64,2048]{1,0:T(8,128)(2,1)S(1)} %shard_map.150.refs_3_), channel_id=1, source_target_pairs={{0,4},{1,5},{2,6},{3,7},{4,0},{5,1},{6,2},{7,3},{8,12},{9,13},{10,... | collective-permute-start | bytes 786440 | tf_op jit(solution)/shard_map/ppermute | solution.py:497
  29.4 13.0 %collective-permute-start.9 = (bf16[64,2048]{1,0:T(8,128)(2,1)S(1)}, bf16[64,2048]{1,0:T(8,128)(2,1)S(1)}, u32[]{:S(2)}, u32[]{:S(2)}) collective-permute-start(bf16[64,2048]{1,0:T(8,128)(2,1)S(1)} %collective-permute-done.8.refs_5_), channel_id=1, source_target_pairs={{0,2},{1,3},{2,0},{3,1},{4,6},{5,7},{6,4},{7,5},{8,10},{9,11},{10,... | collective-permute-start | bytes 786440 | tf_op jit(solution)/shard_map/ppermute | solution.py:497
  30.9 11.6 %collective-permute-start.10 = (bf16[64,2048]{1,0:T(8,128)(2,1)S(1)}, bf16[64,2048]{1,0:T(8,128)(2,1)S(1)}, u32[]{:S(2)}, u32[]{:S(2)}) collective-permute-start(bf16[64,2048]{1,0:T(8,128)(2,1)S(1)} %collective-permute-done.8.refs_5_), channel_id=1, source_target_pairs={{0,4},{1,5},{2,6},{3,7},{4,0},{5,1},{6,2},{7,3},{8,12},{9,13},{10,... | collective-permute-start | bytes 786440 | tf_op jit(solution)/shard_map/ppermute | solution.py:497
  32.8 9.6 %collective-permute-start.11 = (bf16[64,2048]{1,0:T(8,128)(2,1)S(1)}, bf16[64,2048]{1,0:T(8,128)(2,1)S(1)}, u32[]{:S(2)}, u32[]{:S(2)}) collective-permute-start(bf16[64,2048]{1,0:T(8,128)(2,1)S(1)} %collective-permute-done.7.refs_4_), channel_id=1, source_target_pairs={{0,8},{1,9},{2,10},{3,11},{4,12},{5,13},{6,14},{7,15},{8,0},{9,1},... | collective-permute-start | bytes 786440 | tf_op jit(solution)/shard_map/ppermute | solution.py:497
  40.9 15.8 %copy-start.7 = (s32[8]{0:T(128)S(1)}, s32[8]{0:T(128)}, u32[]{:S(2)}) copy-start(s32[8]{0:T(128)} %lengths_ref.1) | copy-start | bytes 100
  40.9 15.8 %copy-start.12 = (s32[8]{0:T(128)S(1)}, s32[8]{0:T(128)}, u32[]{:S(2)}) copy-start(s32[8]{0:T(128)} %param.18) | copy-start | bytes 100

commit v6 on v5

--- a/solution.py
+++ b/solution.py
@@ -121,25 +121,46 @@
     out_ref[rows - gap : rows, :] = other_ref[0:gap, :]
 
 
-def gather_pieces(pieces, tokens_ref):
+def gather_pieces(sizes, pieces, tokens_ref):
+    is_first = lax.axis_index("grp") < sizes[0] // 2
     start = 0
     for end, rest_ref in pieces:
         gap, rows = end.shape[0], rest_ref.shape[0]
-        tokens_ref[start : start + gap, :] = end[...]
-        tokens_ref[start + gap : start + gap + rows, :] = rest_ref[...]
+        last = start + rows
+        own, partner = jnp.where(is_first, start, last), jnp.where(is_first, last, start)
+        tokens_ref[pl.ds(pl.multiple_of(own, 16), gap), :] = end[...]
+        tokens_ref[start + gap : last, :] = rest_ref[0 : rows - gap, :]
+        tokens_ref[pl.ds(pl.multiple_of(partner, 16), gap), :] = rest_ref[rows - gap : rows, :]
         start += gap + rows
     return tokens_ref[...]
 
 
 def statistics(bases, targets, tokens, heads):
+    vocab = heads[0].shape[0]
+    cuts = [0, vocab]
+    if vocab % 16 == 0:
+        cuts = [vocab * i // 2 // 16 * 16 for i in range(2)] + [vocab]
+    chunks = [
+        (base + start, head_ref, start, stop)
+        for base, head_ref in zip(bases, heads)
+        for start, stop in zip(cuts, cuts[1:])
+    ]
+
+    def logits_of(chunk):
+        _, head_ref, start, stop = chunk
+        product = lax.dot_general(
+            head_ref[start:stop, :], tokens, (((1,), (1,)), ((), ())), preferred_element_type=jnp.float32
+        )
+        return product.astype(jnp.bfloat16).astype(jnp.float32)
+
     state = None
-    for base, head_ref in zip(bases, heads):
-        logits = lax.dot_general(
-            head_ref[...], tokens, (((1,), (1,)), ((), ())), preferred_element_type=jnp.float32
-        )
-        logits = logits.astype(jnp.bfloat16).astype(jnp.float32)
+    ready = [logits_of(chunk) for chunk in chunks[:1]]
+    for i, chunk in enumerate(chunks):
+        if i + 1 < len(chunks):
+            ready.append(logits_of(chunks[i + 1]))
+        logits = ready[i]
         entry = lax.broadcasted_iota(jnp.int32, logits.shape, 0)
-        found = jnp.where(entry == targets - base, logits, 0.0)
+        found = jnp.where(entry == targets - chunk[0], logits, 0.0)
         picked = jnp.sum(found, axis=0, keepdims=True)
         top = jnp.max(logits, axis=0, keepdims=True)
         if state is not None:
@@ -210,7 +231,7 @@
 def piece_kernel(sizes, picks, targets_ref, near_ref, far_ref, *refs):
     *pieces, out_ref, tokens_ref = refs
     ends = [ref.at[which] for ref, which in zip(pieces, picks)]
-    tokens = gather_pieces(zip(ends, pieces[len(picks) :]), tokens_ref)
+    tokens = gather_pieces(sizes, zip(ends, pieces[len(picks) :]), tokens_ref)
     state = statistics(bases_of(sizes, near_ref), targets_ref[...], tokens, (near_ref, far_ref))
     rows_of(state, out_ref)
 
@@ -222,17 +243,11 @@
     groups, shards = sizes
     size = 2 * BAL // shards
     ends = (beyond_ref.at[1], corner_ref.at[0], corner_ref.at[1])
-    tokens = gather_pieces(zip(ends, rests), tokens_ref)
+    tokens = gather_pieces(sizes, zip(ends, rests), tokens_ref)
     state = statistics(bases_of(sizes, near_ref), targets_ref[...], tokens, (near_ref, far_ref))
     group, y, _ = place_of(shards)
-    gap = beyond_ref.shape[1]
 
     def settled(rows):
-        blocks = [rows[:, i * size : (i + 1) * size] for i in range(4)]
-        blocks = [
-            jnp.concatenate([b[:, size - gap :], b[:, gap : size - gap], b[:, :gap]], axis=1) for b in blocks
-        ]
-        rows = jnp.where(group < groups // 2, rows, jnp.concatenate(blocks, axis=1))
         turned = jnp.concatenate([rows[:, 2 * size :], rows[:, : 2 * size]], axis=1)
         rows = jnp.where(lax.rem(group, 2) == 1, turned, rows)
         quarters = [rows[:, i * size : (i + 1) * size] for i in (1, 0, 3, 2)]
@@ -308,10 +323,6 @@
         for start, slot in enumerate(SLOTS):
             place = lane - start * size
             here = (place >= 0) & (place < size)
-            gap = size - cap // shards
-            back = jnp.where(place < gap, place + size - gap, place - (size - gap))
-            back = jnp.where((place >= gap) & (place < size - gap), place, back)
-            place = jnp.where(group < half, place, back)
             lower = lax.rem(group, half) ^ (slot // 4 * 2) ^ (slot // 2 % 2)
             quarter = (y ^ (slot % 2)) * CORES + core
             is_lower = place < front(lengths_ref[lower], quarter, shards)

time: 58.3 us -> 58.1 us (level)
  Pallas kernels: 11.9 us -> 11.3 us
where the time goes in v6:
time: 58.1 us; the launch traced here: 57.6 us
  starting transfers between devices  16.1 us (28%)
  Pallas kernels  11.3 us (19%)
  blocking collectives  11.3 us (19%)
  waiting for transfers between devices  9.41 us (16%)
  local copies, waits for them, and re-layouts  8.79 us (15%)
  between operations  0.74 us (1%)
    ppermute x12, starting transfers between devices, swap(): return lax.ppermute(array, axes, partners(sizes, (group_flip, shard_flip)))  16.1 us
    all_to_all x1, blocking collectives, local(): got = lax.all_to_all(sent, axes, 0, 0, tiled=False)  11.3 us
    ppermute x12, waiting for transfers between devices, swap(): return lax.ppermute(array, axes, partners(sizes, (group_flip, shard_flip)))  9.41 us
    unnamed x26, local copies, waits for them, and re-layouts  8.79 us
    pallas_call x3, Pallas kernels, score(): call(kernel, out_shape, [WHOLE] * (3 + len(extras)), 4 * vocab * count *...  7.32 us
    pallas_call x1, Pallas kernels, local(): call(functools.partial(side_kernel, sizes, swapped), (jax.ShapeDtypeStruc...  1.9 us
    pallas_call x1, Pallas kernels, local(): call(functools.partial(final_kernel, sizes), (jax.ShapeDtypeStruct((1, ca...  1.19 us
  transfers between devices with their start and end apart: 12, of which 7 were waited for; matrix products, arithmetic and copies ran while one was open for 0% of the time, Pallas kernels for 12%

profile of v6, /device:TPU:0, one launch (start us, length us, event | category | flops | bytes accessed | tf_op | source)
XLA Modules:
  0.0 57.6 jit_solution(8016743005239388183)
XLA Ops:
  0.6 0.0 copy-start.1
  0.6 1.2 %copy-done.1 = bf16[256,2048]{1,0:T(8,128)(2,1)S(1)} copy-done((bf16[256,2048]{1,0:T(8,128)(2,1)S(1)}, bf16[256,2048]{1,0:T(8,128)(2,1)}, u32[]{:S(2)}) %copy-start.1) | copy-done | bytes 1048600
  1.9 0.7 %copy-done.4 = f32[2048]{0:T(1024)S(1)} copy-done((f32[2048]{0:T(1024)S(1)}, f32[2048]{0:T(1024)}, u32[]{:S(2)}) %copy-start.4) | copy-done | bytes 8216
  2.6 0.4 shard_map.147.here_ref
  3.0 0.5 collective-permute-start.4
  3.5 3.7 %collective-permute-start = (bf16[64,2048]{1,0:T(8,128)(2,1)S(1)}, bf16[64,2048]{1,0:T(8,128)(2,1)S(1)}, u32[]{:S(2)}, u32[]{:S(2)}) collective-permute-start(bf16[64,2048]{1,0:T(8,128)(2,1)S(1)} %shard_map.147.here_ref), channel_id=1, source_target_pairs={{0,16},{1,17},{2,18},{3,19},{4,20},{5,21},{6,22},{7,23},{8,24},{9,... | collective-permute-start | bytes 786440 | tf_op jit(solution)/shard_map/ppermute | solution.py:508
  7.2 0.3 shard_map.148.refs_0_
  7.5 1.6 %collective-permute-start.1 = (bf16[2,16,2048]{2,1,0:T(8,128)(2,1)S(1)}, bf16[2,16,2048]{2,1,0:T(8,128)(2,1)S(1)}, u32[]{:S(2)}, u32[]{:S(2)}) collective-permute-start(bf16[2,16,2048]{2,1,0:T(8,128)(2,1)S(1)} %shard_map.148.refs_0_), channel_id=1, source_target_pairs={{0,4},{1,5},{2,6},{3,7},{4,0},{5,1},{6,2},{7,3},{8,12},{9,13},{10,... | collective-permute-start | bytes 393224 | tf_op jit(solution)/shard_map/ppermute | solution.py:508
  9.1 1.6 %collective-permute-start.2 = (bf16[2,16,2048]{2,1,0:T(8,128)(2,1)S(1)}, bf16[2,16,2048]{2,1,0:T(8,128)(2,1)S(1)}, u32[]{:S(2)}, u32[]{:S(2)}) collective-permute-start(bf16[2,16,2048]{2,1,0:T(8,128)(2,1)S(1)} %shard_map.148.refs_0_), channel_id=1, source_target_pairs={{0,8},{1,9},{2,10},{3,11},{4,12},{5,13},{6,14},{7,15},{8,0},{9,1},... | collective-permute-start | bytes 393224 | tf_op jit(solution)/shard_map/ppermute | solution.py:508
  10.7 0.4 collective-permute-start.3
  11.1 1.6 %copy-done.2 = bf16[2048,512]{1,0:T(8,128)(2,1)S(1)} copy-done((bf16[2048,512]{1,0:T(8,128)(2,1)S(1)}, bf16[2048,512]{1,0:T(8,128)(2,1)}, u32[]{:S(2)}) %copy-start.2) | copy-done | bytes 2097176
  12.7 1.2 %copy-done.3 = bf16[256,2048]{1,0:T(8,128)(2,1)S(1)} copy-done((bf16[256,2048]{1,0:T(8,128)(2,1)S(1)}, bf16[256,2048]{1,0:T(8,128)(2,1)}, u32[]{:S(2)}) %copy-start.3) | copy-done | bytes 1048600
  13.9 0.7 %copy-done.5 = s32[2048]{0:T(1024)S(1)} copy-done((s32[2048]{0:T(1024)S(1)}, s32[2048]{0:T(1024)}, u32[]{:S(2)}) %copy-start.5) | copy-done | bytes 8216
  14.6 0.7 %copy-done.6 = s32[8]{0:T(128)S(1)} copy-done((s32[8]{0:T(128)S(1)}, s32[8]{0:T(128)}, u32[]{:S(2)}) %copy-start.6) | copy-done | bytes 56
  15.2 0.7 %copy-done.8 = f32[512]{0:T(512)S(1)} copy-done((f32[512]{0:T(512)S(1)}, f32[512]{0:T(512)}, u32[]{:S(2)}) %copy-start.8) | copy-done | bytes 2072
  15.9 0.7 %copy-done.9 = s32[256]{0:T(256)S(1)} copy-done((s32[256]{0:T(256)S(1)}, s32[256]{0:T(256)}, u32[]{:S(2)}) %copy-start.9) | copy-done | bytes 1048
  16.6 0.7 %copy-done.10 = s32[256]{0:T(256)S(1)} copy-done((s32[256]{0:T(256)S(1)}, s32[256]{0:T(256)}, u32[]{:S(2)}) %copy-start.10) | copy-done | bytes 1048
  17.3 0.7 %copy-done.11 = s32[25]{0:T(128)S(1)} copy-done((s32[25]{0:T(128)S(1)}, s32[25]{0:T(128)}, u32[]{:S(2)}) %copy-start.11) | copy-done | bytes 124
  17.9 1.9 %shard_map.149 = (f32[25,512]{1,0:T(8,128)S(1)}, f32[1,64]{1,0:T(1,128)S(1)}, s32[1,240]{1,0:T(1,128)S(1)}, s32[1,160]{1,0:T(1,128)S(1)}, s32[1,240]{1,0:T(1,128)S(1)}) custom-call(s32[8]{0:T(128)S(1)} %copy-done.6, s32[1,25]{1,0:T(1,128)S(1)} %bitcast.21, s32[1,256]{1,0:T(1,128)S(1)} %bitcast.19, s32[1,256]{1,0:T(1,128)S(1)} %bitcast.20, ...), custom_call_target="tpu_custom_call" | custom-call | flops 52428800 | bytes 2097152 | tf_op jit(solution)/shard_map/pallas_call | solution.py:525
  19.8 0.0 collective-permute-done.1.refs_1_
  19.9 0.0 collective-permute-done.2.refs_2_.beyond_ref
  19.9 1.7 %collective-permute-done.3.corner_ref = bf16[2,16,2048]{2,1,0:T(8,128)(2,1)S(1)} collective-permute-done((bf16[2,16,2048]{2,1,0:T(8,128)(2,1)S(1)}, bf16[2,16,2048]{2,1,0:T(8,128)(2,1)S(1)}, u32[]{:S(2)}, u32[]{:S(2)}) %collective-permute-start.3) | collective-permute-done | bytes 131104 | tf_op jit(solution)/shard_map/ppermute | solution.py:508
  21.6 0.0 collective-permute-done.other_ref
  21.7 0.0 collective-permute-done.4.far_ref
  21.7 0.2 shard_map.150.refs_3_
  21.8 0.8 %collective-permute-start.8 = (bf16[64,2048]{1,0:T(8,128)(2,1)S(1)}, bf16[64,2048]{1,0:T(8,128)(2,1)S(1)}, u32[]{:S(2)}, u32[]{:S(2)}) collective-permute-start(bf16[64,2048]{1,0:T(8,128)(2,1)S(1)} %shard_map.150.refs_3_), channel_id=1, source_target_pairs={{0,8},{1,9},{2,10},{3,11},{4,12},{5,13},{6,14},{7,15},{8,0},{9,1},... | collective-permute-start | bytes 786440 | tf_op jit(solution)/shard_map/ppermute | solution.py:508
  22.6 1.8 %collective-permute-start.7 = (bf16[64,2048]{1,0:T(8,128)(2,1)S(1)}, bf16[64,2048]{1,0:T(8,128)(2,1)S(1)}, u32[]{:S(2)}, u32[]{:S(2)}) collective-permute-start(bf16[64,2048]{1,0:T(8,128)(2,1)S(1)} %shard_map.150.refs_3_), channel_id=1, source_target_pairs={{0,6},{1,7},{2,4},{3,5},{4,2},{5,3},{6,0},{7,1},{8,14},{9,15},{10,... | collective-permute-start | bytes 786440 | tf_op jit(solution)/shard_map/ppermute | solution.py:508
  24.4 0.4 collective-permute-start.5
  24.8 1.3 %collective-permute-start.6 = (bf16[64,2048]{1,0:T(8,128)(2,1)S(1)}, bf16[64,2048]{1,0:T(8,128)(2,1)S(1)}, u32[]{:S(2)}, u32[]{:S(2)}) collective-permute-start(bf16[64,2048]{1,0:T(8,128)(2,1)S(1)} %shard_map.150.refs_3_), channel_id=1, source_target_pairs={{0,4},{1,5},{2,6},{3,7},{4,0},{5,1},{6,2},{7,3},{8,12},{9,13},{10,... | collective-permute-start | bytes 786440 | tf_op jit(solution)/shard_map/ppermute | solution.py:508
  26.1 3.2 %collective-permute-done.8.refs_5_ = bf16[64,2048]{1,0:T(8,128)(2,1)S(1)} collective-permute-done((bf16[64,2048]{1,0:T(8,128)(2,1)S(1)}, bf16[64,2048]{1,0:T(8,128)(2,1)S(1)}, u32[]{:S(2)}, u32[]{:S(2)}) %collective-permute-start.8) | collective-permute-done | bytes 262176 | tf_op jit(solution)/shard_map/ppermute | solution.py:508
  29.4 1.5 %collective-permute-start.9 = (bf16[64,2048]{1,0:T(8,128)(2,1)S(1)}, bf16[64,2048]{1,0:T(8,128)(2,1)S(1)}, u32[]{:S(2)}, u32[]{:S(2)}) collective-permute-start(bf16[64,2048]{1,0:T(8,128)(2,1)S(1)} %collective-permute-done.8.refs_5_), channel_id=1, source_target_pairs={{0,2},{1,3},{2,0},{3,1},{4,6},{5,7},{6,4},{7,5},{8,10},{9,11},{10,... | collective-permute-start | bytes 786440 | tf_op jit(solution)/shard_map/ppermute | solution.py:508
  30.9 1.2 %collective-permute-start.10 = (bf16[64,2048]{1,0:T(8,128)(2,1)S(1)}, bf16[64,2048]{1,0:T(8,128)(2,1)S(1)}, u32[]{:S(2)}, u32[]{:S(2)}) collective-permute-start(bf16[64,2048]{1,0:T(8,128)(2,1)S(1)} %collective-permute-done.8.refs_5_), channel_id=1, source_target_pairs={{0,4},{1,5},{2,6},{3,7},{4,0},{5,1},{6,2},{7,3},{8,12},{9,13},{10,... | collective-permute-start | bytes 786440 | tf_op jit(solution)/shard_map/ppermute | solution.py:508
  32.1 0.7 %collective-permute-done.7.refs_4_ = bf16[64,2048]{1,0:T(8,128)(2,1)S(1)} collective-permute-done((bf16[64,2048]{1,0:T(8,128)(2,1)S(1)}, bf16[64,2048]{1,0:T(8,128)(2,1)S(1)}, u32[]{:S(2)}, u32[]{:S(2)}) %collective-permute-start.7) | collective-permute-done | bytes 262176 | tf_op jit(solution)/shard_map/ppermute | solution.py:508
  32.8 1.3 %collective-permute-start.11 = (bf16[64,2048]{1,0:T(8,128)(2,1)S(1)}, bf16[64,2048]{1,0:T(8,128)(2,1)S(1)}, u32[]{:S(2)}, u32[]{:S(2)}) collective-permute-start(bf16[64,2048]{1,0:T(8,128)(2,1)S(1)} %collective-permute-done.7.refs_4_), channel_id=1, source_target_pairs={{0,8},{1,9},{2,10},{3,11},{4,12},{5,13},{6,14},{7,15},{8,0},{9,1},... | collective-permute-start | bytes 786440 | tf_op jit(solution)/shard_map/ppermute | solution.py:508
  34.1 0.0 copy-done
  34.1 2.4 %shard_map.151.first_ref = f32[8,240]{1,0:T(8,128)S(1)} custom-call(s32[1,240]{1,0:T(1,128)S(1)} %get-tuple-element.38.targets_ref, bf16[784,2048]{1,0:T(8,128)(2,1)S(1)} %copy-done, bf16[784,2048]{1,0:T(8,128)(2,1)S(1)} %collective-permute-done.4.far_ref, bf16[2,16,2048]{2,1,0:T(8,128)(2,1)S(1)} %shard_map.148.refs_0_, ...), custom_call_target="tpu_custom_call" | custom-call | flops 1541406720 | bytes 7405568 | tf_op jit(solution)/shard_map/pallas_call | solution.py:274
  36.5 0.4 collective-permute-done.5.refs_2_
  36.8 1.6 %collective-permute-done.6.refs_3_ = bf16[64,2048]{1,0:T(8,128)(2,1)S(1)} collective-permute-done((bf16[64,2048]{1,0:T(8,128)(2,1)S(1)}, bf16[64,2048]{1,0:T(8,128)(2,1)S(1)}, u32[]{:S(2)}, u32[]{:S(2)}) %collective-permute-start.6) | collective-permute-done | bytes 262176 | tf_op jit(solution)/shard_map/ppermute | solution.py:508
  38.5 2.3 %shard_map.152.second_ref = f32[8,160]{1,0:T(8,128)S(1)} custom-call(s32[1,160]{1,0:T(1,128)S(1)} %get-tuple-element.42.targets_ref, bf16[784,2048]{1,0:T(8,128)(2,1)S(1)} %copy-done, bf16[784,2048]{1,0:T(8,128)(2,1)S(1)} %collective-permute-done.4.far_ref, bf16[2,16,2048]{2,1,0:T(8,128)(2,1)S(1)} %shard_map.148.refs_0_, ...), custom_call_target="tpu_custom_call" | custom-call | flops 1027604480 | bytes 7077888 | tf_op jit(solution)/shard_map/pallas_call | solution.py:274
  40.8 0.0 copy-start.7
  40.8 0.0 copy-start.12
  40.8 1.6 %collective-permute-done.9.refs_0_ = bf16[64,2048]{1,0:T(8,128)(2,1)S(1)} collective-permute-done((bf16[64,2048]{1,0:T(8,128)(2,1)S(1)}, bf16[64,2048]{1,0:T(8,128)(2,1)S(1)}, u32[]{:S(2)}, u32[]{:S(2)}) %collective-permute-start.9) | collective-permute-done | bytes 262176 | tf_op jit(solution)/shard_map/ppermute | solution.py:508
  42.4 0.1 collective-permute-done.10.refs_1_
  42.5 0.0 collective-permute-done.11.refs_2_
  42.5 2.6 %shard_map.153 = f32[32,8,128]{2,1,0:T(8,128)S(1)} custom-call(s32[1,240]{1,0:T(1,128)S(1)} %get-tuple-element.35.targets_ref, bf16[784,2048]{1,0:T(8,128)(2,1)S(1)} %copy-done, bf16[784,2048]{1,0:T(8,128)(2,1)S(1)} %collective-permute-done.4.far_ref, f32[8,240]{1,0:T(8,128)S(1)} %shard_map.151.first_ref, f32[8,160]{1,0:T(8,128)S(1)} %shard_map.152.second_ref, ...), custom_call_target="tpu_custom_call" | custom-call | flops 1541406720 | bytes 7405568 | tf_op jit(solution)/shard_map/pallas_call | solution.py:274
  45.1 11.3 %all_to_all.5 = f32[32,8,128]{2,1,0:T(8,128)S(1)} all-to-all(f32[32,8,128]{2,1,0:T(8,128)S(1)} %shard_map.153), channel_id=1, replica_groups=mesh['grp'=8,'vocab'=4] {'grp','vocab'}, dimensions={0} | all-to-all | bytes 262144 | tf_op jit(solution)/shard_map/all_to_all | solution.py:633
  56.4 0.0 copy-done.7
  56.5 1.2 %shard_map.154 = (f32[1,256]{1,0:T(1,128)}, f32[1,256]{1,0:T(1,128)}, f32[1,4]{1,0:T(1,128)}, bf16[25,512]{1,0:T(8,128)(2,1)}) custom-call(s32[1,8]{1,0:T(1,128)S(1)} %bitcast.17, s32[1,8]{1,0:T(1,128)S(1)} %bitcast.22, f32[16,2,8,128]{3,2,1,0:T(8,128)S(1)} %bitcast.12, f32[25,512]{1,0:T(8,128)S(1)} %get-tuple-element.47.turned_ref), custom_call_target="tpu_custom_call" | custom-call | flops 16777216 | bytes 131072 | tf_op jit(solution)/shard_map/pallas_call | solution.py:635
  (11 shorter events, 0.0 us)
Async XLA Ops:
  0.6 1.2 %copy-start.1 = (bf16[256,2048]{1,0:T(8,128)(2,1)S(1)}, bf16[256,2048]{1,0:T(8,128)(2,1)}, u32[]{:S(2)}) copy-start(bf16[256,2048]{1,0:T(8,128)(2,1)} %hidden_ref.3) | copy-start | bytes 3145732
  1.9 0.7 %copy-start.4 = (f32[2048]{0:T(1024)S(1)}, f32[2048]{0:T(1024)}, u32[]{:S(2)}) copy-start(f32[2048]{0:T(1024)} %param.13) | copy-start | bytes 24580
  2.6 31.5 %copy-start = (bf16[784,2048]{1,0:T(8,128)(2,1)S(1)}, bf16[784,2048]{1,0:T(8,128)(2,1)}, u32[]{:S(2)}) copy-start(bf16[784,2048]{1,0:T(8,128)(2,1)} %near_ref.2) | copy-start | bytes 9633796
  3.0 18.7 %collective-permute-start.4 = (bf16[784,2048]{1,0:T(8,128)(2,1)}, bf16[784,2048]{1,0:T(8,128)(2,1)S(1)}, u32[]{:S(2)}, u32[]{:S(2)}) collective-permute-start(bf16[784,2048]{1,0:T(8,128)(2,1)} %near_ref.2), channel_id=1, source_target_pairs={{0,1},{1,0},{2,3},{3,2},{4,5},{5,4},{6,7},{7,6},{8,9},{9,8},{10,11... | collective-permute-start | bytes 9633800 | tf_op jit(solution)/shard_map/ppermute | solution.py:508
  3.5 18.2 %collective-permute-start = (bf16[64,2048]{1,0:T(8,128)(2,1)S(1)}, bf16[64,2048]{1,0:T(8,128)(2,1)S(1)}, u32[]{:S(2)}, u32[]{:S(2)}) collective-permute-start(bf16[64,2048]{1,0:T(8,128)(2,1)S(1)} %shard_map.147.here_ref), channel_id=1, source_target_pairs={{0,16},{1,17},{2,18},{3,19},{4,20},{5,21},{6,22},{7,23},{8,24},{9,... | collective-permute-start | bytes 786440 | tf_op jit(solution)/shard_map/ppermute | solution.py:508
  7.5 12.3 %collective-permute-start.1 = (bf16[2,16,2048]{2,1,0:T(8,128)(2,1)S(1)}, bf16[2,16,2048]{2,1,0:T(8,128)(2,1)S(1)}, u32[]{:S(2)}, u32[]{:S(2)}) collective-permute-start(bf16[2,16,2048]{2,1,0:T(8,128)(2,1)S(1)} %shard_map.148.refs_0_), channel_id=1, source_target_pairs={{0,4},{1,5},{2,6},{3,7},{4,0},{5,1},{6,2},{7,3},{8,12},{9,13},{10,... | collective-permute-start | bytes 393224 | tf_op jit(solution)/shard_map/ppermute | solution.py:508
  9.1 10.8 %collective-permute-start.2 = (bf16[2,16,2048]{2,1,0:T(8,128)(2,1)S(1)}, bf16[2,16,2048]{2,1,0:T(8,128)(2,1)S(1)}, u32[]{:S(2)}, u32[]{:S(2)}) collective-permute-start(bf16[2,16,2048]{2,1,0:T(8,128)(2,1)S(1)} %shard_map.148.refs_0_), channel_id=1, source_target_pairs={{0,8},{1,9},{2,10},{3,11},{4,12},{5,13},{6,14},{7,15},{8,0},{9,1},... | collective-permute-start | bytes 393224 | tf_op jit(solution)/shard_map/ppermute | solution.py:508
  10.7 11.0 %collective-permute-start.3 = (bf16[2,16,2048]{2,1,0:T(8,128)(2,1)S(1)}, bf16[2,16,2048]{2,1,0:T(8,128)(2,1)S(1)}, u32[]{:S(2)}, u32[]{:S(2)}) collective-permute-start(bf16[2,16,2048]{2,1,0:T(8,128)(2,1)S(1)} %shard_map.148.refs_0_), channel_id=1, source_target_pairs={{0,12},{1,13},{2,14},{3,15},{4,8},{5,9},{6,10},{7,11},{8,4},{9,5},... | collective-permute-start | bytes 393224 | tf_op jit(solution)/shard_map/ppermute | solution.py:508
  11.1 1.6 %copy-start.2 = (bf16[2048,512]{1,0:T(8,128)(2,1)S(1)}, bf16[2048,512]{1,0:T(8,128)(2,1)}, u32[]{:S(2)}) copy-start(bf16[2048,512]{1,0:T(8,128)(2,1)} %weight_hbm.1) | copy-start | bytes 6291460
  12.7 1.2 %copy-start.3 = (bf16[256,2048]{1,0:T(8,128)(2,1)S(1)}, bf16[256,2048]{1,0:T(8,128)(2,1)}, u32[]{:S(2)}) copy-start(bf16[256,2048]{1,0:T(8,128)(2,1)} %input_hbm.1) | copy-start | bytes 3145732
  13.9 0.7 %copy-start.5 = (s32[2048]{0:T(1024)S(1)}, s32[2048]{0:T(1024)}, u32[]{:S(2)}) copy-start(s32[2048]{0:T(1024)} %param.15) | copy-start | bytes 24580
  14.6 0.7 %copy-start.6 = (s32[8]{0:T(128)S(1)}, s32[8]{0:T(128)}, u32[]{:S(2)}) copy-start(s32[8]{0:T(128)} %lengths_ref.1) | copy-start | bytes 100
  15.2 0.7 %copy-start.8 = (f32[512]{0:T(512)S(1)}, f32[512]{0:T(512)}, u32[]{:S(2)}) copy-start(f32[512]{0:T(512)} %param.21) | copy-start | bytes 6148
  15.9 0.7 %copy-start.9 = (s32[256]{0:T(256)S(1)}, s32[256]{0:T(256)}, u32[]{:S(2)}) copy-start(s32[256]{0:T(256)} %param.22) | copy-start | bytes 3076
  16.6 0.7 %copy-start.10 = (s32[256]{0:T(256)S(1)}, s32[256]{0:T(256)}, u32[]{:S(2)}) copy-start(s32[256]{0:T(256)} %param.17) | copy-start | bytes 3076
  17.3 0.7 %copy-start.11 = (s32[25]{0:T(128)S(1)}, s32[25]{0:T(128)}, u32[]{:S(2)}) copy-start(s32[25]{0:T(128)} %param.23) | copy-start | bytes 304
  21.8 7.6 %collective-permute-start.8 = (bf16[64,2048]{1,0:T(8,128)(2,1)S(1)}, bf16[64,2048]{1,0:T(8,128)(2,1)S(1)}, u32[]{:S(2)}, u32[]{:S(2)}) collective-permute-start(bf16[64,2048]{1,0:T(8,128)(2,1)S(1)} %shard_map.150.refs_3_), channel_id=1, source_target_pairs={{0,8},{1,9},{2,10},{3,11},{4,12},{5,13},{6,14},{7,15},{8,0},{9,1},... | collective-permute-start | bytes 786440 | tf_op jit(solution)/shard_map/ppermute | solution.py:508
  22.6 10.2 %collective-permute-start.7 = (bf16[64,2048]{1,0:T(8,128)(2,1)S(1)}, bf16[64,2048]{1,0:T(8,128)(2,1)S(1)}, u32[]{:S(2)}, u32[]{:S(2)}) collective-permute-start(bf16[64,2048]{1,0:T(8,128)(2,1)S(1)} %shard_map.150.refs_3_), channel_id=1, source_target_pairs={{0,6},{1,7},{2,4},{3,5},{4,2},{5,3},{6,0},{7,1},{8,14},{9,15},{10,... | collective-permute-start | bytes 786440 | tf_op jit(solution)/shard_map/ppermute | solution.py:508
  24.4 12.4 %collective-permute-start.5 = (bf16[64,2048]{1,0:T(8,128)(2,1)S(1)}, bf16[64,2048]{1,0:T(8,128)(2,1)S(1)}, u32[]{:S(2)}, u32[]{:S(2)}) collective-permute-start(bf16[64,2048]{1,0:T(8,128)(2,1)S(1)} %shard_map.150.refs_3_), channel_id=1, source_target_pairs={{0,2},{1,3},{2,0},{3,1},{4,6},{5,7},{6,4},{7,5},{8,10},{9,11},{10,... | collective-permute-start | bytes 786440 | tf_op jit(solution)/shard_map/ppermute | solution.py:508
  24.8 13.6 %collective-permute-start.6 = (bf16[64,2048]{1,0:T(8,128)(2,1)S(1)}, bf16[64,2048]{1,0:T(8,128)(2,1)S(1)}, u32[]{:S(2)}, u32[]{:S(2)}) collective-permute-start(bf16[64,2048]{1,0:T(8,128)(2,1)S(1)} %shard_map.150.refs_3_), channel_id=1, source_target_pairs={{0,4},{1,5},{2,6},{3,7},{4,0},{5,1},{6,2},{7,3},{8,12},{9,13},{10,... | collective-permute-start | bytes 786440 | tf_op jit(solution)/shard_map/ppermute | solution.py:508
  29.4 13.0 %collective-permute-start.9 = (bf16[64,2048]{1,0:T(8,128)(2,1)S(1)}, bf16[64,2048]{1,0:T(8,128)(2,1)S(1)}, u32[]{:S(2)}, u32[]{:S(2)}) collective-permute-start(bf16[64,2048]{1,0:T(8,128)(2,1)S(1)} %collective-permute-done.8.refs_5_), channel_id=1, source_target_pairs={{0,2},{1,3},{2,0},{3,1},{4,6},{5,7},{6,4},{7,5},{8,10},{9,11},{10,... | collective-permute-start | bytes 786440 | tf_op jit(solution)/shard_map/ppermute | solution.py:508
  30.9 11.6 %collective-permute-start.10 = (bf16[64,2048]{1,0:T(8,128)(2,1)S(1)}, bf16[64,2048]{1,0:T(8,128)(2,1)S(1)}, u32[]{:S(2)}, u32[]{:S(2)}) collective-permute-start(bf16[64,2048]{1,0:T(8,128)(2,1)S(1)} %collective-permute-done.8.refs_5_), channel_id=1, source_target_pairs={{0,4},{1,5},{2,6},{3,7},{4,0},{5,1},{6,2},{7,3},{8,12},{9,13},{10,... | collective-permute-start | bytes 786440 | tf_op jit(solution)/shard_map/ppermute | solution.py:508
  32.8 9.6 %collective-permute-start.11 = (bf16[64,2048]{1,0:T(8,128)(2,1)S(1)}, bf16[64,2048]{1,0:T(8,128)(2,1)S(1)}, u32[]{:S(2)}, u32[]{:S(2)}) collective-permute-start(bf16[64,2048]{1,0:T(8,128)(2,1)S(1)} %collective-permute-done.7.refs_4_), channel_id=1, source_target_pairs={{0,8},{1,9},{2,10},{3,11},{4,12},{5,13},{6,14},{7,15},{8,0},{9,1},... | collective-permute-start | bytes 786440 | tf_op jit(solution)/shard_map/ppermute | solution.py:508
  40.8 15.7 %copy-start.7 = (s32[8]{0:T(128)S(1)}, s32[8]{0:T(128)}, u32[]{:S(2)}) copy-start(s32[8]{0:T(128)} %lengths_ref.1) | copy-start | bytes 100
  40.8 15.7 %copy-start.12 = (s32[8]{0:T(128)S(1)}, s32[8]{0:T(128)}, u32[]{:S(2)}) copy-start(s32[8]{0:T(128)} %param.18) | copy-start | bytes 100

commit v7 on v6

--- a/solution.py
+++ b/solution.py
@@ -266,7 +266,7 @@
         for group in range(groups):
             if group % (groups // 2) // 2 == which:
                 for shard in range(shards):
-                    out_ref[group * shards + shard] = block
+                    out_ref[shard * groups + group] = block
 
 
 def score(kernel, out_shape, targets, heads, extras, count, scratch=True):
@@ -396,7 +396,9 @@
     cap = logprob_ref.shape[1]
     size = 2 * BAL // shards
     tokens = 2 * parts * size
-    columns = [merged(got_ref[:, core]) for core in range(CORES)]
+    columns = [
+        merged(jnp.concatenate([got_ref[part, core] for part in range(parts)], axis=0)) for core in range(CORES)
+    ]
 
     column, span = lax.rem(group, 2), tokens // 2
     halves = [[both[:, :span], both[:, span:]] for both in columns]
@@ -420,7 +422,7 @@
     found = jnp.dot(terms, pick, preferred_element_type=jnp.float32)
     found = found[0:4] + found[4:8] + found[8:12]
     def summed(who, logprob):
-        note = got_ref[who * parts, 0][7:8, LANES // 2 :]
+        note = got_ref[0, 0, who][7:8, LANES // 2 :]
         breaks = [note[:, BREAKS + i : BREAKS + i + 1].astype(jnp.int32) for i in range(1, SEGS)]
         live = slots < chosen(lengths_ref, who)
         logprob = jnp.where(live, logprob, 0.0)
@@ -464,7 +466,7 @@
     squares = jnp.zeros((1, count), jnp.float32)
     for part in range(parts):
         for core in range(CORES):
-            squares += got_ref[group * parts + part, core][7:8, LANES // 2 : LANES // 2 + count]
+            squares += got_ref[part, core, group][7:8, LANES // 2 : LANES // 2 + count]
     squares = upright(squares)
     scale = jnp.sqrt(squares / (width * shards) + NORM_EPS)
     keys_ref[...] = (turned_ref[...] / scale).astype(jnp.bfloat16)
@@ -628,9 +630,9 @@
         extra = jnp.broadcast_to(extra, (sets, LANES // 2))
         stats = packed(state, extra).reshape(8, sets, LANES).transpose(1, 0, 2)
         sent = jnp.broadcast_to(
-            stats[None, :, None, None], (2, sets, 2, shards, 8, LANES)
+            stats[None, None, :, None], (shards, 2, sets, 2, 8, LANES)
         ).reshape(sent_shape.shape)
-    got = lax.all_to_all(sent, axes, 0, 0, tiled=False)
+    got = lax.all_to_all(sent, ("vocab", "grp"), 0, 0, tiled=False)
 
     logprob, entropy, means, keys = call(
         functools.partial(final_kernel, sizes),
@@ -646,7 +648,7 @@
     )(
         group_lengths.reshape(1, groups),
         continues.reshape(1, groups),
-        got.reshape(groups * parts, CORES, 8, LANES),
+        got.reshape(parts, CORES, groups, 8, LANES),
         turned,
     )
     return logprob.reshape(cap), entropy.reshape(cap), means.reshape(SEGS), keys

time: 58.1 us -> 57.6 us (level)
  no operation moved by 1% of the time
where the time goes in v7:
time: 57.6 us; the launch traced here: 57.2 us
  starting transfers between devices  16.1 us (28%)
  Pallas kernels  11.3 us (20%)
  blocking collectives  10.8 us (19%)
  waiting for transfers between devices  9.41 us (16%)
  local copies, waits for them, and re-layouts  8.79 us (15%)
  between operations  0.74 us (1%)
    ppermute x12, starting transfers between devices, swap(): return lax.ppermute(array, axes, partners(sizes, (group_flip, shard_flip)))  16.1 us
    all_to_all x1, blocking collectives, local(): got = lax.all_to_all(sent, ('vocab', 'grp'), 0, 0, tiled=False)  10.8 us
    ppermute x12, waiting for transfers between devices, swap(): return lax.ppermute(array, axes, partners(sizes, (group_flip, shard_flip)))  9.41 us
    unnamed x26, local copies, waits for them, and re-layouts  8.79 us
    pallas_call x3, Pallas kernels, score(): call(kernel, out_shape, [WHOLE] * (3 + len(extras)), 4 * vocab * count *...  7.32 us
    pallas_call x1, Pallas kernels, local(): call(functools.partial(side_kernel, sizes, swapped), (jax.ShapeDtypeStruc...  1.9 us
    pallas_call x1, Pallas kernels, local(): call(functools.partial(final_kernel, sizes), (jax.ShapeDtypeStruct((1, ca...  1.19 us
  transfers between devices with their start and end apart: 12, of which 7 were waited for; matrix products, arithmetic and copies ran while one was open for 0% of the time, Pallas kernels for 12%

profile of v7, /device:TPU:0, one launch (start us, length us, event | category | flops | bytes accessed | tf_op | source)
XLA Modules:
  0.0 57.2 jit_solution(7225387799221591954)
XLA Ops:
  0.6 0.0 copy-start.1
  0.6 1.2 %copy-done.1 = bf16[256,2048]{1,0:T(8,128)(2,1)S(1)} copy-done((bf16[256,2048]{1,0:T(8,128)(2,1)S(1)}, bf16[256,2048]{1,0:T(8,128)(2,1)}, u32[]{:S(2)}) %copy-start.1) | copy-done | bytes 1048600
  1.9 0.7 %copy-done.4 = f32[2048]{0:T(1024)S(1)} copy-done((f32[2048]{0:T(1024)S(1)}, f32[2048]{0:T(1024)}, u32[]{:S(2)}) %copy-start.4) | copy-done | bytes 8216
  2.6 0.4 shard_map.147.here_ref
  3.0 0.5 collective-permute-start.4
  3.5 3.7 %collective-permute-start = (bf16[64,2048]{1,0:T(8,128)(2,1)S(1)}, bf16[64,2048]{1,0:T(8,128)(2,1)S(1)}, u32[]{:S(2)}, u32[]{:S(2)}) collective-permute-start(bf16[64,2048]{1,0:T(8,128)(2,1)S(1)} %shard_map.147.here_ref), channel_id=1, source_target_pairs={{0,16},{1,17},{2,18},{3,19},{4,20},{5,21},{6,22},{7,23},{8,24},{9,... | collective-permute-start | bytes 786440 | tf_op jit(solution)/shard_map/ppermute | solution.py:510
  7.2 0.3 shard_map.148.refs_0_
  7.5 1.6 %collective-permute-start.1 = (bf16[2,16,2048]{2,1,0:T(8,128)(2,1)S(1)}, bf16[2,16,2048]{2,1,0:T(8,128)(2,1)S(1)}, u32[]{:S(2)}, u32[]{:S(2)}) collective-permute-start(bf16[2,16,2048]{2,1,0:T(8,128)(2,1)S(1)} %shard_map.148.refs_0_), channel_id=1, source_target_pairs={{0,4},{1,5},{2,6},{3,7},{4,0},{5,1},{6,2},{7,3},{8,12},{9,13},{10,... | collective-permute-start | bytes 393224 | tf_op jit(solution)/shard_map/ppermute | solution.py:510
  9.1 1.6 %collective-permute-start.2 = (bf16[2,16,2048]{2,1,0:T(8,128)(2,1)S(1)}, bf16[2,16,2048]{2,1,0:T(8,128)(2,1)S(1)}, u32[]{:S(2)}, u32[]{:S(2)}) collective-permute-start(bf16[2,16,2048]{2,1,0:T(8,128)(2,1)S(1)} %shard_map.148.refs_0_), channel_id=1, source_target_pairs={{0,8},{1,9},{2,10},{3,11},{4,12},{5,13},{6,14},{7,15},{8,0},{9,1},... | collective-permute-start | bytes 393224 | tf_op jit(solution)/shard_map/ppermute | solution.py:510
  10.7 0.4 collective-permute-start.3
  11.1 1.6 %copy-done.2 = bf16[2048,512]{1,0:T(8,128)(2,1)S(1)} copy-done((bf16[2048,512]{1,0:T(8,128)(2,1)S(1)}, bf16[2048,512]{1,0:T(8,128)(2,1)}, u32[]{:S(2)}) %copy-start.2) | copy-done | bytes 2097176
  12.7 1.2 %copy-done.3 = bf16[256,2048]{1,0:T(8,128)(2,1)S(1)} copy-done((bf16[256,2048]{1,0:T(8,128)(2,1)S(1)}, bf16[256,2048]{1,0:T(8,128)(2,1)}, u32[]{:S(2)}) %copy-start.3) | copy-done | bytes 1048600
  13.9 0.7 %copy-done.5 = s32[2048]{0:T(1024)S(1)} copy-done((s32[2048]{0:T(1024)S(1)}, s32[2048]{0:T(1024)}, u32[]{:S(2)}) %copy-start.5) | copy-done | bytes 8216
  14.6 0.7 %copy-done.6 = s32[8]{0:T(128)S(1)} copy-done((s32[8]{0:T(128)S(1)}, s32[8]{0:T(128)}, u32[]{:S(2)}) %copy-start.6) | copy-done | bytes 56
  15.2 0.7 %copy-done.8 = f32[512]{0:T(512)S(1)} copy-done((f32[512]{0:T(512)S(1)}, f32[512]{0:T(512)}, u32[]{:S(2)}) %copy-start.8) | copy-done | bytes 2072
  15.9 0.7 %copy-done.9 = s32[256]{0:T(256)S(1)} copy-done((s32[256]{0:T(256)S(1)}, s32[256]{0:T(256)}, u32[]{:S(2)}) %copy-start.9) | copy-done | bytes 1048
  16.6 0.7 %copy-done.10 = s32[256]{0:T(256)S(1)} copy-done((s32[256]{0:T(256)S(1)}, s32[256]{0:T(256)}, u32[]{:S(2)}) %copy-start.10) | copy-done | bytes 1048
  17.3 0.7 %copy-done.11 = s32[25]{0:T(128)S(1)} copy-done((s32[25]{0:T(128)S(1)}, s32[25]{0:T(128)}, u32[]{:S(2)}) %copy-start.11) | copy-done | bytes 124
  17.9 1.9 %shard_map.149 = (f32[25,512]{1,0:T(8,128)S(1)}, f32[1,64]{1,0:T(1,128)S(1)}, s32[1,240]{1,0:T(1,128)S(1)}, s32[1,160]{1,0:T(1,128)S(1)}, s32[1,240]{1,0:T(1,128)S(1)}) custom-call(s32[8]{0:T(128)S(1)} %copy-done.6, s32[1,25]{1,0:T(1,128)S(1)} %bitcast.21, s32[1,256]{1,0:T(1,128)S(1)} %bitcast.19, s32[1,256]{1,0:T(1,128)S(1)} %bitcast.20, ...), custom_call_target="tpu_custom_call" | custom-call | flops 52428800 | bytes 2097152 | tf_op jit(solution)/shard_map/pallas_call | solution.py:527
  19.8 0.0 collective-permute-done.1.refs_1_
  19.9 0.0 collective-permute-done.2.refs_2_.beyond_ref
  19.9 1.7 %collective-permute-done.3.corner_ref = bf16[2,16,2048]{2,1,0:T(8,128)(2,1)S(1)} collective-permute-done((bf16[2,16,2048]{2,1,0:T(8,128)(2,1)S(1)}, bf16[2,16,2048]{2,1,0:T(8,128)(2,1)S(1)}, u32[]{:S(2)}, u32[]{:S(2)}) %collective-permute-start.3) | collective-permute-done | bytes 131104 | tf_op jit(solution)/shard_map/ppermute | solution.py:510
  21.6 0.0 collective-permute-done.other_ref
  21.7 0.0 collective-permute-done.4.far_ref
  21.7 0.2 shard_map.150.refs_3_
  21.8 0.8 %collective-permute-start.8 = (bf16[64,2048]{1,0:T(8,128)(2,1)S(1)}, bf16[64,2048]{1,0:T(8,128)(2,1)S(1)}, u32[]{:S(2)}, u32[]{:S(2)}) collective-permute-start(bf16[64,2048]{1,0:T(8,128)(2,1)S(1)} %shard_map.150.refs_3_), channel_id=1, source_target_pairs={{0,8},{1,9},{2,10},{3,11},{4,12},{5,13},{6,14},{7,15},{8,0},{9,1},... | collective-permute-start | bytes 786440 | tf_op jit(solution)/shard_map/ppermute | solution.py:510
  22.6 1.8 %collective-permute-start.7 = (bf16[64,2048]{1,0:T(8,128)(2,1)S(1)}, bf16[64,2048]{1,0:T(8,128)(2,1)S(1)}, u32[]{:S(2)}, u32[]{:S(2)}) collective-permute-start(bf16[64,2048]{1,0:T(8,128)(2,1)S(1)} %shard_map.150.refs_3_), channel_id=1, source_target_pairs={{0,6},{1,7},{2,4},{3,5},{4,2},{5,3},{6,0},{7,1},{8,14},{9,15},{10,... | collective-permute-start | bytes 786440 | tf_op jit(solution)/shard_map/ppermute | solution.py:510
  24.4 0.4 collective-permute-start.5
  24.8 1.3 %collective-permute-start.6 = (bf16[64,2048]{1,0:T(8,128)(2,1)S(1)}, bf16[64,2048]{1,0:T(8,128)(2,1)S(1)}, u32[]{:S(2)}, u32[]{:S(2)}) collective-permute-start(bf16[64,2048]{1,0:T(8,128)(2,1)S(1)} %shard_map.150.refs_3_), channel_id=1, source_target_pairs={{0,4},{1,5},{2,6},{3,7},{4,0},{5,1},{6,2},{7,3},{8,12},{9,13},{10,... | collective-permute-start | bytes 786440 | tf_op jit(solution)/shard_map/ppermute | solution.py:510
  26.1 3.2 %collective-permute-done.8.refs_5_ = bf16[64,2048]{1,0:T(8,128)(2,1)S(1)} collective-permute-done((bf16[64,2048]{1,0:T(8,128)(2,1)S(1)}, bf16[64,2048]{1,0:T(8,128)(2,1)S(1)}, u32[]{:S(2)}, u32[]{:S(2)}) %collective-permute-start.8) | collective-permute-done | bytes 262176 | tf_op jit(solution)/shard_map/ppermute | solution.py:510
  29.4 1.5 %collective-permute-start.9 = (bf16[64,2048]{1,0:T(8,128)(2,1)S(1)}, bf16[64,2048]{1,0:T(8,128)(2,1)S(1)}, u32[]{:S(2)}, u32[]{:S(2)}) collective-permute-start(bf16[64,2048]{1,0:T(8,128)(2,1)S(1)} %collective-permute-done.8.refs_5_), channel_id=1, source_target_pairs={{0,2},{1,3},{2,0},{3,1},{4,6},{5,7},{6,4},{7,5},{8,10},{9,11},{10,... | collective-permute-start | bytes 786440 | tf_op jit(solution)/shard_map/ppermute | solution.py:510
  30.9 1.2 %collective-permute-start.10 = (bf16[64,2048]{1,0:T(8,128)(2,1)S(1)}, bf16[64,2048]{1,0:T(8,128)(2,1)S(1)}, u32[]{:S(2)}, u32[]{:S(2)}) collective-permute-start(bf16[64,2048]{1,0:T(8,128)(2,1)S(1)} %collective-permute-done.8.refs_5_), channel_id=1, source_target_pairs={{0,4},{1,5},{2,6},{3,7},{4,0},{5,1},{6,2},{7,3},{8,12},{9,13},{10,... | collective-permute-start | bytes 786440 | tf_op jit(solution)/shard_map/ppermute | solution.py:510
  32.1 0.7 %collective-permute-done.7.refs_4_ = bf16[64,2048]{1,0:T(8,128)(2,1)S(1)} collective-permute-done((bf16[64,2048]{1,0:T(8,128)(2,1)S(1)}, bf16[64,2048]{1,0:T(8,128)(2,1)S(1)}, u32[]{:S(2)}, u32[]{:S(2)}) %collective-permute-start.7) | collective-permute-done | bytes 262176 | tf_op jit(solution)/shard_map/ppermute | solution.py:510
  32.8 1.3 %collective-permute-start.11 = (bf16[64,2048]{1,0:T(8,128)(2,1)S(1)}, bf16[64,2048]{1,0:T(8,128)(2,1)S(1)}, u32[]{:S(2)}, u32[]{:S(2)}) collective-permute-start(bf16[64,2048]{1,0:T(8,128)(2,1)S(1)} %collective-permute-done.7.refs_4_), channel_id=1, source_target_pairs={{0,8},{1,9},{2,10},{3,11},{4,12},{5,13},{6,14},{7,15},{8,0},{9,1},... | collective-permute-start | bytes 786440 | tf_op jit(solution)/shard_map/ppermute | solution.py:510
  34.1 0.0 copy-done
  34.1 2.4 %shard_map.151.first_ref = f32[8,240]{1,0:T(8,128)S(1)} custom-call(s32[1,240]{1,0:T(1,128)S(1)} %get-tuple-element.38.targets_ref, bf16[784,2048]{1,0:T(8,128)(2,1)S(1)} %copy-done, bf16[784,2048]{1,0:T(8,128)(2,1)S(1)} %collective-permute-done.4.far_ref, bf16[2,16,2048]{2,1,0:T(8,128)(2,1)S(1)} %shard_map.148.refs_0_, ...), custom_call_target="tpu_custom_call" | custom-call | flops 1541406720 | bytes 7405568 | tf_op jit(solution)/shard_map/pallas_call | solution.py:274
  36.5 0.4 collective-permute-done.5.refs_2_
  36.8 1.6 %collective-permute-done.6.refs_3_ = bf16[64,2048]{1,0:T(8,128)(2,1)S(1)} collective-permute-done((bf16[64,2048]{1,0:T(8,128)(2,1)S(1)}, bf16[64,2048]{1,0:T(8,128)(2,1)S(1)}, u32[]{:S(2)}, u32[]{:S(2)}) %collective-permute-start.6) | collective-permute-done | bytes 262176 | tf_op jit(solution)/shard_map/ppermute | solution.py:510
  38.5 2.3 %shard_map.152.second_ref = f32[8,160]{1,0:T(8,128)S(1)} custom-call(s32[1,160]{1,0:T(1,128)S(1)} %get-tuple-element.42.targets_ref, bf16[784,2048]{1,0:T(8,128)(2,1)S(1)} %copy-done, bf16[784,2048]{1,0:T(8,128)(2,1)S(1)} %collective-permute-done.4.far_ref, bf16[2,16,2048]{2,1,0:T(8,128)(2,1)S(1)} %shard_map.148.refs_0_, ...), custom_call_target="tpu_custom_call" | custom-call | flops 1027604480 | bytes 7077888 | tf_op jit(solution)/shard_map/pallas_call | solution.py:274
  40.8 0.0 copy-start.7
  40.8 0.0 copy-start.12
  40.8 1.6 %collective-permute-done.9.refs_0_ = bf16[64,2048]{1,0:T(8,128)(2,1)S(1)} collective-permute-done((bf16[64,2048]{1,0:T(8,128)(2,1)S(1)}, bf16[64,2048]{1,0:T(8,128)(2,1)S(1)}, u32[]{:S(2)}, u32[]{:S(2)}) %collective-permute-start.9) | collective-permute-done | bytes 262176 | tf_op jit(solution)/shard_map/ppermute | solution.py:510
  42.4 0.1 collective-permute-done.10.refs_1_
  42.5 0.0 collective-permute-done.11.refs_2_
  42.5 2.6 %shard_map.153 = f32[32,8,128]{2,1,0:T(8,128)S(1)} custom-call(s32[1,240]{1,0:T(1,128)S(1)} %get-tuple-element.35.targets_ref, bf16[784,2048]{1,0:T(8,128)(2,1)S(1)} %copy-done, bf16[784,2048]{1,0:T(8,128)(2,1)S(1)} %collective-permute-done.4.far_ref, f32[8,240]{1,0:T(8,128)S(1)} %shard_map.151.first_ref, f32[8,160]{1,0:T(8,128)S(1)} %shard_map.152.second_ref, ...), custom_call_target="tpu_custom_call" | custom-call | flops 1541406720 | bytes 7405568 | tf_op jit(solution)/shard_map/pallas_call | solution.py:274
  45.1 10.8 %all_to_all.5 = f32[32,8,128]{2,1,0:T(8,128)S(1)} all-to-all(f32[32,8,128]{2,1,0:T(8,128)S(1)} %shard_map.153), channel_id=1, replica_groups=mesh['grp'=8,'vocab'=4] {'vocab','grp'}, dimensions={0} | all-to-all | bytes 262144 | tf_op jit(solution)/shard_map/all_to_all | solution.py:635
  56.0 0.0 copy-done.7
  56.0 1.2 %shard_map.154 = (f32[1,256]{1,0:T(1,128)}, f32[1,256]{1,0:T(1,128)}, f32[1,4]{1,0:T(1,128)}, bf16[25,512]{1,0:T(8,128)(2,1)}) custom-call(s32[1,8]{1,0:T(1,128)S(1)} %bitcast.17, s32[1,8]{1,0:T(1,128)S(1)} %bitcast.22, f32[2,2,8,8,128]{4,3,2,1,0:T(8,128)S(1)} %bitcast.12, f32[25,512]{1,0:T(8,128)S(1)} %get-tuple-element.47.turned_ref), custom_call_target="tpu_custom_call" | custom-call | flops 16777216 | bytes 131072 | tf_op jit(solution)/shard_map/pallas_call | solution.py:637
  (11 shorter events, 0.0 us)
Async XLA Ops:
  0.6 1.2 %copy-start.1 = (bf16[256,2048]{1,0:T(8,128)(2,1)S(1)}, bf16[256,2048]{1,0:T(8,128)(2,1)}, u32[]{:S(2)}) copy-start(bf16[256,2048]{1,0:T(8,128)(2,1)} %hidden_ref.3) | copy-start | bytes 3145732
  1.9 0.7 %copy-start.4 = (f32[2048]{0:T(1024)S(1)}, f32[2048]{0:T(1024)}, u32[]{:S(2)}) copy-start(f32[2048]{0:T(1024)} %param.13) | copy-start | bytes 24580
  2.6 31.5 %copy-start = (bf16[784,2048]{1,0:T(8,128)(2,1)S(1)}, bf16[784,2048]{1,0:T(8,128)(2,1)}, u32[]{:S(2)}) copy-start(bf16[784,2048]{1,0:T(8,128)(2,1)} %near_ref.2) | copy-start | bytes 9633796
  3.0 18.7 %collective-permute-start.4 = (bf16[784,2048]{1,0:T(8,128)(2,1)}, bf16[784,2048]{1,0:T(8,128)(2,1)S(1)}, u32[]{:S(2)}, u32[]{:S(2)}) collective-permute-start(bf16[784,2048]{1,0:T(8,128)(2,1)} %near_ref.2), channel_id=1, source_target_pairs={{0,1},{1,0},{2,3},{3,2},{4,5},{5,4},{6,7},{7,6},{8,9},{9,8},{10,11... | collective-permute-start | bytes 9633800 | tf_op jit(solution)/shard_map/ppermute | solution.py:510
  3.5 18.2 %collective-permute-start = (bf16[64,2048]{1,0:T(8,128)(2,1)S(1)}, bf16[64,2048]{1,0:T(8,128)(2,1)S(1)}, u32[]{:S(2)}, u32[]{:S(2)}) collective-permute-start(bf16[64,2048]{1,0:T(8,128)(2,1)S(1)} %shard_map.147.here_ref), channel_id=1, source_target_pairs={{0,16},{1,17},{2,18},{3,19},{4,20},{5,21},{6,22},{7,23},{8,24},{9,... | collective-permute-start | bytes 786440 | tf_op jit(solution)/shard_map/ppermute | solution.py:510
  7.5 12.3 %collective-permute-start.1 = (bf16[2,16,2048]{2,1,0:T(8,128)(2,1)S(1)}, bf16[2,16,2048]{2,1,0:T(8,128)(2,1)S(1)}, u32[]{:S(2)}, u32[]{:S(2)}) collective-permute-start(bf16[2,16,2048]{2,1,0:T(8,128)(2,1)S(1)} %shard_map.148.refs_0_), channel_id=1, source_target_pairs={{0,4},{1,5},{2,6},{3,7},{4,0},{5,1},{6,2},{7,3},{8,12},{9,13},{10,... | collective-permute-start | bytes 393224 | tf_op jit(solution)/shard_map/ppermute | solution.py:510
  9.1 10.8 %collective-permute-start.2 = (bf16[2,16,2048]{2,1,0:T(8,128)(2,1)S(1)}, bf16[2,16,2048]{2,1,0:T(8,128)(2,1)S(1)}, u32[]{:S(2)}, u32[]{:S(2)}) collective-permute-start(bf16[2,16,2048]{2,1,0:T(8,128)(2,1)S(1)} %shard_map.148.refs_0_), channel_id=1, source_target_pairs={{0,8},{1,9},{2,10},{3,11},{4,12},{5,13},{6,14},{7,15},{8,0},{9,1},... | collective-permute-start | bytes 393224 | tf_op jit(solution)/shard_map/ppermute | solution.py:510
  10.7 11.0 %collective-permute-start.3 = (bf16[2,16,2048]{2,1,0:T(8,128)(2,1)S(1)}, bf16[2,16,2048]{2,1,0:T(8,128)(2,1)S(1)}, u32[]{:S(2)}, u32[]{:S(2)}) collective-permute-start(bf16[2,16,2048]{2,1,0:T(8,128)(2,1)S(1)} %shard_map.148.refs_0_), channel_id=1, source_target_pairs={{0,12},{1,13},{2,14},{3,15},{4,8},{5,9},{6,10},{7,11},{8,4},{9,5},... | collective-permute-start | bytes 393224 | tf_op jit(solution)/shard_map/ppermute | solution.py:510
  11.1 1.6 %copy-start.2 = (bf16[2048,512]{1,0:T(8,128)(2,1)S(1)}, bf16[2048,512]{1,0:T(8,128)(2,1)}, u32[]{:S(2)}) copy-start(bf16[2048,512]{1,0:T(8,128)(2,1)} %weight_hbm.1) | copy-start | bytes 6291460
  12.7 1.2 %copy-start.3 = (bf16[256,2048]{1,0:T(8,128)(2,1)S(1)}, bf16[256,2048]{1,0:T(8,128)(2,1)}, u32[]{:S(2)}) copy-start(bf16[256,2048]{1,0:T(8,128)(2,1)} %input_hbm.1) | copy-start | bytes 3145732
  13.9 0.7 %copy-start.5 = (s32[2048]{0:T(1024)S(1)}, s32[2048]{0:T(1024)}, u32[]{:S(2)}) copy-start(s32[2048]{0:T(1024)} %param.15) | copy-start | bytes 24580
  14.6 0.7 %copy-start.6 = (s32[8]{0:T(128)S(1)}, s32[8]{0:T(128)}, u32[]{:S(2)}) copy-start(s32[8]{0:T(128)} %lengths_ref.1) | copy-start | bytes 100
  15.2 0.7 %copy-start.8 = (f32[512]{0:T(512)S(1)}, f32[512]{0:T(512)}, u32[]{:S(2)}) copy-start(f32[512]{0:T(512)} %param.21) | copy-start | bytes 6148
  15.9 0.7 %copy-start.9 = (s32[256]{0:T(256)S(1)}, s32[256]{0:T(256)}, u32[]{:S(2)}) copy-start(s32[256]{0:T(256)} %param.22) | copy-start | bytes 3076
  16.6 0.7 %copy-start.10 = (s32[256]{0:T(256)S(1)}, s32[256]{0:T(256)}, u32[]{:S(2)}) copy-start(s32[256]{0:T(256)} %param.17) | copy-start | bytes 3076
  17.3 0.7 %copy-start.11 = (s32[25]{0:T(128)S(1)}, s32[25]{0:T(128)}, u32[]{:S(2)}) copy-start(s32[25]{0:T(128)} %param.23) | copy-start | bytes 304
  21.8 7.6 %collective-permute-start.8 = (bf16[64,2048]{1,0:T(8,128)(2,1)S(1)}, bf16[64,2048]{1,0:T(8,128)(2,1)S(1)}, u32[]{:S(2)}, u32[]{:S(2)}) collective-permute-start(bf16[64,2048]{1,0:T(8,128)(2,1)S(1)} %shard_map.150.refs_3_), channel_id=1, source_target_pairs={{0,8},{1,9},{2,10},{3,11},{4,12},{5,13},{6,14},{7,15},{8,0},{9,1},... | collective-permute-start | bytes 786440 | tf_op jit(solution)/shard_map/ppermute | solution.py:510
  22.6 10.2 %collective-permute-start.7 = (bf16[64,2048]{1,0:T(8,128)(2,1)S(1)}, bf16[64,2048]{1,0:T(8,128)(2,1)S(1)}, u32[]{:S(2)}, u32[]{:S(2)}) collective-permute-start(bf16[64,2048]{1,0:T(8,128)(2,1)S(1)} %shard_map.150.refs_3_), channel_id=1, source_target_pairs={{0,6},{1,7},{2,4},{3,5},{4,2},{5,3},{6,0},{7,1},{8,14},{9,15},{10,... | collective-permute-start | bytes 786440 | tf_op jit(solution)/shard_map/ppermute | solution.py:510
  24.4 12.4 %collective-permute-start.5 = (bf16[64,2048]{1,0:T(8,128)(2,1)S(1)}, bf16[64,2048]{1,0:T(8,128)(2,1)S(1)}, u32[]{:S(2)}, u32[]{:S(2)}) collective-permute-start(bf16[64,2048]{1,0:T(8,128)(2,1)S(1)} %shard_map.150.refs_3_), channel_id=1, source_target_pairs={{0,2},{1,3},{2,0},{3,1},{4,6},{5,7},{6,4},{7,5},{8,10},{9,11},{10,... | collective-permute-start | bytes 786440 | tf_op jit(solution)/shard_map/ppermute | solution.py:510
  24.8 13.6 %collective-permute-start.6 = (bf16[64,2048]{1,0:T(8,128)(2,1)S(1)}, bf16[64,2048]{1,0:T(8,128)(2,1)S(1)}, u32[]{:S(2)}, u32[]{:S(2)}) collective-permute-start(bf16[64,2048]{1,0:T(8,128)(2,1)S(1)} %shard_map.150.refs_3_), channel_id=1, source_target_pairs={{0,4},{1,5},{2,6},{3,7},{4,0},{5,1},{6,2},{7,3},{8,12},{9,13},{10,... | collective-permute-start | bytes 786440 | tf_op jit(solution)/shard_map/ppermute | solution.py:510
  29.4 13.0 %collective-permute-start.9 = (bf16[64,2048]{1,0:T(8,128)(2,1)S(1)}, bf16[64,2048]{1,0:T(8,128)(2,1)S(1)}, u32[]{:S(2)}, u32[]{:S(2)}) collective-permute-start(bf16[64,2048]{1,0:T(8,128)(2,1)S(1)} %collective-permute-done.8.refs_5_), channel_id=1, source_target_pairs={{0,2},{1,3},{2,0},{3,1},{4,6},{5,7},{6,4},{7,5},{8,10},{9,11},{10,... | collective-permute-start | bytes 786440 | tf_op jit(solution)/shard_map/ppermute | solution.py:510
  30.9 11.6 %collective-permute-start.10 = (bf16[64,2048]{1,0:T(8,128)(2,1)S(1)}, bf16[64,2048]{1,0:T(8,128)(2,1)S(1)}, u32[]{:S(2)}, u32[]{:S(2)}) collective-permute-start(bf16[64,2048]{1,0:T(8,128)(2,1)S(1)} %collective-permute-done.8.refs_5_), channel_id=1, source_target_pairs={{0,4},{1,5},{2,6},{3,7},{4,0},{5,1},{6,2},{7,3},{8,12},{9,13},{10,... | collective-permute-start | bytes 786440 | tf_op jit(solution)/shard_map/ppermute | solution.py:510
  32.8 9.6 %collective-permute-start.11 = (bf16[64,2048]{1,0:T(8,128)(2,1)S(1)}, bf16[64,2048]{1,0:T(8,128)(2,1)S(1)}, u32[]{:S(2)}, u32[]{:S(2)}) collective-permute-start(bf16[64,2048]{1,0:T(8,128)(2,1)S(1)} %collective-permute-done.7.refs_4_), channel_id=1, source_target_pairs={{0,8},{1,9},{2,10},{3,11},{4,12},{5,13},{6,14},{7,15},{8,0},{9,1},... | collective-permute-start | bytes 786440 | tf_op jit(solution)/shard_map/ppermute | solution.py:510
  40.8 15.2 %copy-start.7 = (s32[8]{0:T(128)S(1)}, s32[8]{0:T(128)}, u32[]{:S(2)}) copy-start(s32[8]{0:T(128)} %lengths_ref.1) | copy-start | bytes 100
  40.8 15.2 %copy-start.12 = (s32[8]{0:T(128)S(1)}, s32[8]{0:T(128)}, u32[]{:S(2)}) copy-start(s32[8]{0:T(128)} %param.18) | copy-start | bytes 100

commit v8 on v7

--- a/solution.py
+++ b/solution.py
@@ -469,7 +469,7 @@
             squares += got_ref[part, core, group][7:8, LANES // 2 : LANES // 2 + count]
     squares = upright(squares)
     scale = jnp.sqrt(squares / (width * shards) + NORM_EPS)
-    keys_ref[...] = (turned_ref[...] / scale).astype(jnp.bfloat16)
+    keys_ref[...] = (turned_ref[...] * (1.0 / scale)).astype(jnp.bfloat16)
 
 
 def partners(sizes, flips):

time: 57.6 us -> 57.6 us (level)
  no operation moved by 1% of the time
where the time goes in v8:
time: 57.6 us; the launch traced here: 57.2 us
  starting transfers between devices  16.1 us (28%)
  Pallas kernels  11.3 us (20%)
  blocking collectives  10.8 us (19%)
  waiting for transfers between devices  9.41 us (16%)
  local copies, waits for them, and re-layouts  8.79 us (15%)
  between operations  0.74 us (1%)
    ppermute x12, starting transfers between devices, swap(): return lax.ppermute(array, axes, partners(sizes, (group_flip, shard_flip)))  16.1 us
    all_to_all x1, blocking collectives, local(): got = lax.all_to_all(sent, ('vocab', 'grp'), 0, 0, tiled=False)  10.8 us
    ppermute x12, waiting for transfers between devices, swap(): return lax.ppermute(array, axes, partners(sizes, (group_flip, shard_flip)))  9.41 us
    unnamed x26, local copies, waits for them, and re-layouts  8.79 us
    pallas_call x3, Pallas kernels, score(): call(kernel, out_shape, [WHOLE] * (3 + len(extras)), 4 * vocab * count *...  7.32 us
    pallas_call x1, Pallas kernels, local(): call(functools.partial(side_kernel, sizes, swapped), (jax.ShapeDtypeStruc...  1.9 us
    pallas_call x1, Pallas kernels, local(): call(functools.partial(final_kernel, sizes), (jax.ShapeDtypeStruct((1, ca...  1.19 us
  transfers between devices with their start and end apart: 12, of which 7 were waited for; matrix products, arithmetic and copies ran while one was open for 0% of the time, Pallas kernels for 12%

profile of v8, /device:TPU:0, one launch (start us, length us, event | category | flops | bytes accessed | tf_op | source)
XLA Modules:
  0.0 57.2 jit_solution(7225387799221591954)
XLA Ops:
  0.6 0.0 copy-start.1
  0.6 1.2 %copy-done.1 = bf16[256,2048]{1,0:T(8,128)(2,1)S(1)} copy-done((bf16[256,2048]{1,0:T(8,128)(2,1)S(1)}, bf16[256,2048]{1,0:T(8,128)(2,1)}, u32[]{:S(2)}) %copy-start.1) | copy-done | bytes 1048600
  1.9 0.7 %copy-done.4 = f32[2048]{0:T(1024)S(1)} copy-done((f32[2048]{0:T(1024)S(1)}, f32[2048]{0:T(1024)}, u32[]{:S(2)}) %copy-start.4) | copy-done | bytes 8216
  2.6 0.4 shard_map.147.here_ref
  3.0 0.5 collective-permute-start.4
  3.5 3.7 %collective-permute-start = (bf16[64,2048]{1,0:T(8,128)(2,1)S(1)}, bf16[64,2048]{1,0:T(8,128)(2,1)S(1)}, u32[]{:S(2)}, u32[]{:S(2)}) collective-permute-start(bf16[64,2048]{1,0:T(8,128)(2,1)S(1)} %shard_map.147.here_ref), channel_id=1, source_target_pairs={{0,16},{1,17},{2,18},{3,19},{4,20},{5,21},{6,22},{7,23},{8,24},{9,... | collective-permute-start | bytes 786440 | tf_op jit(solution)/shard_map/ppermute | solution.py:510
  7.2 0.3 shard_map.148.refs_0_
  7.5 1.6 %collective-permute-start.1 = (bf16[2,16,2048]{2,1,0:T(8,128)(2,1)S(1)}, bf16[2,16,2048]{2,1,0:T(8,128)(2,1)S(1)}, u32[]{:S(2)}, u32[]{:S(2)}) collective-permute-start(bf16[2,16,2048]{2,1,0:T(8,128)(2,1)S(1)} %shard_map.148.refs_0_), channel_id=1, source_target_pairs={{0,4},{1,5},{2,6},{3,7},{4,0},{5,1},{6,2},{7,3},{8,12},{9,13},{10,... | collective-permute-start | bytes 393224 | tf_op jit(solution)/shard_map/ppermute | solution.py:510
  9.1 1.6 %collective-permute-start.2 = (bf16[2,16,2048]{2,1,0:T(8,128)(2,1)S(1)}, bf16[2,16,2048]{2,1,0:T(8,128)(2,1)S(1)}, u32[]{:S(2)}, u32[]{:S(2)}) collective-permute-start(bf16[2,16,2048]{2,1,0:T(8,128)(2,1)S(1)} %shard_map.148.refs_0_), channel_id=1, source_target_pairs={{0,8},{1,9},{2,10},{3,11},{4,12},{5,13},{6,14},{7,15},{8,0},{9,1},... | collective-permute-start | bytes 393224 | tf_op jit(solution)/shard_map/ppermute | solution.py:510
  10.7 0.4 collective-permute-start.3
  11.1 1.6 %copy-done.2 = bf16[2048,512]{1,0:T(8,128)(2,1)S(1)} copy-done((bf16[2048,512]{1,0:T(8,128)(2,1)S(1)}, bf16[2048,512]{1,0:T(8,128)(2,1)}, u32[]{:S(2)}) %copy-start.2) | copy-done | bytes 2097176
  12.7 1.2 %copy-done.3 = bf16[256,2048]{1,0:T(8,128)(2,1)S(1)} copy-done((bf16[256,2048]{1,0:T(8,128)(2,1)S(1)}, bf16[256,2048]{1,0:T(8,128)(2,1)}, u32[]{:S(2)}) %copy-start.3) | copy-done | bytes 1048600
  13.9 0.7 %copy-done.5 = s32[2048]{0:T(1024)S(1)} copy-done((s32[2048]{0:T(1024)S(1)}, s32[2048]{0:T(1024)}, u32[]{:S(2)}) %copy-start.5) | copy-done | bytes 8216
  14.6 0.7 %copy-done.6 = s32[8]{0:T(128)S(1)} copy-done((s32[8]{0:T(128)S(1)}, s32[8]{0:T(128)}, u32[]{:S(2)}) %copy-start.6) | copy-done | bytes 56
  15.2 0.7 %copy-done.8 = f32[512]{0:T(512)S(1)} copy-done((f32[512]{0:T(512)S(1)}, f32[512]{0:T(512)}, u32[]{:S(2)}) %copy-start.8) | copy-done | bytes 2072
  15.9 0.7 %copy-done.9 = s32[256]{0:T(256)S(1)} copy-done((s32[256]{0:T(256)S(1)}, s32[256]{0:T(256)}, u32[]{:S(2)}) %copy-start.9) | copy-done | bytes 1048
  16.6 0.7 %copy-done.10 = s32[256]{0:T(256)S(1)} copy-done((s32[256]{0:T(256)S(1)}, s32[256]{0:T(256)}, u32[]{:S(2)}) %copy-start.10) | copy-done | bytes 1048
  17.3 0.7 %copy-done.11 = s32[25]{0:T(128)S(1)} copy-done((s32[25]{0:T(128)S(1)}, s32[25]{0:T(128)}, u32[]{:S(2)}) %copy-start.11) | copy-done | bytes 124
  17.9 1.9 %shard_map.149 = (f32[25,512]{1,0:T(8,128)S(1)}, f32[1,64]{1,0:T(1,128)S(1)}, s32[1,240]{1,0:T(1,128)S(1)}, s32[1,160]{1,0:T(1,128)S(1)}, s32[1,240]{1,0:T(1,128)S(1)}) custom-call(s32[8]{0:T(128)S(1)} %copy-done.6, s32[1,25]{1,0:T(1,128)S(1)} %bitcast.21, s32[1,256]{1,0:T(1,128)S(1)} %bitcast.19, s32[1,256]{1,0:T(1,128)S(1)} %bitcast.20, ...), custom_call_target="tpu_custom_call" | custom-call | flops 52428800 | bytes 2097152 | tf_op jit(solution)/shard_map/pallas_call | solution.py:527
  19.8 0.0 collective-permute-done.1.refs_1_
  19.9 0.0 collective-permute-done.2.refs_2_.beyond_ref
  19.9 1.7 %collective-permute-done.3.corner_ref = bf16[2,16,2048]{2,1,0:T(8,128)(2,1)S(1)} collective-permute-done((bf16[2,16,2048]{2,1,0:T(8,128)(2,1)S(1)}, bf16[2,16,2048]{2,1,0:T(8,128)(2,1)S(1)}, u32[]{:S(2)}, u32[]{:S(2)}) %collective-permute-start.3) | collective-permute-done | bytes 131104 | tf_op jit(solution)/shard_map/ppermute | solution.py:510
  21.6 0.0 collective-permute-done.other_ref
  21.7 0.0 collective-permute-done.4.far_ref
  21.7 0.2 shard_map.150.refs_3_
  21.8 0.8 %collective-permute-start.8 = (bf16[64,2048]{1,0:T(8,128)(2,1)S(1)}, bf16[64,2048]{1,0:T(8,128)(2,1)S(1)}, u32[]{:S(2)}, u32[]{:S(2)}) collective-permute-start(bf16[64,2048]{1,0:T(8,128)(2,1)S(1)} %shard_map.150.refs_3_), channel_id=1, source_target_pairs={{0,8},{1,9},{2,10},{3,11},{4,12},{5,13},{6,14},{7,15},{8,0},{9,1},... | collective-permute-start | bytes 786440 | tf_op jit(solution)/shard_map/ppermute | solution.py:510
  22.6 1.8 %collective-permute-start.7 = (bf16[64,2048]{1,0:T(8,128)(2,1)S(1)}, bf16[64,2048]{1,0:T(8,128)(2,1)S(1)}, u32[]{:S(2)}, u32[]{:S(2)}) collective-permute-start(bf16[64,2048]{1,0:T(8,128)(2,1)S(1)} %shard_map.150.refs_3_), channel_id=1, source_target_pairs={{0,6},{1,7},{2,4},{3,5},{4,2},{5,3},{6,0},{7,1},{8,14},{9,15},{10,... | collective-permute-start | bytes 786440 | tf_op jit(solution)/shard_map/ppermute | solution.py:510
  24.4 0.4 collective-permute-start.5
  24.8 1.3 %collective-permute-start.6 = (bf16[64,2048]{1,0:T(8,128)(2,1)S(1)}, bf16[64,2048]{1,0:T(8,128)(2,1)S(1)}, u32[]{:S(2)}, u32[]{:S(2)}) collective-permute-start(bf16[64,2048]{1,0:T(8,128)(2,1)S(1)} %shard_map.150.refs_3_), channel_id=1, source_target_pairs={{0,4},{1,5},{2,6},{3,7},{4,0},{5,1},{6,2},{7,3},{8,12},{9,13},{10,... | collective-permute-start | bytes 786440 | tf_op jit(solution)/shard_map/ppermute | solution.py:510
  26.1 3.2 %collective-permute-done.8.refs_5_ = bf16[64,2048]{1,0:T(8,128)(2,1)S(1)} collective-permute-done((bf16[64,2048]{1,0:T(8,128)(2,1)S(1)}, bf16[64,2048]{1,0:T(8,128)(2,1)S(1)}, u32[]{:S(2)}, u32[]{:S(2)}) %collective-permute-start.8) | collective-permute-done | bytes 262176 | tf_op jit(solution)/shard_map/ppermute | solution.py:510
  29.4 1.5 %collective-permute-start.9 = (bf16[64,2048]{1,0:T(8,128)(2,1)S(1)}, bf16[64,2048]{1,0:T(8,128)(2,1)S(1)}, u32[]{:S(2)}, u32[]{:S(2)}) collective-permute-start(bf16[64,2048]{1,0:T(8,128)(2,1)S(1)} %collective-permute-done.8.refs_5_), channel_id=1, source_target_pairs={{0,2},{1,3},{2,0},{3,1},{4,6},{5,7},{6,4},{7,5},{8,10},{9,11},{10,... | collective-permute-start | bytes 786440 | tf_op jit(solution)/shard_map/ppermute | solution.py:510
  30.9 1.2 %collective-permute-start.10 = (bf16[64,2048]{1,0:T(8,128)(2,1)S(1)}, bf16[64,2048]{1,0:T(8,128)(2,1)S(1)}, u32[]{:S(2)}, u32[]{:S(2)}) collective-permute-start(bf16[64,2048]{1,0:T(8,128)(2,1)S(1)} %collective-permute-done.8.refs_5_), channel_id=1, source_target_pairs={{0,4},{1,5},{2,6},{3,7},{4,0},{5,1},{6,2},{7,3},{8,12},{9,13},{10,... | collective-permute-start | bytes 786440 | tf_op jit(solution)/shard_map/ppermute | solution.py:510
  32.1 0.7 %collective-permute-done.7.refs_4_ = bf16[64,2048]{1,0:T(8,128)(2,1)S(1)} collective-permute-done((bf16[64,2048]{1,0:T(8,128)(2,1)S(1)}, bf16[64,2048]{1,0:T(8,128)(2,1)S(1)}, u32[]{:S(2)}, u32[]{:S(2)}) %collective-permute-start.7) | collective-permute-done | bytes 262176 | tf_op jit(solution)/shard_map/ppermute | solution.py:510
  32.8 1.3 %collective-permute-start.11 = (bf16[64,2048]{1,0:T(8,128)(2,1)S(1)}, bf16[64,2048]{1,0:T(8,128)(2,1)S(1)}, u32[]{:S(2)}, u32[]{:S(2)}) collective-permute-start(bf16[64,2048]{1,0:T(8,128)(2,1)S(1)} %collective-permute-done.7.refs_4_), channel_id=1, source_target_pairs={{0,8},{1,9},{2,10},{3,11},{4,12},{5,13},{6,14},{7,15},{8,0},{9,1},... | collective-permute-start | bytes 786440 | tf_op jit(solution)/shard_map/ppermute | solution.py:510
  34.1 0.0 copy-done
  34.1 2.4 %shard_map.151.first_ref = f32[8,240]{1,0:T(8,128)S(1)} custom-call(s32[1,240]{1,0:T(1,128)S(1)} %get-tuple-element.38.targets_ref, bf16[784,2048]{1,0:T(8,128)(2,1)S(1)} %copy-done, bf16[784,2048]{1,0:T(8,128)(2,1)S(1)} %collective-permute-done.4.far_ref, bf16[2,16,2048]{2,1,0:T(8,128)(2,1)S(1)} %shard_map.148.refs_0_, ...), custom_call_target="tpu_custom_call" | custom-call | flops 1541406720 | bytes 7405568 | tf_op jit(solution)/shard_map/pallas_call | solution.py:274
  36.5 0.4 collective-permute-done.5.refs_2_
  36.8 1.6 %collective-permute-done.6.refs_3_ = bf16[64,2048]{1,0:T(8,128)(2,1)S(1)} collective-permute-done((bf16[64,2048]{1,0:T(8,128)(2,1)S(1)}, bf16[64,2048]{1,0:T(8,128)(2,1)S(1)}, u32[]{:S(2)}, u32[]{:S(2)}) %collective-permute-start.6) | collective-permute-done | bytes 262176 | tf_op jit(solution)/shard_map/ppermute | solution.py:510
  38.5 2.3 %shard_map.152.second_ref = f32[8,160]{1,0:T(8,128)S(1)} custom-call(s32[1,160]{1,0:T(1,128)S(1)} %get-tuple-element.42.targets_ref, bf16[784,2048]{1,0:T(8,128)(2,1)S(1)} %copy-done, bf16[784,2048]{1,0:T(8,128)(2,1)S(1)} %collective-permute-done.4.far_ref, bf16[2,16,2048]{2,1,0:T(8,128)(2,1)S(1)} %shard_map.148.refs_0_, ...), custom_call_target="tpu_custom_call" | custom-call | flops 1027604480 | bytes 7077888 | tf_op jit(solution)/shard_map/pallas_call | solution.py:274
  40.8 0.0 copy-start.7
  40.8 0.0 copy-start.12
  40.8 1.6 %collective-permute-done.9.refs_0_ = bf16[64,2048]{1,0:T(8,128)(2,1)S(1)} collective-permute-done((bf16[64,2048]{1,0:T(8,128)(2,1)S(1)}, bf16[64,2048]{1,0:T(8,128)(2,1)S(1)}, u32[]{:S(2)}, u32[]{:S(2)}) %collective-permute-start.9) | collective-permute-done | bytes 262176 | tf_op jit(solution)/shard_map/ppermute | solution.py:510
  42.4 0.1 collective-permute-done.10.refs_1_
  42.5 0.0 collective-permute-done.11.refs_2_
  42.5 2.6 %shard_map.153 = f32[32,8,128]{2,1,0:T(8,128)S(1)} custom-call(s32[1,240]{1,0:T(1,128)S(1)} %get-tuple-element.35.targets_ref, bf16[784,2048]{1,0:T(8,128)(2,1)S(1)} %copy-done, bf16[784,2048]{1,0:T(8,128)(2,1)S(1)} %collective-permute-done.4.far_ref, f32[8,240]{1,0:T(8,128)S(1)} %shard_map.151.first_ref, f32[8,160]{1,0:T(8,128)S(1)} %shard_map.152.second_ref, ...), custom_call_target="tpu_custom_call" | custom-call | flops 1541406720 | bytes 7405568 | tf_op jit(solution)/shard_map/pallas_call | solution.py:274
  45.1 10.8 %all_to_all.5 = f32[32,8,128]{2,1,0:T(8,128)S(1)} all-to-all(f32[32,8,128]{2,1,0:T(8,128)S(1)} %shard_map.153), channel_id=1, replica_groups=mesh['grp'=8,'vocab'=4] {'vocab','grp'}, dimensions={0} | all-to-all | bytes 262144 | tf_op jit(solution)/shard_map/all_to_all | solution.py:635
  56.0 0.0 copy-done.7
  56.0 1.2 %shard_map.154 = (f32[1,256]{1,0:T(1,128)}, f32[1,256]{1,0:T(1,128)}, f32[1,4]{1,0:T(1,128)}, bf16[25,512]{1,0:T(8,128)(2,1)}) custom-call(s32[1,8]{1,0:T(1,128)S(1)} %bitcast.17, s32[1,8]{1,0:T(1,128)S(1)} %bitcast.22, f32[2,2,8,8,128]{4,3,2,1,0:T(8,128)S(1)} %bitcast.12, f32[25,512]{1,0:T(8,128)S(1)} %get-tuple-element.47.turned_ref), custom_call_target="tpu_custom_call" | custom-call | flops 16777216 | bytes 131072 | tf_op jit(solution)/shard_map/pallas_call | solution.py:637
  (11 shorter events, 0.0 us)
Async XLA Ops:
  0.6 1.2 %copy-start.1 = (bf16[256,2048]{1,0:T(8,128)(2,1)S(1)}, bf16[256,2048]{1,0:T(8,128)(2,1)}, u32[]{:S(2)}) copy-start(bf16[256,2048]{1,0:T(8,128)(2,1)} %hidden_ref.3) | copy-start | bytes 3145732
  1.9 0.7 %copy-start.4 = (f32[2048]{0:T(1024)S(1)}, f32[2048]{0:T(1024)}, u32[]{:S(2)}) copy-start(f32[2048]{0:T(1024)} %param.13) | copy-start | bytes 24580
  2.6 31.5 %copy-start = (bf16[784,2048]{1,0:T(8,128)(2,1)S(1)}, bf16[784,2048]{1,0:T(8,128)(2,1)}, u32[]{:S(2)}) copy-start(bf16[784,2048]{1,0:T(8,128)(2,1)} %near_ref.2) | copy-start | bytes 9633796
  3.0 18.7 %collective-permute-start.4 = (bf16[784,2048]{1,0:T(8,128)(2,1)}, bf16[784,2048]{1,0:T(8,128)(2,1)S(1)}, u32[]{:S(2)}, u32[]{:S(2)}) collective-permute-start(bf16[784,2048]{1,0:T(8,128)(2,1)} %near_ref.2), channel_id=1, source_target_pairs={{0,1},{1,0},{2,3},{3,2},{4,5},{5,4},{6,7},{7,6},{8,9},{9,8},{10,11... | collective-permute-start | bytes 9633800 | tf_op jit(solution)/shard_map/ppermute | solution.py:510
  3.5 18.2 %collective-permute-start = (bf16[64,2048]{1,0:T(8,128)(2,1)S(1)}, bf16[64,2048]{1,0:T(8,128)(2,1)S(1)}, u32[]{:S(2)}, u32[]{:S(2)}) collective-permute-start(bf16[64,2048]{1,0:T(8,128)(2,1)S(1)} %shard_map.147.here_ref), channel_id=1, source_target_pairs={{0,16},{1,17},{2,18},{3,19},{4,20},{5,21},{6,22},{7,23},{8,24},{9,... | collective-permute-start | bytes 786440 | tf_op jit(solution)/shard_map/ppermute | solution.py:510
  7.5 12.3 %collective-permute-start.1 = (bf16[2,16,2048]{2,1,0:T(8,128)(2,1)S(1)}, bf16[2,16,2048]{2,1,0:T(8,128)(2,1)S(1)}, u32[]{:S(2)}, u32[]{:S(2)}) collective-permute-start(bf16[2,16,2048]{2,1,0:T(8,128)(2,1)S(1)} %shard_map.148.refs_0_), channel_id=1, source_target_pairs={{0,4},{1,5},{2,6},{3,7},{4,0},{5,1},{6,2},{7,3},{8,12},{9,13},{10,... | collective-permute-start | bytes 393224 | tf_op jit(solution)/shard_map/ppermute | solution.py:510
  9.1 10.8 %collective-permute-start.2 = (bf16[2,16,2048]{2,1,0:T(8,128)(2,1)S(1)}, bf16[2,16,2048]{2,1,0:T(8,128)(2,1)S(1)}, u32[]{:S(2)}, u32[]{:S(2)}) collective-permute-start(bf16[2,16,2048]{2,1,0:T(8,128)(2,1)S(1)} %shard_map.148.refs_0_), channel_id=1, source_target_pairs={{0,8},{1,9},{2,10},{3,11},{4,12},{5,13},{6,14},{7,15},{8,0},{9,1},... | collective-permute-start | bytes 393224 | tf_op jit(solution)/shard_map/ppermute | solution.py:510
  10.7 11.0 %collective-permute-start.3 = (bf16[2,16,2048]{2,1,0:T(8,128)(2,1)S(1)}, bf16[2,16,2048]{2,1,0:T(8,128)(2,1)S(1)}, u32[]{:S(2)}, u32[]{:S(2)}) collective-permute-start(bf16[2,16,2048]{2,1,0:T(8,128)(2,1)S(1)} %shard_map.148.refs_0_), channel_id=1, source_target_pairs={{0,12},{1,13},{2,14},{3,15},{4,8},{5,9},{6,10},{7,11},{8,4},{9,5},... | collective-permute-start | bytes 393224 | tf_op jit(solution)/shard_map/ppermute | solution.py:510
  11.1 1.6 %copy-start.2 = (bf16[2048,512]{1,0:T(8,128)(2,1)S(1)}, bf16[2048,512]{1,0:T(8,128)(2,1)}, u32[]{:S(2)}) copy-start(bf16[2048,512]{1,0:T(8,128)(2,1)} %weight_hbm.1) | copy-start | bytes 6291460
  12.7 1.2 %copy-start.3 = (bf16[256,2048]{1,0:T(8,128)(2,1)S(1)}, bf16[256,2048]{1,0:T(8,128)(2,1)}, u32[]{:S(2)}) copy-start(bf16[256,2048]{1,0:T(8,128)(2,1)} %input_hbm.1) | copy-start | bytes 3145732
  13.9 0.7 %copy-start.5 = (s32[2048]{0:T(1024)S(1)}, s32[2048]{0:T(1024)}, u32[]{:S(2)}) copy-start(s32[2048]{0:T(1024)} %param.15) | copy-start | bytes 24580
  14.6 0.7 %copy-start.6 = (s32[8]{0:T(128)S(1)}, s32[8]{0:T(128)}, u32[]{:S(2)}) copy-start(s32[8]{0:T(128)} %lengths_ref.1) | copy-start | bytes 100
  15.2 0.7 %copy-start.8 = (f32[512]{0:T(512)S(1)}, f32[512]{0:T(512)}, u32[]{:S(2)}) copy-start(f32[512]{0:T(512)} %param.21) | copy-start | bytes 6148
  15.9 0.7 %copy-start.9 = (s32[256]{0:T(256)S(1)}, s32[256]{0:T(256)}, u32[]{:S(2)}) copy-start(s32[256]{0:T(256)} %param.22) | copy-start | bytes 3076
  16.6 0.7 %copy-start.10 = (s32[256]{0:T(256)S(1)}, s32[256]{0:T(256)}, u32[]{:S(2)}) copy-start(s32[256]{0:T(256)} %param.17) | copy-start | bytes 3076
  17.3 0.7 %copy-start.11 = (s32[25]{0:T(128)S(1)}, s32[25]{0:T(128)}, u32[]{:S(2)}) copy-start(s32[25]{0:T(128)} %param.23) | copy-start | bytes 304
  21.8 7.6 %collective-permute-start.8 = (bf16[64,2048]{1,0:T(8,128)(2,1)S(1)}, bf16[64,2048]{1,0:T(8,128)(2,1)S(1)}, u32[]{:S(2)}, u32[]{:S(2)}) collective-permute-start(bf16[64,2048]{1,0:T(8,128)(2,1)S(1)} %shard_map.150.refs_3_), channel_id=1, source_target_pairs={{0,8},{1,9},{2,10},{3,11},{4,12},{5,13},{6,14},{7,15},{8,0},{9,1},... | collective-permute-start | bytes 786440 | tf_op jit(solution)/shard_map/ppermute | solution.py:510
  22.6 10.2 %collective-permute-start.7 = (bf16[64,2048]{1,0:T(8,128)(2,1)S(1)}, bf16[64,2048]{1,0:T(8,128)(2,1)S(1)}, u32[]{:S(2)}, u32[]{:S(2)}) collective-permute-start(bf16[64,2048]{1,0:T(8,128)(2,1)S(1)} %shard_map.150.refs_3_), channel_id=1, source_target_pairs={{0,6},{1,7},{2,4},{3,5},{4,2},{5,3},{6,0},{7,1},{8,14},{9,15},{10,... | collective-permute-start | bytes 786440 | tf_op jit(solution)/shard_map/ppermute | solution.py:510
  24.4 12.4 %collective-permute-start.5 = (bf16[64,2048]{1,0:T(8,128)(2,1)S(1)}, bf16[64,2048]{1,0:T(8,128)(2,1)S(1)}, u32[]{:S(2)}, u32[]{:S(2)}) collective-permute-start(bf16[64,2048]{1,0:T(8,128)(2,1)S(1)} %shard_map.150.refs_3_), channel_id=1, source_target_pairs={{0,2},{1,3},{2,0},{3,1},{4,6},{5,7},{6,4},{7,5},{8,10},{9,11},{10,... | collective-permute-start | bytes 786440 | tf_op jit(solution)/shard_map/ppermute | solution.py:510
  24.8 13.6 %collective-permute-start.6 = (bf16[64,2048]{1,0:T(8,128)(2,1)S(1)}, bf16[64,2048]{1,0:T(8,128)(2,1)S(1)}, u32[]{:S(2)}, u32[]{:S(2)}) collective-permute-start(bf16[64,2048]{1,0:T(8,128)(2,1)S(1)} %shard_map.150.refs_3_), channel_id=1, source_target_pairs={{0,4},{1,5},{2,6},{3,7},{4,0},{5,1},{6,2},{7,3},{8,12},{9,13},{10,... | collective-permute-start | bytes 786440 | tf_op jit(solution)/shard_map/ppermute | solution.py:510
  29.4 13.0 %collective-permute-start.9 = (bf16[64,2048]{1,0:T(8,128)(2,1)S(1)}, bf16[64,2048]{1,0:T(8,128)(2,1)S(1)}, u32[]{:S(2)}, u32[]{:S(2)}) collective-permute-start(bf16[64,2048]{1,0:T(8,128)(2,1)S(1)} %collective-permute-done.8.refs_5_), channel_id=1, source_target_pairs={{0,2},{1,3},{2,0},{3,1},{4,6},{5,7},{6,4},{7,5},{8,10},{9,11},{10,... | collective-permute-start | bytes 786440 | tf_op jit(solution)/shard_map/ppermute | solution.py:510
  30.9 11.6 %collective-permute-start.10 = (bf16[64,2048]{1,0:T(8,128)(2,1)S(1)}, bf16[64,2048]{1,0:T(8,128)(2,1)S(1)}, u32[]{:S(2)}, u32[]{:S(2)}) collective-permute-start(bf16[64,2048]{1,0:T(8,128)(2,1)S(1)} %collective-permute-done.8.refs_5_), channel_id=1, source_target_pairs={{0,4},{1,5},{2,6},{3,7},{4,0},{5,1},{6,2},{7,3},{8,12},{9,13},{10,... | collective-permute-start | bytes 786440 | tf_op jit(solution)/shard_map/ppermute | solution.py:510
  32.8 9.6 %collective-permute-start.11 = (bf16[64,2048]{1,0:T(8,128)(2,1)S(1)}, bf16[64,2048]{1,0:T(8,128)(2,1)S(1)}, u32[]{:S(2)}, u32[]{:S(2)}) collective-permute-start(bf16[64,2048]{1,0:T(8,128)(2,1)S(1)} %collective-permute-done.7.refs_4_), channel_id=1, source_target_pairs={{0,8},{1,9},{2,10},{3,11},{4,12},{5,13},{6,14},{7,15},{8,0},{9,1},... | collective-permute-start | bytes 786440 | tf_op jit(solution)/shard_map/ppermute | solution.py:510
  40.8 15.2 %copy-start.7 = (s32[8]{0:T(128)S(1)}, s32[8]{0:T(128)}, u32[]{:S(2)}) copy-start(s32[8]{0:T(128)} %lengths_ref.1) | copy-start | bytes 100
  40.8 15.2 %copy-start.12 = (s32[8]{0:T(128)S(1)}, s32[8]{0:T(128)}, u32[]{:S(2)}) copy-start(s32[8]{0:T(128)} %param.18) | copy-start | bytes 100
